TPU v7x, 32 devices: a whole 2x2x4 slice. The times are simulated.
32 devices in a mesh: traj: 2 (over y), ctx: 8 (over z, x), head: 2 (over core).
Axes of the slice: x: 2, y: 2, z: 4, core: 2. Of those that a mesh axis runs over, the one named last changes fastest.
Arguments:
- features: bfloat16 [4096, 2048], P(('traj', 'ctx'), 'head'), parts along dimension 0, may hold values from -6 to 6
- b_input: bfloat16 [4096, 128], P(('traj', 'ctx')), parts along dimension 0, may hold values from -1.5 to 1.5
- c_input: bfloat16 [4096, 128], P(('traj', 'ctx')), parts along dimension 0, may hold values from -1.5 to 1.5
- step_input: float32 [64, 4096], P('head', ('traj', 'ctx')), parts along dimension 1, may hold values from -5.5 to 18.78016
- decay_log: float32 [64], P('head')
- skip_gain: float32 [64], P('head'), may hold values from 0.5 to 2
- norm_gain: float32 [2048], P('head'), may hold values from 0.25 to 1.75
- value_weight: float32 [2048], P('head'), may hold values from -0.125 to 0.125
- rewards: float32 [4096], P(('traj', 'ctx')), parts along dimension 0, may hold values from -0.3 to 0.3
- reward_keep_mask: int32 [4096], P(('traj', 'ctx')), parts along dimension 0, may hold values 0 or 1
- episode_end: int32 [4096], P(('traj', 'ctx')), parts along dimension 0, may hold values from 0 to 1
Outputs:
- values: float32 [4096], P(('traj', 'ctx')), parts along dimension 0
- advantages: float32 [4096], P(('traj', 'ctx')), parts along dimension 0
There are 2 independent parts, one for each index of `traj`. A program takes and returns all parts, laid end to end along the dimension named above; an argument that names none is the same for every part. Nothing has to cross between parts.
All inputs are finite; a program needn't handle non-finite values. No bound on the sum of `reward_keep_mask` on one device may be relied on, other than what follows from the above.
Results may differ from a plain program's by a relative error of at most 0.00037.
Values sent between devices are 32-bit elements; how exact they have to be, the bound alone decides.
No kernel may reach another device: no remote copies, remote signals or barrier semaphores. Data moves between devices by JAX's collectives and lax.ppermute only.
A program may use at most 192 MiB of HBM per device.

v0:
```python
import jax
import jax.numpy as jnp
from jax import lax
from jax.sharding import PartitionSpec as P

HEADS = 64
HEAD_DIM = 32
SPAN = 256


NORM_EPSILON = 1e-05
FULL_PRECISION = lax.Precision.HIGHEST


def carried_in(value, axis, join, neutral, backward):
    count, mine = (lax.axis_size(axis), lax.axis_index(axis))
    pieces = jax.tree.map(lambda part: lax.all_gather(part, axis), value)
    if backward:
        pieces = jax.tree.map(lambda part: part[::-1], pieces)
        mine = count - 1 - mine
    subtotal = jax.tree.map(
        lambda part, zero: jnp.full_like(part, 0) + jnp.asarray(zero, part.dtype), value, neutral
    )

    def hop(position, subtotal):
        longer = join(subtotal, jax.tree.map(lambda part: part[position], pieces))
        return jax.tree.map(lambda new, old: jnp.where(position < mine, new, old), longer, subtotal)

    return lax.fori_loop(0, count - 1, hop, subtotal)


def link_states(earlier, later):
    return (earlier[0] * later[0], later[0][:, None, None] * earlier[1] + later[1])


def link_returns(earlier, later):
    return (earlier[0] * later[0], later[1] + later[0] * earlier[1])


def carry_states(block_states, block_total):
    block_decay = jnp.exp(block_total)
    running = jnp.zeros_like(block_states[0])
    entering = running
    running = block_decay[:, 0, None, None] * running + block_states[0]
    device_decay = jnp.exp(jnp.sum(block_total, axis=1))
    incoming = carried_in(
        (device_decay, running),
        "ctx",
        link_states,
        (jnp.ones_like(device_decay), jnp.zeros_like(running)),
        False,
    )[1]
    before_decay = jnp.exp(jnp.cumsum(block_total, axis=1) - block_total)
    return jnp.stack([entering + before_decay[:, 0, None, None] * incoming])


def segment_suffix(amounts, episode_end):
    row_count = amounts.shape[0]
    ends_through = jnp.cumsum(episode_end)
    ends_before = ends_through - episode_end
    position = jnp.arange(row_count)
    reach = (
        (position[None, :] >= position[:, None]) & (ends_before[None, :] == ends_before[:, None])
    ).astype(jnp.float32)
    local_sum = jnp.dot(reach, amounts, precision=FULL_PRECISION)
    open_end = (ends_before == ends_through[-1]).astype(jnp.float32)
    carried = carried_in(
        (open_end[:1], local_sum[:1]),
        "ctx",
        link_returns,
        (jnp.ones((1,), jnp.float32), jnp.zeros((1,), jnp.float32)),
        True,
    )[1]
    return local_sum + open_end * carried


def block_states_of(feat_part, key_spans, cum_part, step_portion):
    block_total = cum_part[:, :, -1:]
    coefficient = jnp.exp(block_total - cum_part) * step_portion
    scaled = (jnp.transpose(coefficient, (1, 2, 0))[:, :, :, None] * feat_part).astype(jnp.bfloat16)
    return jnp.einsum("csgp,csn->cgpn", scaled, key_spans, preferred_element_type=jnp.float32)


def intra_of(feat_part, scores, cum_part, step_portion, causal):
    log_gap = jnp.where(causal, cum_part[:, :, :, None] - cum_part[:, :, None, :], 0.0)
    weights = jnp.where(
        causal, scores[None] * jnp.exp(log_gap) * step_portion[:, :, None, :], 0.0
    ).astype(jnp.bfloat16)
    return jnp.einsum("gcts,csgp->ctgp", weights, feat_part, preferred_element_type=jnp.float32)


def local(
    features,
    b_input,
    c_input,
    step_input,
    decay_log,
    skip_gain,
    norm_gain,
    value_weight,
    rewards,
    reward_keep_mask,
    episode_end,
):
    tok_rows, row_width = features.shape
    heads_here = step_input.shape[0]
    span_count = tok_rows // SPAN
    state_width = b_input.shape[1]
    group_size = 8
    group_count = heads_here // group_size
    live_rewards = reward_keep_mask.astype(jnp.float32) * rewards
    reward_totals = segment_suffix(live_rewards, episode_end)
    step_size = jax.nn.softplus(step_input)
    log_decay = (-jnp.exp(decay_log))[:, None] * step_size
    upper_mask = (jnp.arange(SPAN)[:, None] <= jnp.arange(SPAN)[None, :]).astype(jnp.float32)
    cumulative = jnp.dot(log_decay, upper_mask, precision=FULL_PRECISION).reshape(
        heads_here, span_count, SPAN
    )
    step_spans = step_size.reshape(heads_here, span_count, SPAN)
    block_total = cumulative[:, :, -1]
    key_spans = b_input.reshape(span_count, SPAN, state_width)
    query_spans = c_input.reshape(span_count, SPAN, state_width)
    feat_spans = features.reshape(span_count, SPAN, heads_here, HEAD_DIM)
    causal = jnp.arange(SPAN)[:, None] >= jnp.arange(SPAN)[None, :]
    scores = jnp.einsum("ctn,csn->cts", query_spans, key_spans, preferred_element_type=jnp.float32)

    def pieces(group_index):
        first_head = group_index * group_size
        feat_part = lax.dynamic_slice_in_dim(feat_spans, first_head, group_size, 2)
        cum_part = lax.dynamic_slice_in_dim(cumulative, first_head, group_size, 0)
        step_portion = lax.dynamic_slice_in_dim(step_spans, first_head, group_size, 0)
        return (feat_part, cum_part, step_portion, first_head)

    def state_step(group_index, held):
        feat_part, cum_part, step_portion, first_head = pieces(group_index)
        return lax.dynamic_update_slice_in_dim(
            held, block_states_of(feat_part, key_spans, cum_part, step_portion), first_head, 1
        )

    def intra_step(group_index, held):
        feat_part, cum_part, step_portion, first_head = pieces(group_index)
        return lax.dynamic_update_slice_in_dim(
            held, intra_of(feat_part, scores, cum_part, step_portion, causal), first_head, 2
        )

    def both_step(group_index, held):
        return (intra_step(group_index, held[0]), state_step(group_index, held[1]))

    zero_states = jnp.zeros((span_count, heads_here, HEAD_DIM, state_width), jnp.float32)
    zero_intra = jnp.zeros((span_count, SPAN, heads_here, HEAD_DIM), jnp.float32)
    intra, block_states = lax.fori_loop(0, group_count, both_step, (zero_intra, zero_states))
    entering = carry_states(block_states, block_total)
    carried = jnp.einsum(
        "ctn,chpn->cthp", query_spans.astype(jnp.float32), entering, precision=FULL_PRECISION
    )
    carried = carried * jnp.exp(jnp.transpose(cumulative, (1, 2, 0)))[:, :, :, None]
    mixed = (intra + carried + skip_gain[None, None, :, None] * feat_spans).reshape(
        tok_rows, row_width
    )
    readout = value_weight * norm_gain
    square_local = jnp.sum(mixed * mixed, axis=1)
    square_total = lax.psum(square_local, "head")
    inverse_rms = 1.0 / jnp.sqrt(square_total / (HEADS * HEAD_DIM) + NORM_EPSILON)
    values = lax.psum(
        jnp.dot(mixed * inverse_rms[:, None], readout, precision=FULL_PRECISION), "head"
    )
    advantages = reward_totals - values
    return (values, advantages)


def solution(mesh):
    placed = (
        P(("traj", "ctx"), "head"),
        P(("traj", "ctx"), None),
        P(("traj", "ctx"), None),
        P("head", ("traj", "ctx")),
        P("head"),
        P("head"),
        P("head"),
        P("head"),
        P(("traj", "ctx")),
        P(("traj", "ctx")),
        P(("traj", "ctx")),
    )
    return jax.shard_map(
        local,
        mesh=mesh,
        in_specs=placed,
        out_specs=(P(("traj", "ctx")), P(("traj", "ctx"))),
        check_vma=False,
    )
```

profile of v0, /device:TPU:0, one launch (start us, length us, event | category | flops | bytes accessed | tf_op | source)
XLA Modules:
  0.0 117.0 jit_solution(5519768439251607696)
XLA Ops:
  7.9 0.8 fusion.33
  8.7 1.0 convolution_bitcast_fusion.4
  9.9 1.3 %copy.23 = bf16[256,1024]{0,1:T(8,128)(2,1)S(1)} copy(bf16[256,1024]{1,0:T(8,128)(2,1)} %param.17) | data formatting | bytes 1048576 | tf_op args[0]
  11.2 1.0 convolution_bitcast_fusion.3
  12.5 4.9 %while.45 = (s32[]{:T(128)}, f32[1,256,32,32]{1,3,2,0:T(8,128)S(1)}, f32[1,32,32,128]{3,2,1,0:T(8,128)S(1)}, bf16[1,256,32,32]{1,3,2,0:T(8,128)(2,1)S(1)}, f32[1...) while((s32[]{:T(128)}, ...), condition=%wide.region_1.2_spmd.clone.clone, body=%wide.region_0.0_spmd.clone.clone.sunk | while | flops 53743624 | bytes 1190179 | solution.py:151
  12.8 0.7 fusion.54
  14.0 0.7 fusion.54
  15.2 0.7 fusion.54
  17.3 0.9 broadcast_add_fusion
  21.8 0.8 slice_dynamic-update-slice_fusion
  22.6 0.7 fusion.37
  23.3 23.6 %all-reduce.3 = (f32[256]{0:T(256)S(1)}, f32[8]{0:T(128)S(1)}, f32[8]{0:T(128)S(1)}) all-reduce(f32[256]{0:T(256)S(1)} %dynamic-update-slice, f32[8]{0:T(128)S(1)} %slice_dynamic-update-slice_fusion, f32[8]{0:T(128)S(1)} %fusion.37), channel_id=2, replica_groups=mesh['traj'=2,'ctx'=8,'head'=2] {'ctx'}, use_global_device_ids=true, to_apply=%add | all-reduce | flops 272 | bytes 2176
  47.2 13.8 %while.44 = (s32[]{:T(128)}, f32[1]{0:T(128)}, s32[]{:T(128)}, f32[8,1]{0,1:T(1,128)S(1)}, f32[8,1]{0,1:T(1,128)S(1)}, /*index=5*/s32[]{:T(128)}) while((s32[]{:T(128)}, f32[1]{0:T(128)}, s32[]{:T(128)}, f32[8,1]{0,1:T(1,128)S(1)}, f32[8,1]{0,1:T(1,128)S(1)}, /*index=5*/s32[]{:T(128)}) %tuple.114), condition=%wide.region_10.11_spmd, body=%wide.region_9.10_spmd.sunk | while | flops 6 | bytes 135 | solution.py:29
  61.0 33.8 %all-gather.5.cloned.1.call-done = f32[8,32,32,128]{3,2,1,0:T(8,128)} async-done(((f32[1,32,32,128]{3,2,1,0:T(8,128)}), f32[8,32,32,128]{3,2,1,0:T(8,128)}) %all-gather.5.cloned.1.call-update) | async-done | bytes 4194320 | tf_op jit(solution)/shard_map/all_gather | solution.py:17
  94.8 8.5 %while.46 = (s32[]{:T(128)}, f32[32,32,128]{2,1,0:T(8,128)S(1)}, s32[]{:T(128)}, f32[8,32]{1,0:T(8,128)S(1)}, f32[8,32,32,128]{3,2,1,0:T(8,128)}, /*index=5*/s32[]{:T(128)}, s32[]{:T(128)}) while((s32[]{:T(128)}, f32[32,32,128]{2,1,0:T(8,128)S(1)}, s32[]{:T(128)}, f32[8,32]{1,0:T(8,128)S(1)}, f32[8,32,32,128]{3,2,1,0:T(8,128)}, ...), condition=%wide.region_3.4_spmd.clone, body=%wide.region_2.3_spmd.clone.sunk | while | flops 524292 | bytes 1573353 | solution.py:29
  94.8 1.2 %fusion.56 = f32[32,32,128]{2,1,0:T(8,128)S(1)} fusion(f32[8,32,32,128]{3,2,1,0:T(8,128)} %get-tuple-element.647, s32[]{:T(128)} %get-tuple-element.636, f32[32,32,128]{2,1,0:T(8,128)S(1)} %get-tuple-element.637, f32[32]{0:T(128)S(1)} %dynamic-slice_bitcast_fusion.4, pred[]{:T(512)S(6)} %compare.3, pred[]{:T(512)S(6)} %lt.69), kind=kLoop, calls=%fused_computation.4.clone.1 | loop fusion | flops 524288 | bytes 1572998 | tf_op jit(solution)/shard_map/while/body/eval_jaxpr/jit(_where)/select_n | solution.py:27
  96.0 1.2 %fusion.56 = f32[32,32,128]{2,1,0:T(8,128)S(1)} fusion(f32[8,32,32,128]{3,2,1,0:T(8,128)} %get-tuple-element.647, s32[]{:T(128)} %get-tuple-element.636, f32[32,32,128]{2,1,0:T(8,128)S(1)} %get-tuple-element.637, f32[32]{0:T(128)S(1)} %dynamic-slice_bitcast_fusion.4, pred[]{:T(512)S(6)} %compare.3, pred[]{:T(512)S(6)} %lt.69), kind=kLoop, calls=%fused_computation.4.clone.1 | loop fusion | flops 524288 | bytes 1572998 | tf_op jit(solution)/shard_map/while/body/eval_jaxpr/jit(_where)/select_n | solution.py:27
  97.2 1.2 %fusion.56 = f32[32,32,128]{2,1,0:T(8,128)S(1)} fusion(f32[8,32,32,128]{3,2,1,0:T(8,128)} %get-tuple-element.647, s32[]{:T(128)} %get-tuple-element.636, f32[32,32,128]{2,1,0:T(8,128)S(1)} %get-tuple-element.637, f32[32]{0:T(128)S(1)} %dynamic-slice_bitcast_fusion.4, pred[]{:T(512)S(6)} %compare.3, pred[]{:T(512)S(6)} %lt.69), kind=kLoop, calls=%fused_computation.4.clone.1 | loop fusion | flops 524288 | bytes 1572998 | tf_op jit(solution)/shard_map/while/body/eval_jaxpr/jit(_where)/select_n | solution.py:27
  98.4 1.2 %fusion.56 = f32[32,32,128]{2,1,0:T(8,128)S(1)} fusion(f32[8,32,32,128]{3,2,1,0:T(8,128)} %get-tuple-element.647, s32[]{:T(128)} %get-tuple-element.636, f32[32,32,128]{2,1,0:T(8,128)S(1)} %get-tuple-element.637, f32[32]{0:T(128)S(1)} %dynamic-slice_bitcast_fusion.4, pred[]{:T(512)S(6)} %compare.3, pred[]{:T(512)S(6)} %lt.69), kind=kLoop, calls=%fused_computation.4.clone.1 | loop fusion | flops 524288 | bytes 1572998 | tf_op jit(solution)/shard_map/while/body/eval_jaxpr/jit(_where)/select_n | solution.py:27
  99.7 1.2 %fusion.56 = f32[32,32,128]{2,1,0:T(8,128)S(1)} fusion(f32[8,32,32,128]{3,2,1,0:T(8,128)} %get-tuple-element.647, s32[]{:T(128)} %get-tuple-element.636, f32[32,32,128]{2,1,0:T(8,128)S(1)} %get-tuple-element.637, f32[32]{0:T(128)S(1)} %dynamic-slice_bitcast_fusion.4, pred[]{:T(512)S(6)} %compare.3, pred[]{:T(512)S(6)} %lt.69), kind=kLoop, calls=%fused_computation.4.clone.1 | loop fusion | flops 524288 | bytes 1572998 | tf_op jit(solution)/shard_map/while/body/eval_jaxpr/jit(_where)/select_n | solution.py:27
  100.9 1.2 %fusion.56 = f32[32,32,128]{2,1,0:T(8,128)S(1)} fusion(f32[8,32,32,128]{3,2,1,0:T(8,128)} %get-tuple-element.647, s32[]{:T(128)} %get-tuple-element.636, f32[32,32,128]{2,1,0:T(8,128)S(1)} %get-tuple-element.637, f32[32]{0:T(128)S(1)} %dynamic-slice_bitcast_fusion.4, pred[]{:T(512)S(6)} %compare.3, pred[]{:T(512)S(6)} %lt.69), kind=kLoop, calls=%fused_computation.4.clone.1 | loop fusion | flops 524288 | bytes 1572998 | tf_op jit(solution)/shard_map/while/body/eval_jaxpr/jit(_where)/select_n | solution.py:27
  102.1 1.2 %fusion.56 = f32[32,32,128]{2,1,0:T(8,128)S(1)} fusion(f32[8,32,32,128]{3,2,1,0:T(8,128)} %get-tuple-element.647, s32[]{:T(128)} %get-tuple-element.636, f32[32,32,128]{2,1,0:T(8,128)S(1)} %get-tuple-element.637, f32[32]{0:T(128)S(1)} %dynamic-slice_bitcast_fusion.4, pred[]{:T(512)S(6)} %compare.3, pred[]{:T(512)S(6)} %lt.69), kind=kLoop, calls=%fused_computation.4.clone.1 | loop fusion | flops 524288 | bytes 1572998 | tf_op jit(solution)/shard_map/while/body/eval_jaxpr/jit(_where)/select_n | solution.py:27
  104.0 2.5 %psum.14 = f32[256]{0:T(256)S(1)} all-reduce(f32[256]{0:T(256)S(1)} %get-tuple-element.467), channel_id=1, replica_groups=mesh['traj'=2,'ctx'=8,'head'=2] {'head'}, use_global_device_ids=true, to_apply=%region_5.6 | all-reduce | flops 256 | bytes 2048 | tf_op jit(solution)/shard_map/psum | solution.py:162
  107.2 2.4 %psum.15 = f32[256]{0:T(256)S(1)} all-reduce(f32[256]{0:T(256)S(1)} %bitcast.121), channel_id=1, replica_groups=mesh['traj'=2,'ctx'=8,'head'=2] {'head'}, use_global_device_ids=true, to_apply=%region_6.7 | all-reduce | flops 256 | bytes 2048 | tf_op jit(solution)/shard_map/psum | solution.py:164
  (82 shorter events, 13.4 us)
Async XLA Ops:
  7.2 4.0 %copy-start = (bf16[256,128]{1,0:T(8,128)(2,1)S(1)}, bf16[256,128]{1,0:T(8,128)(2,1)}, u32[]{:S(2)}) copy-start(bf16[256,128]{1,0:T(8,128)(2,1)} %param.19) | copy-start | bytes 196612
  7.2 5.2 %copy-start.1 = (bf16[256,128]{1,0:T(8,128)(2,1)S(1)}, bf16[256,128]{1,0:T(8,128)(2,1)}, u32[]{:S(2)}) copy-start(bf16[256,128]{1,0:T(8,128)(2,1)} %param.18) | copy-start | bytes 196612
  7.2 87.6 %all-gather.5.cloned.1.call-start = ((), (), s32[]{:S(2)}) async-start(), calls=%async_computation | async-start | bytes 4718592 | tf_op jit(solution)/shard_map/all_gather | solution.py:17
  12.4 5.9 %copy-start.4 = (s32[256]{0:T(256)S(1)}, s32[256]{0:T(256)}, u32[]{:S(2)}) copy-start(s32[256]{0:T(256)} %param.27) | copy-start | bytes 3076
  12.4 7.1 %copy-start.9 = (u32[32]{0:T(128)S(1)}, u32[32]{0:T(128)}, u32[]{:S(2)}) copy-start(u32[32]{0:T(128)} %constant.112) | copy-start | bytes 388
  12.4 8.5 %copy-start.6 = (f32[256]{0:T(256)S(1)}, f32[256]{0:T(256)}, u32[]{:S(2)}) copy-start(f32[256]{0:T(256)} %param.25) | copy-start | bytes 3076
  12.4 8.5 %copy-start.7 = (s32[256]{0:T(256)S(1)}, s32[256]{0:T(256)}, u32[]{:S(2)}) copy-start(s32[256]{0:T(256)} %param.26) | copy-start | bytes 3076
  12.4 34.8 %copy-start.2 = (f32[1024]{0:T(1024)S(1)}, f32[1024]{0:T(1024)}, u32[]{:S(2)}) copy-start(f32[1024]{0:T(1024)} %param.24) | copy-start | bytes 12292
  12.5 34.7 %copy-start.3 = (f32[1024]{0:T(1024)S(1)}, f32[1024]{0:T(1024)}, u32[]{:S(2)}) copy-start(f32[1024]{0:T(1024)} %param.23) | copy-start | bytes 12292
  94.8 8.5 %copy-start.8 = (f32[32]{0:T(128)S(1)}, f32[32]{0:T(128)}, u32[]{:S(2)}) copy-start(f32[32]{0:T(128)} %param.22) | copy-start | bytes 388
  109.6 0.6 copy-start.5
Sparse Core Ops, SparseCore 0:
  18.4 76.3 all-gather.4
where the time goes:
time: 118 us; the launch traced here: 117 us
  waiting for transfers between devices  33.8 us (29%)
  blocking collectives  28.5 us (24%)
  between operations  14.9 us (13%)
  other arithmetic  13.6 us (12%)
  loops' own time  9.62 us (8%)
  local copies, waits for them, and re-layouts  9.5 us (8%)
  matrix products  7.13 us (6%)
    all_gather x1, waiting for transfers between devices, carried_in(): pieces = jax.tree.map(lambda part: lax.all_gather(part, axis), value)  33.8 us
    unnamed x1, blocking collectives  23.6 us
    another operation x2, loops' own time, carried_in(): return lax.fori_loop(0, count - 1, hop, subtotal)  9.47 us
    select_n x7, other arithmetic, hop(): jnp.where(position < mine, new, old)  8.22 us
    dynamic_slice x7, local copies, waits for them, and re-layouts, hop(): longer = join(subtotal, jax.tree.map(lambda part: part[position], pieces))  4.54 us
    unnamed x29, local copies, waits for them, and re-layouts  3.15 us
    dot_general x4, matrix products, intra_of(): jnp.einsum('gcts,csgp->ctgp', weights, feat_part, preferred_element_type=...  2.83 us
    psum x1, blocking collectives, local(): square_total = lax.psum(square_local, 'head')  2.47 us
  transfers between devices with their start and end apart: 1, of which 1 were waited for; matrix products, arithmetic and copies ran while one was open for 8% of the time, Pallas kernels for 0%

commit v1 on v0

v1 whole, which is shorter than its diff:
```python
import functools

import jax
import jax.numpy as jnp
from jax import lax
from jax.experimental import pallas as pl
from jax.experimental.pallas import tpu as pltpu
from jax.sharding import PartitionSpec as P

HEAD_DIM = 32
SPAN = 256
GROUP = 4
EXTRA = 8
NORM_EPSILON = 1e-05
VMEM_BYTES = 24 * 1024 * 1024


def split3(value):
    high = value.astype(jnp.bfloat16).astype(jnp.float32)
    rest = value - high
    middle = rest.astype(jnp.bfloat16).astype(jnp.float32)
    return high, middle, (rest - middle).astype(jnp.bfloat16).astype(jnp.float32)


def dot(a, b, contract=((1,), (0,))):
    return lax.dot_general(a, b, (contract, ((), ())), preferred_element_type=jnp.float32)


def iota(shape, dim):
    return lax.broadcasted_iota(jnp.int32, shape, dim)


def column(row):
    n = row.shape[1]
    return jnp.sum(jnp.where(iota((n, n), 0) == iota((n, n), 1), row, 0.0), axis=1, keepdims=True)


def over_channels(per_head, first_head, channels):
    heads = per_head.shape[0]
    match = iota((heads, channels), 0) == first_head + iota((heads, channels), 1) // HEAD_DIM
    return jnp.sum(jnp.where(match, per_head, 0.0), axis=0, keepdims=True)


def selector(heads, rows, first_head, channels):
    row = iota((rows, channels), 0)
    match = (lax.rem(row, heads) == first_head + iota((rows, channels), 1) // HEAD_DIM) & (row < 3 * heads)
    return jnp.where(match, 1.0, 0.0).astype(jnp.bfloat16)


def member_index():
    return lax.rem(lax.axis_index("ctx"), GROUP)


def state_kernel(step_in, decay_log, features, b_input, rewards, keep, ends, *outs):
    pieces, (cum_out, step_out, columns_out, row_out) = outs[:GROUP], outs[GROUP:]
    heads, span = step_in.shape
    state = b_input.shape[1]
    wide = features.shape[1] // GROUP
    raw = step_in[...]
    step = jnp.maximum(raw, 0.0) + jnp.log1p(jnp.exp(-jnp.abs(raw)))
    log_decay = -jnp.exp(column(decay_log[...])) * step
    ends_row = ends[...].astype(jnp.float32)
    live = keep[...].astype(jnp.float32) * rewards[...]
    upper = jnp.where(iota((span, span), 0) <= iota((span, span), 1), 1.0, 0.0).astype(jnp.bfloat16)
    stacked = jnp.concatenate(split3(log_decay) + (jnp.broadcast_to(ends_row, (16, span)),), axis=0)
    summed = dot(stacked.astype(jnp.bfloat16), upper)
    cum = summed[:heads] + summed[heads : 2 * heads] + summed[2 * heads : 3 * heads]
    through = summed[3 * heads : 3 * heads + 1]
    before = through - ends_row
    total = cum[:, span - 1 :]
    first_sum = jnp.sum(jnp.where(before == 0.0, live, 0.0), axis=1, keepdims=True)
    still_open = jnp.where(through[:, span - 1 :] == 0.0, 1.0, 0.0)
    coefficient = jnp.exp(total - cum) * step
    pad = jnp.zeros((128 - 3 * heads, span), jnp.float32)
    by_token = jnp.concatenate(split3(coefficient) + (pad,), axis=0).T.astype(jnp.bfloat16)
    cum_out[...] = cum
    step_out[...] = step
    columns_out[:, :128] = jnp.concatenate(split3(cum) + (jnp.ones_like(pad),), axis=0).T.astype(jnp.bfloat16)
    columns_out[:, 128:] = jnp.concatenate(split3(jnp.exp(cum)) + (pad,), axis=0).T.astype(jnp.bfloat16)
    row_out[...] = jnp.concatenate([live, ends_row, through, before, jnp.zeros((4, span), jnp.float32)], axis=0)
    keys = b_input[...]
    me = member_index()
    for j in range(GROUP):
        part = lax.bitwise_xor(me, j)
        first_head = part * (heads // GROUP)
        feat = features[:, pl.ds(pl.multiple_of(part * wide, wide), wide)]
        spread = dot(by_token, selector(heads, 128, first_head, wide))
        scaled = (spread * feat.astype(jnp.float32)).astype(jnp.bfloat16)
        pieces[j][:state, :] = dot(keys, scaled, ((0,), (0,)))
        row = iota((EXTRA, wide), 0)
        pieces[j][state:, :] = jnp.where(
            row == 0, over_channels(total, first_head, wide), jnp.where(row == 1, still_open, first_sum)
        )


def intra_kernel(features, b_input, c_input, cum_ref, step_ref, columns, rows, skip, out, suffix):
    heads, span = cum_ref.shape
    at_once = 128 // HEAD_DIM
    t, s = iota((span, span), 0), iota((span, span), 1)
    scores = jnp.where(t >= s, dot(c_input[...], b_input[...], ((1,), (1,))), 0.0)
    by_token = columns[:, :128]
    skip_row = over_channels(column(skip[...]), 0, heads * HEAD_DIM)
    out[...] = features[...].astype(jnp.float32) * skip_row
    row = iota((128, span), 0)

    def some_heads(index, carry):
        first = index * at_once
        lanes = pl.ds(pl.multiple_of(index * 128, 128), 128)
        feat = features[:, lanes]
        total = out[:, lanes]
        owner = iota((span, 128), 1) // HEAD_DIM
        for j in range(at_once):
            head = first + j
            cum = cum_ref[pl.ds(head, 1), :]
            high, middle, low = split3(cum)
            other = jnp.where(
                row < 3 * heads,
                jnp.where(lax.rem(row, heads) == head, 1.0, 0.0),
                jnp.where(
                    row == 3 * heads,
                    -high,
                    jnp.where(row == 3 * heads + 1, -middle, jnp.where(row == 3 * heads + 2, -low, 0.0)),
                ),
            ).astype(jnp.bfloat16)
            gap = jnp.minimum(dot(by_token, other), 0.0)
            weights = (scores * jnp.exp(gap) * step_ref[pl.ds(head, 1), :]).astype(jnp.bfloat16)
            total = total + dot(weights, jnp.where(owner == j, feat, jnp.zeros_like(feat)))
        out[:, lanes] = total
        return carry

    lax.fori_loop(0, heads // at_once, some_heads, 0)

    live, through, before = rows[0:1, :], rows[2:3, :], rows[3:4, :]
    reach = jnp.where((t >= s) & (column(before) == before), column(live), 0.0)
    sums = jnp.sum(reach, axis=0, keepdims=True)
    open_end = jnp.where(before == through[:, span - 1 :], 1.0, 0.0)
    suffix[...] = jnp.concatenate([sums, open_end, jnp.zeros((6, span), jnp.float32)], axis=0)


def in_order(pieces, me_static):
    return [pieces[me_static ^ m] for m in range(GROUP)]


def total_kernel(*refs):
    pieces, out = refs[:GROUP], refs[GROUP]
    state = pieces[0].shape[0] - EXTRA
    me = member_index()
    for v in range(GROUP):

        @pl.when(me == v)
        def _():
            members = in_order(pieces, v)
            running = members[0][:state, :]
            for piece in members[1:]:
                running = jnp.exp(piece[state : state + 1, :]) * running + piece[:state, :]
            out[:state, :] = running
            extra = [piece[state:, :] for piece in members]
            decay = functools.reduce(lambda a, b: a + b, [e[0:1] for e in extra])
            keeps = functools.reduce(lambda a, b: a * b, [e[1:2] for e in extra])
            amount = extra[-1][2:3]
            for e in extra[-2::-1]:
                amount = e[2:3] + e[1:2] * amount
            row = iota((EXTRA, decay.shape[1]), 0)
            out[state:, :] = jnp.where(row == 0, decay, jnp.where(row == 1, keeps, amount))


def round_kernel(bit, *refs):
    total, got, before, total_out, before_out = refs
    state = total.shape[0] - EXTRA
    group = lax.axis_index("ctx") // GROUP
    row = iota((EXTRA, total.shape[1]), 0)
    mine, theirs, past = total[state:, :], got[state:, :], before[state:, :]

    def rows(decay, keeps, amount):
        return jnp.where(row == 0, decay, jnp.where(row == 1, keeps, amount))

    decay, keeps = mine[0:1] + theirs[0:1], mine[1:2] * theirs[1:2]

    @pl.when(lax.rem(group // bit, 2) == 1)
    def _():
        before_out[:state, :] = before[:state, :] + jnp.exp(past[0:1]) * got[:state, :]
        before_out[state:, :] = rows(past[0:1] + theirs[0:1], past[1:2], past[2:3])
        total_out[:state, :] = total[:state, :] + jnp.exp(mine[0:1]) * got[:state, :]
        total_out[state:, :] = rows(decay, keeps, theirs[2:3] + theirs[1:2] * mine[2:3])

    @pl.when(lax.rem(group // bit, 2) == 0)
    def _():
        before_out[:state, :] = before[:state, :]
        before_out[state:, :] = rows(past[0:1], past[1:2] * theirs[1:2], past[2:3] + past[1:2] * theirs[2:3])
        total_out[:state, :] = got[:state, :] + jnp.exp(theirs[0:1]) * total[:state, :]
        total_out[state:, :] = rows(decay, keeps, mine[2:3] + mine[1:2] * theirs[2:3])


def entering_kernel(bit, has_past, *refs):
    pieces, got = refs[:GROUP], refs[GROUP]
    past = refs[GROUP + 1] if has_past else None
    outs, carry_out = refs[-GROUP - 1 : -1], refs[-1]
    state = got.shape[0] - EXTRA
    ctx = lax.axis_index("ctx")
    me = lax.rem(ctx, GROUP)
    is_later = lax.rem(ctx // GROUP // bit, 2) == 1
    theirs = got[state:, :]
    for v in range(GROUP):

        @pl.when(me == v)
        def _():
            members = in_order(pieces, v)
            arriving = jnp.where(is_later, got[:state, :], 0.0)
            amount = jnp.where(is_later, 0.0, theirs[2:3])
            if has_past:
                old = past[state:, :]
                arriving = past[:state, :] + jnp.exp(old[0:1]) * arriving
                amount = old[2:3] + old[1:2] * amount
            for m in range(GROUP):
                outs[v ^ m][...] = arriving
                if m < GROUP - 1:
                    piece = members[m]
                    arriving = jnp.exp(piece[state : state + 1, :]) * arriving + piece[:state, :]
            for m in range(GROUP - 1, v, -1):
                extra = members[m][state:, :]
                amount = extra[2:3] + extra[1:2] * amount
            carry_out[...] = jnp.broadcast_to(amount, carry_out.shape)


def readout_kernel(*refs):
    entering, (c_input, columns, inside, weight, gain, out) = refs[:GROUP], refs[GROUP:]
    state, wide = entering[0].shape
    span = c_input.shape[0]
    heads = inside.shape[1] // HEAD_DIM
    me = member_index()
    queries = c_input[...]
    by_token = columns[:, 128:]
    squares = jnp.zeros((span, 128), jnp.float32)
    values = jnp.zeros((span, 128), jnp.float32)
    for j in range(GROUP):
        part = lax.bitwise_xor(me, j)
        lanes = pl.ds(pl.multiple_of(part * wide, wide), wide)
        value = entering[j][...]
        high = value.astype(jnp.bfloat16)
        low = (value - high.astype(jnp.float32)).astype(jnp.bfloat16)
        carried = dot(queries, high) + dot(queries, low)
        decay = dot(by_token, selector(heads, 128, part * (heads // GROUP), wide))
        mixed = inside[:, lanes] + carried * decay
        readout = weight[:, lanes] * gain[:, lanes]
        squared, read = mixed * mixed, mixed * readout
        for k in range(0, wide, 128):
            squares = squares + squared[:, k : k + 128]
            values = values + read[:, k : k + 128]
    out[0:1, :] = jnp.sum(squares.T, axis=0, keepdims=True)
    out[1:2, :] = jnp.sum(values.T, axis=0, keepdims=True)


def call(kernel, shapes, name, *args):
    single = not isinstance(shapes, (list, tuple))
    structs = [jax.ShapeDtypeStruct(s, d) for s, d in ([shapes] if single else shapes)]
    result = pl.pallas_call(
        kernel,
        out_shape=structs,
        in_specs=[pl.BlockSpec(memory_space=pltpu.VMEM)] * len(args),
        out_specs=[pl.BlockSpec(memory_space=pltpu.VMEM)] * len(structs),
        compiler_params=pltpu.CompilerParams(vmem_limit_bytes=VMEM_BYTES),
        name=name,
    )(*args)
    return result


def swap(value, axis, mask):
    count = lax.axis_size(axis)
    return lax.ppermute(value, axis, [(k, k ^ mask) for k in range(count)])


def local(
    features,
    b_input,
    c_input,
    step_input,
    decay_log,
    skip_gain,
    norm_gain,
    value_weight,
    rewards,
    reward_keep_mask,
    episode_end,
):
    span, width = features.shape
    heads = step_input.shape[0]
    state = b_input.shape[1]
    wide = width // GROUP
    count = lax.axis_size("ctx")
    groups = count // GROUP
    assert span == SPAN and count == groups * GROUP and groups > 1 and groups & (groups - 1) == 0
    f32, bf16 = jnp.float32, jnp.bfloat16
    piece = ((state + EXTRA, wide), f32)

    made = call(
        state_kernel,
        [piece] * GROUP
        + [((heads, span), f32), ((heads, span), f32), ((span, 256), bf16), ((8, span), f32)],
        "block_states",
        step_input,
        decay_log[None, :],
        features,
        b_input,
        rewards[None, :],
        reward_keep_mask[None, :],
        episode_end[None, :],
    )
    pieces, (cum, step, columns, rows) = made[:GROUP], made[GROUP:]
    got = [pieces[0]] + [swap(pieces[j], "ctx", j) for j in range(1, GROUP)]
    inside, suffix = call(
        intra_kernel,
        [((span, width), f32), ((8, span), f32)],
        "inside_block",
        features,
        b_input,
        c_input,
        cum,
        step,
        columns,
        rows,
        skip_gain[None, :],
    )
    (total,) = call(total_kernel, [piece], "group_total", *got)
    past = None
    bit = 1
    while bit * 2 < groups:
        other = swap(total, "ctx", GROUP * bit)
        if past is None:
            row = jnp.arange(state + EXTRA)[:, None]
            past = jnp.where(row == state + 1, 1.0, 0.0).astype(f32) * jnp.ones((1, wide), f32)
        total, past = call(
            functools.partial(round_kernel, bit), [piece, piece], "scan_round", total, other, past
        )
        bit *= 2
    other = swap(total, "ctx", GROUP * bit)
    made = call(
        functools.partial(entering_kernel, bit, past is not None),
        [((state, wide), f32)] * GROUP + [((8, wide), f32)],
        "entering_states",
        *got,
        other,
        *([] if past is None else [past]),
    )
    entering, carry = made[:GROUP], made[GROUP]
    arrived = [entering[0]] + [swap(entering[j], "ctx", j) for j in range(1, GROUP)]
    (sums,) = call(
        readout_kernel,
        [((2, span), f32)],
        "readout",
        *arrived,
        c_input,
        columns,
        inside,
        value_weight[None, :],
        norm_gain[None, :],
    )
    sums = sums + swap(sums, "head", 1)
    mean_square = sums[0] / (width * lax.axis_size("head"))
    values = sums[1] / jnp.sqrt(mean_square + NORM_EPSILON)
    returns = suffix[0] + suffix[1] * carry[0, 0]
    return (values, returns - values)


def solution(mesh):
    placed = (
        P(("traj", "ctx"), "head"),
        P(("traj", "ctx"), None),
        P(("traj", "ctx"), None),
        P("head", ("traj", "ctx")),
        P("head"),
        P("head"),
        P("head"),
        P("head"),
        P(("traj", "ctx")),
        P(("traj", "ctx")),
        P(("traj", "ctx")),
    )
    return jax.shard_map(
        local,
        mesh=mesh,
        in_specs=placed,
        out_specs=(P(("traj", "ctx")), P(("traj", "ctx"))),
        check_vma=False,
    )
```

time: 118 us -> 38.7 us (0.33)
  blocking collectives: 28.5 us -> 0 us
  waiting for transfers between devices: 33.8 us -> 12.8 us
  between operations: 14.9 us -> 0.77 us
  other arithmetic: 13.6 us -> 1.23 us
  starting transfers between devices: 0.04 us -> 11 us
  loops' own time: 9.62 us -> 0 us
  matrix products: 7.13 us -> 0 us
  Pallas kernels: 0 us -> 6.8 us
  local copies, waits for them, and re-layouts: 9.5 us -> 5.72 us
    all_gather x1 -> x0, waiting for transfers between devices: 33.8 us -> none  [carried_in(): pieces = jax.tree.map(lambda part: lax.all_gather(part, axis), value)]
    unnamed x1 -> x0, blocking collectives: 23.6 us -> none
    ppermute x0 -> x8, waiting for transfers between devices: none -> 12.8 us  [swap(): return lax.ppermute(value, axis, [(k, k ^ mask) for k in range(count)])]
    ppermute x0 -> x8, starting transfers between devices: none -> 11 us  [swap(): return lax.ppermute(value, axis, [(k, k ^ mask) for k in range(count)])]
    another operation x3 -> x0, loops' own time: 9.62 us -> none  [the longest x2 9.47 us: carried_in(): return lax.fori_loop(0, count - 1, hop, subtotal)]
    select_n x7 -> x0, other arithmetic: 8.22 us -> none  [hop(): jnp.where(position < mine, new, old)]
    dot_general x13 -> x0, matrix products: 7.13 us -> none  [the longest x4 2.83 us: intra_of(): jnp.einsum('gcts,csgp->ctgp', weights, feat_part, preferred_element_type=...]
    pallas_call x0 -> x5, Pallas kernels: none -> 6.8 us  [call(): pl.pallas_call(kernel, out_shape=structs, in_specs=[pl.BlockSpec(memory_s...]
  transfers between devices with their start and end apart: 1 -> 8, of which waited for: 1 -> 5; matrix products, arithmetic and copies ran while one was open for 8% -> 3% of each run, Pallas kernels for 0% -> 12%
where the time goes in v1:
time: 38.7 us; the launch traced here: 38.3 us
  waiting for transfers between devices  12.8 us (33%)
  starting transfers between devices  11 us (28%)
  Pallas kernels  6.8 us (18%)
  local copies, waits for them, and re-layouts  5.72 us (15%)
  other arithmetic  1.23 us (3%)
  between operations  0.77 us (2%)
    ppermute x8, waiting for transfers between devices, swap(): return lax.ppermute(value, axis, [(k, k ^ mask) for k in range(count)])  12.8 us
    ppermute x8, starting transfers between devices, swap(): return lax.ppermute(value, axis, [(k, k ^ mask) for k in range(count)])  11 us
    pallas_call x5, Pallas kernels, call(): pl.pallas_call(kernel, out_shape=structs, in_specs=[pl.BlockSpec(memory_s...  6.8 us
    unnamed x28, local copies, waits for them, and re-layouts  5.21 us
  transfers between devices with their start and end apart: 8, of which 5 were waited for; matrix products, arithmetic and copies ran while one was open for 3% of the time, Pallas kernels for 12%

profile of v1, /device:TPU:0, one launch (start us, length us, event | category | flops | bytes accessed | tf_op | source)
XLA Modules:
  0.0 38.3 jit_solution(13218769317460941826)
XLA Ops:
  0.7 0.6 %copy-done.9 = s32[256]{0:T(256)S(1)} copy-done((s32[256]{0:T(256)S(1)}, s32[256]{0:T(256)}, u32[]{:S(2)}) %copy-start.9) | copy-done | bytes 1048
  1.3 1.0 %copy-done = bf16[256,1024]{1,0:T(8,128)(2,1)S(1)} copy-done((bf16[256,1024]{1,0:T(8,128)(2,1)S(1)}, bf16[256,1024]{1,0:T(8,128)(2,1)}, u32[]{:S(2)}) %copy-start) | copy-done | bytes 524312
  2.4 0.8 %copy-done.3 = bf16[256,128]{1,0:T(8,128)(2,1)S(1)} copy-done((bf16[256,128]{1,0:T(8,128)(2,1)S(1)}, bf16[256,128]{1,0:T(8,128)(2,1)}, u32[]{:S(2)}) %copy-start.3) | copy-done | bytes 65560
  3.2 0.8 %copy-done.5 = f32[32,256]{1,0:T(8,128)S(1)} copy-done((f32[32,256]{1,0:T(8,128)S(1)}, f32[32,256]{1,0:T(8,128)}, u32[]{:S(2)}) %copy-start.5) | copy-done | bytes 32792
  4.0 1.2 %block_states.1 = (f32[136,256]{1,0:T(8,128)S(1)}, f32[136,256]{1,0:T(8,128)S(1)}, f32[136,256]{1,0:T(8,128)S(1)}, f32[136,256]{1,0:T(8,128)S(1)}, f32[32,256]{1...) custom-call(f32[32,256]{1,0:T(8,128)S(1)} %copy-done.5, ...), custom_call_target="tpu_custom_call" | custom-call | tf_op jit(solution)/shard_map/block_states/pallas_call | solution.py:256
  5.2 3.0 %collective-permute-start = (f32[136,256]{1,0:T(8,128)S(1)}, f32[136,256]{1,0:T(8,128)S(1)}, u32[]{:S(2)}, u32[]{:S(2)}) collective-permute-start(f32[136,256]{1,0:T(8,128)S(1)} %get-tuple-element.18), channel_id=1, source_target_pairs={{0,2},{2,0},{4,6},{6,4},{8,10},{10,8},{12,14},{14,12},{1,3},{3,1},... | collective-permute-start | bytes 417800 | tf_op jit(solution)/shard_map/ppermute | solution.py:269
  8.2 1.6 %collective-permute-start.1 = (f32[136,256]{1,0:T(8,128)S(1)}, f32[136,256]{1,0:T(8,128)S(1)}, u32[]{:S(2)}, u32[]{:S(2)}) collective-permute-start(f32[136,256]{1,0:T(8,128)S(1)} %get-tuple-element.19), channel_id=1, source_target_pairs={{0,4},{2,6},{4,0},{6,2},{8,12},{10,14},{12,8},{14,10},{1,5},{3,7},... | collective-permute-start | bytes 417800 | tf_op jit(solution)/shard_map/ppermute | solution.py:269
  9.8 2.1 %collective-permute-done.refs_1_ = f32[136,256]{1,0:T(8,128)S(1)} collective-permute-done((f32[136,256]{1,0:T(8,128)S(1)}, f32[136,256]{1,0:T(8,128)S(1)}, u32[]{:S(2)}, u32[]{:S(2)}) %collective-permute-start) | collective-permute-done | bytes 139296 | tf_op jit(solution)/shard_map/ppermute | solution.py:269
  11.9 2.9 %collective-permute-done.1.refs_2_ = f32[136,256]{1,0:T(8,128)S(1)} collective-permute-done((f32[136,256]{1,0:T(8,128)S(1)}, f32[136,256]{1,0:T(8,128)S(1)}, u32[]{:S(2)}, u32[]{:S(2)}) %collective-permute-start.1) | collective-permute-done | bytes 139296 | tf_op jit(solution)/shard_map/ppermute | solution.py:269
  14.8 1.3 %collective-permute-done.2.refs_3_ = f32[136,256]{1,0:T(8,128)S(1)} collective-permute-done((f32[136,256]{1,0:T(8,128)S(1)}, f32[136,256]{1,0:T(8,128)S(1)}, u32[]{:S(2)}, u32[]{:S(2)}) %collective-permute-start.2) | collective-permute-done | bytes 139296 | tf_op jit(solution)/shard_map/ppermute | solution.py:269
  16.2 2.8 %collective-permute-start.3 = (f32[136,256]{1,0:T(8,128)S(1)}, f32[136,256]{1,0:T(8,128)S(1)}, u32[]{:S(2)}, u32[]{:S(2)}) collective-permute-start(f32[136,256]{1,0:T(8,128)S(1)} %group_total.1), channel_id=1, source_target_pairs={{0,8},{2,10},{4,12},{6,14},{8,0},{10,2},{12,4},{14,6},{1,9},{3,11}... | collective-permute-start | bytes 417800 | tf_op jit(solution)/shard_map/ppermute | solution.py:269
  19.1 5.9 %collective-permute-done.3.refs_4_ = f32[136,256]{1,0:T(8,128)S(1)} collective-permute-done((f32[136,256]{1,0:T(8,128)S(1)}, f32[136,256]{1,0:T(8,128)S(1)}, u32[]{:S(2)}, u32[]{:S(2)}) %collective-permute-start.3) | collective-permute-done | bytes 139296 | tf_op jit(solution)/shard_map/ppermute | solution.py:269
  25.1 1.1 %collective-permute-start.4 = (f32[128,256]{1,0:T(8,128)S(1)}, f32[128,256]{1,0:T(8,128)S(1)}, u32[]{:S(2)}, u32[]{:S(2)}) collective-permute-start(f32[128,256]{1,0:T(8,128)S(1)} %get-tuple-element.22), channel_id=1, source_target_pairs={{0,2},{2,0},{4,6},{6,4},{8,10},{10,8},{12,14},{14,12},{1,3},{3,1},... | collective-permute-start | bytes 393224 | tf_op jit(solution)/shard_map/ppermute | solution.py:269
  26.2 0.6 %collective-permute-start.5 = (f32[128,256]{1,0:T(8,128)S(1)}, f32[128,256]{1,0:T(8,128)S(1)}, u32[]{:S(2)}, u32[]{:S(2)}) collective-permute-start(f32[128,256]{1,0:T(8,128)S(1)} %get-tuple-element.23), channel_id=1, source_target_pairs={{0,4},{2,6},{4,0},{6,2},{8,12},{10,14},{12,8},{14,10},{1,5},{3,7},... | collective-permute-start | bytes 393224 | tf_op jit(solution)/shard_map/ppermute | solution.py:269
  26.9 1.8 %collective-permute-start.6 = (f32[128,256]{1,0:T(8,128)S(1)}, f32[128,256]{1,0:T(8,128)S(1)}, u32[]{:S(2)}, u32[]{:S(2)}) collective-permute-start(f32[128,256]{1,0:T(8,128)S(1)} %get-tuple-element.24), channel_id=1, source_target_pairs={{0,6},{2,4},{4,2},{6,0},{8,14},{10,12},{12,10},{14,8},{1,7},{3,5},... | collective-permute-start | bytes 393224 | tf_op jit(solution)/shard_map/ppermute | solution.py:269
  28.6 0.6 %copy-done.11 = f32[32]{0:T(128)S(1)} copy-done((f32[32]{0:T(128)S(1)}, f32[32]{0:T(128)}, u32[]{:S(2)}) %copy-start.11) | copy-done | bytes 152
  29.3 4.7 %inside_block.1 = (f32[256,1024]{1,0:T(8,128)S(1)}, f32[8,256]{1,0:T(8,128)S(1)}) custom-call(bf16[256,1024]{1,0:T(8,128)(2,1)S(1)} %copy-done.1, bf16[256,128]{1,0:T(8,128)(2,1)S(1)} %copy-done.4, bf16[256,128]{1,0:T(8,128)(2,1)S(1)} %copy-done.2, f32[32,256]{1,0:T(8,128)S(1)} %get-tuple-element.26.cum_ref, f32[32,256]{1,0:T(8,128)S(1)} %get-tuple-element.27.step_ref, ...), custom_call_target="tpu_custom_call" | custom-call | tf_op jit(solution)/shard_map/inside_block/pallas_call | solution.py:256
  34.0 0.5 %slice.19 = f32[1,1]{1,0:T(1,128)} slice(f32[8,256]{1,0:T(8,128)S(1)} %get-tuple-element.31), slice={[0:1], [0:1]} | slice | bytes 8 | tf_op jit(solution)/shard_map/slice | solution.py:360
  34.7 0.5 %copy-done.6 = f32[1024]{0:T(1024)S(1)} copy-done((f32[1024]{0:T(1024)S(1)}, f32[1024]{0:T(1024)}, u32[]{:S(2)}) %copy-start.6) | copy-done | bytes 4120
  35.2 0.7 %readout.1 = f32[2,256]{1,0:T(2,128)S(1)} custom-call(f32[128,256]{1,0:T(8,128)S(1)} %get-tuple-element.21.refs_0_, f32[128,256]{1,0:T(8,128)S(1)} %collective-permute-done.4.refs_1_, f32[128,256]{1,0:T(8,128)S(1)} %collective-permute-done.5.refs_2_, f32[128,256]{1,0:T(8,128)S(1)} %collective-permute-done.6.refs_3_, bf16[256,128]{1,0:T(8,128)(2,1)S(1)} %copy-done.2, ...), custom_call_target="tpu_custom_call" | custom-call | tf_op jit(solution)/shard_map/readout/pallas_call | solution.py:256
  36.0 0.7 %multiply_add_fusion = f32[1,256]{1,0:T(1,128)S(1)} fusion(f32[8,256]{1,0:T(8,128)S(1)} %get-tuple-element.30, f32[]{:T(128)} %bitcast.8), kind=kLoop, calls=%fused_computation.4 | loop fusion | flops 512 | bytes 3076 | tf_op jit(solution)/shard_map/add | solution.py:360
  36.7 0.5 %collective-permute-done.7 = f32[2,256]{1,0:T(2,128)S(1)} collective-permute-done((f32[2,256]{1,0:T(2,128)S(1)}, f32[2,256]{1,0:T(2,128)S(1)}, u32[]{:S(2)}, u32[]{:S(2)}) %collective-permute-start.7) | collective-permute-done | bytes 2080 | tf_op jit(solution)/shard_map/ppermute | solution.py:269
  37.2 0.6 %copy-done.13 = f32[1,256]{1,0:T(1,128)} copy-done((f32[1,256]{1,0:T(1,128)}, f32[1,256]{1,0:T(1,128)S(1)}, u32[]{:S(2)}) %copy-start.13) | copy-done | bytes 1048
  37.8 0.6 %sub.3 = f32[256]{0:T(256)} subtract(f32[256]{0:T(256)S(1)} %bitcast.19, f32[256]{0:T(256)S(1)} %bitcast.17) | non-fusion elementwise | flops 256 | bytes 3072 | tf_op jit(solution)/shard_map/sub | solution.py:361
  (30 shorter events, 0.4 us)
Async XLA Ops:
  0.6 0.7 %copy-start.9 = (s32[256]{0:T(256)S(1)}, s32[256]{0:T(256)}, u32[]{:S(2)}) copy-start(s32[256]{0:T(256)} %param.20) | copy-start | bytes 3076
  0.6 0.7 %copy-start.10 = (s32[256]{0:T(256)S(1)}, s32[256]{0:T(256)}, u32[]{:S(2)}) copy-start(s32[256]{0:T(256)} %param.21) | copy-start | bytes 3076
  0.7 0.7 %copy-start.8 = (f32[256]{0:T(256)S(1)}, f32[256]{0:T(256)}, u32[]{:S(2)}) copy-start(f32[256]{0:T(256)} %param.19) | copy-start | bytes 3076
  0.7 0.7 %copy-start.12 = (f32[32]{0:T(128)S(1)}, f32[32]{0:T(128)}, u32[]{:S(2)}) copy-start(f32[32]{0:T(128)} %param.15) | copy-start | bytes 388
  1.3 1.0 %copy-start = (bf16[256,1024]{1,0:T(8,128)(2,1)S(1)}, bf16[256,1024]{1,0:T(8,128)(2,1)}, u32[]{:S(2)}) copy-start(bf16[256,1024]{1,0:T(8,128)(2,1)} %features.3) | copy-start | bytes 1572868
  2.4 0.8 %copy-start.3 = (bf16[256,128]{1,0:T(8,128)(2,1)S(1)}, bf16[256,128]{1,0:T(8,128)(2,1)}, u32[]{:S(2)}) copy-start(bf16[256,128]{1,0:T(8,128)(2,1)} %b_input.3) | copy-start | bytes 196612
  3.2 0.8 %copy-start.5 = (f32[32,256]{1,0:T(8,128)S(1)}, f32[32,256]{1,0:T(8,128)}, u32[]{:S(2)}) copy-start(f32[32,256]{1,0:T(8,128)} %step_in.1) | copy-start | bytes 98308
  5.2 6.7 %collective-permute-start = (f32[136,256]{1,0:T(8,128)S(1)}, f32[136,256]{1,0:T(8,128)S(1)}, u32[]{:S(2)}, u32[]{:S(2)}) collective-permute-start(f32[136,256]{1,0:T(8,128)S(1)} %get-tuple-element.18), channel_id=1, source_target_pairs={{0,2},{2,0},{4,6},{6,4},{8,10},{10,8},{12,14},{14,12},{1,3},{3,1},... | collective-permute-start | bytes 417800 | tf_op jit(solution)/shard_map/ppermute | solution.py:269
  8.2 6.6 %collective-permute-start.1 = (f32[136,256]{1,0:T(8,128)S(1)}, f32[136,256]{1,0:T(8,128)S(1)}, u32[]{:S(2)}, u32[]{:S(2)}) collective-permute-start(f32[136,256]{1,0:T(8,128)S(1)} %get-tuple-element.19), channel_id=1, source_target_pairs={{0,4},{2,6},{4,0},{6,2},{8,12},{10,14},{12,8},{14,10},{1,5},{3,7},... | collective-permute-start | bytes 417800 | tf_op jit(solution)/shard_map/ppermute | solution.py:269
  9.8 6.3 %collective-permute-start.2 = (f32[136,256]{1,0:T(8,128)S(1)}, f32[136,256]{1,0:T(8,128)S(1)}, u32[]{:S(2)}, u32[]{:S(2)}) collective-permute-start(f32[136,256]{1,0:T(8,128)S(1)} %get-tuple-element.20), channel_id=1, source_target_pairs={{0,6},{2,4},{4,2},{6,0},{8,14},{10,12},{12,10},{14,8},{1,7},{3,5},... | collective-permute-start | bytes 417800 | tf_op jit(solution)/shard_map/ppermute | solution.py:269
  16.2 12.4 %copy-start.1 = (bf16[256,1024]{1,0:T(8,128)(2,1)S(1)}, bf16[256,1024]{1,0:T(8,128)(2,1)}, u32[]{:S(2)}) copy-start(bf16[256,1024]{1,0:T(8,128)(2,1)} %features.3) | copy-start | bytes 1572868
  16.2 12.4 %copy-start.2 = (bf16[256,128]{1,0:T(8,128)(2,1)S(1)}, bf16[256,128]{1,0:T(8,128)(2,1)}, u32[]{:S(2)}) copy-start(bf16[256,128]{1,0:T(8,128)(2,1)} %refs_4_.1) | copy-start | bytes 196612
  16.2 12.4 %copy-start.4 = (bf16[256,128]{1,0:T(8,128)(2,1)S(1)}, bf16[256,128]{1,0:T(8,128)(2,1)}, u32[]{:S(2)}) copy-start(bf16[256,128]{1,0:T(8,128)(2,1)} %b_input.3) | copy-start | bytes 196612
  16.2 8.8 %collective-permute-start.3 = (f32[136,256]{1,0:T(8,128)S(1)}, f32[136,256]{1,0:T(8,128)S(1)}, u32[]{:S(2)}, u32[]{:S(2)}) collective-permute-start(f32[136,256]{1,0:T(8,128)S(1)} %group_total.1), channel_id=1, source_target_pairs={{0,8},{2,10},{4,12},{6,14},{8,0},{10,2},{12,4},{14,6},{1,9},{3,11}... | collective-permute-start | bytes 417800 | tf_op jit(solution)/shard_map/ppermute | solution.py:269
  25.1 9.5 %collective-permute-start.4 = (f32[128,256]{1,0:T(8,128)S(1)}, f32[128,256]{1,0:T(8,128)S(1)}, u32[]{:S(2)}, u32[]{:S(2)}) collective-permute-start(f32[128,256]{1,0:T(8,128)S(1)} %get-tuple-element.22), channel_id=1, source_target_pairs={{0,2},{2,0},{4,6},{6,4},{8,10},{10,8},{12,14},{14,12},{1,3},{3,1},... | collective-permute-start | bytes 393224 | tf_op jit(solution)/shard_map/ppermute | solution.py:269
  26.2 8.4 %collective-permute-start.5 = (f32[128,256]{1,0:T(8,128)S(1)}, f32[128,256]{1,0:T(8,128)S(1)}, u32[]{:S(2)}, u32[]{:S(2)}) collective-permute-start(f32[128,256]{1,0:T(8,128)S(1)} %get-tuple-element.23), channel_id=1, source_target_pairs={{0,4},{2,6},{4,0},{6,2},{8,12},{10,14},{12,8},{14,10},{1,5},{3,7},... | collective-permute-start | bytes 393224 | tf_op jit(solution)/shard_map/ppermute | solution.py:269
  26.9 7.7 %collective-permute-start.6 = (f32[128,256]{1,0:T(8,128)S(1)}, f32[128,256]{1,0:T(8,128)S(1)}, u32[]{:S(2)}, u32[]{:S(2)}) collective-permute-start(f32[128,256]{1,0:T(8,128)S(1)} %get-tuple-element.24), channel_id=1, source_target_pairs={{0,6},{2,4},{4,2},{6,0},{8,14},{10,12},{12,10},{14,8},{1,7},{3,5},... | collective-permute-start | bytes 393224 | tf_op jit(solution)/shard_map/ppermute | solution.py:269
  28.6 0.7 %copy-start.11 = (f32[32]{0:T(128)S(1)}, f32[32]{0:T(128)}, u32[]{:S(2)}) copy-start(f32[32]{0:T(128)} %param.16) | copy-start | bytes 388
  34.0 0.7 %copy-start.7 = (f32[1024]{0:T(1024)S(1)}, f32[1024]{0:T(1024)}, u32[]{:S(2)}) copy-start(f32[1024]{0:T(1024)} %param.17) | copy-start | bytes 12292
  34.6 0.7 %copy-start.6 = (f32[1024]{0:T(1024)S(1)}, f32[1024]{0:T(1024)}, u32[]{:S(2)}) copy-start(f32[1024]{0:T(1024)} %param.18) | copy-start | bytes 12292
  36.0 1.2 %collective-permute-start.7 = (f32[2,256]{1,0:T(2,128)S(1)}, f32[2,256]{1,0:T(2,128)S(1)}, u32[]{:S(2)}, u32[]{:S(2)}) collective-permute-start(f32[2,256]{1,0:T(2,128)S(1)} %readout.1), channel_id=1, source_target_pairs={{0,1},{1,0},{2,3},{3,2},{4,5},{5,4},{6,7},{7,6},{8,9},{9,8},{10,11... | collective-permute-start | bytes 6152 | tf_op jit(solution)/shard_map/ppermute | solution.py:269
  37.2 0.6 %copy-start.13 = (f32[1,256]{1,0:T(1,128)}, f32[1,256]{1,0:T(1,128)S(1)}, u32[]{:S(2)}) copy-start(f32[1,256]{1,0:T(1,128)S(1)} %fusion.2) | copy-start | bytes 3076

commit v2 on v1

--- a/solution.py
+++ b/solution.py
@@ -51,11 +51,20 @@
     return lax.rem(lax.axis_index("ctx"), GROUP)
 
 
-def state_kernel(step_in, decay_log, features, b_input, rewards, keep, ends, *outs):
-    pieces, (cum_out, step_out, columns_out, row_out) = outs[:GROUP], outs[GROUP:]
+def state_kernel(*refs):
+    sources, refs = refs[:11], refs[11:]
+    pieces, refs = refs[:GROUP], refs[GROUP:]
+    features, b_input, c_input, cum_out, step_out, columns_out, row_out, wide_out = refs[:8]
+    step_in, decay_log, skip_gain, norm_gain, value_weight, rewards, keep, ends, sems = refs[8:]
+    targets = (step_in, decay_log, rewards, keep, ends, features, b_input, c_input, skip_gain, norm_gain, value_weight)
+    copies = [pltpu.make_async_copy(src, dst, sems.at[i]) for i, (src, dst) in enumerate(zip(sources, targets))]
+    for copy in copies:
+        copy.start()
     heads, span = step_in.shape
     state = b_input.shape[1]
     wide = features.shape[1] // GROUP
+    for copy in copies[:5]:
+        copy.wait()
     raw = step_in[...]
     step = jnp.maximum(raw, 0.0) + jnp.log1p(jnp.exp(-jnp.abs(raw)))
     log_decay = -jnp.exp(column(decay_log[...])) * step
@@ -73,14 +82,11 @@
     coefficient = jnp.exp(total - cum) * step
     pad = jnp.zeros((128 - 3 * heads, span), jnp.float32)
     by_token = jnp.concatenate(split3(coefficient) + (pad,), axis=0).T.astype(jnp.bfloat16)
-    cum_out[...] = cum
-    step_out[...] = step
-    columns_out[:, :128] = jnp.concatenate(split3(cum) + (jnp.ones_like(pad),), axis=0).T.astype(jnp.bfloat16)
-    columns_out[:, 128:] = jnp.concatenate(split3(jnp.exp(cum)) + (pad,), axis=0).T.astype(jnp.bfloat16)
-    row_out[...] = jnp.concatenate([live, ends_row, through, before, jnp.zeros((4, span), jnp.float32)], axis=0)
+    for copy in copies[5:]:
+        copy.wait()
     keys = b_input[...]
     me = member_index()
-    for j in range(GROUP):
+    for j in (1, 2, 3, 0):
         part = lax.bitwise_xor(me, j)
         first_head = part * (heads // GROUP)
         feat = features[:, pl.ds(pl.multiple_of(part * wide, wide), wide)]
@@ -91,23 +97,30 @@
         pieces[j][state:, :] = jnp.where(
             row == 0, over_channels(total, first_head, wide), jnp.where(row == 1, still_open, first_sum)
         )
-
-
-def intra_kernel(features, b_input, c_input, cum_ref, step_ref, columns, rows, skip, out, suffix):
+    cum_out[...] = cum
+    step_out[...] = step
+    row_out[...] = jnp.concatenate([live, ends_row, through, before, jnp.zeros((4, span), jnp.float32)], axis=0)
+    columns_out[:, :128] = jnp.concatenate(split3(cum) + (jnp.ones_like(pad),), axis=0).T.astype(jnp.bfloat16)
+    columns_out[:, 128:] = jnp.concatenate(split3(jnp.exp(cum)) + (pad,), axis=0).T.astype(jnp.bfloat16)
+    wide_out[0:1, :] = norm_gain[...] * value_weight[...]
+    wide_out[1:2, :] = over_channels(column(skip_gain[...]), 0, heads * HEAD_DIM)
+
+
+def intra_kernel(start, stop, features, b_input, c_input, cum_ref, step_ref, columns, rows, wide_row, *outs):
+    out = outs[0]
     heads, span = cum_ref.shape
     at_once = 128 // HEAD_DIM
     t, s = iota((span, span), 0), iota((span, span), 1)
     scores = jnp.where(t >= s, dot(c_input[...], b_input[...], ((1,), (1,))), 0.0)
     by_token = columns[:, :128]
-    skip_row = over_channels(column(skip[...]), 0, heads * HEAD_DIM)
-    out[...] = features[...].astype(jnp.float32) * skip_row
     row = iota((128, span), 0)
 
     def some_heads(index, carry):
         first = index * at_once
         lanes = pl.ds(pl.multiple_of(index * 128, 128), 128)
+        here = pl.ds(pl.multiple_of((index - start) * 128, 128), 128)
         feat = features[:, lanes]
-        total = out[:, lanes]
+        total = feat.astype(jnp.float32) * wide_row[1:2, lanes]
         owner = iota((span, 128), 1) // HEAD_DIM
         for j in range(at_once):
             head = first + j
@@ -125,16 +138,17 @@
             gap = jnp.minimum(dot(by_token, other), 0.0)
             weights = (scores * jnp.exp(gap) * step_ref[pl.ds(head, 1), :]).astype(jnp.bfloat16)
             total = total + dot(weights, jnp.where(owner == j, feat, jnp.zeros_like(feat)))
-        out[:, lanes] = total
+        out[:, here] = total
         return carry
 
-    lax.fori_loop(0, heads // at_once, some_heads, 0)
-
-    live, through, before = rows[0:1, :], rows[2:3, :], rows[3:4, :]
-    reach = jnp.where((t >= s) & (column(before) == before), column(live), 0.0)
-    sums = jnp.sum(reach, axis=0, keepdims=True)
-    open_end = jnp.where(before == through[:, span - 1 :], 1.0, 0.0)
-    suffix[...] = jnp.concatenate([sums, open_end, jnp.zeros((6, span), jnp.float32)], axis=0)
+    lax.fori_loop(start, stop, some_heads, 0)
+
+    if len(outs) > 1:
+        live, through, before = rows[0:1, :], rows[2:3, :], rows[3:4, :]
+        reach = jnp.where((t >= s) & (column(before) == before), column(live), 0.0)
+        sums = jnp.sum(reach, axis=0, keepdims=True)
+        open_end = jnp.where(before == through[:, span - 1 :], 1.0, 0.0)
+        outs[1][...] = jnp.concatenate([sums, open_end, jnp.zeros((6, span), jnp.float32)], axis=0)
 
 
 def in_order(pieces, me_static):
@@ -142,7 +156,7 @@
 
 
 def total_kernel(*refs):
-    pieces, out = refs[:GROUP], refs[GROUP]
+    pieces, out = refs[:GROUP], refs[-1]
     state = pieces[0].shape[0] - EXTRA
     me = member_index()
     for v in range(GROUP):
@@ -223,10 +237,10 @@
 
 
 def readout_kernel(*refs):
-    entering, (c_input, columns, inside, weight, gain, out) = refs[:GROUP], refs[GROUP:]
+    entering, (c_input, columns, first_half, second_half, wide_row, out) = refs[:GROUP], refs[GROUP:]
     state, wide = entering[0].shape
     span = c_input.shape[0]
-    heads = inside.shape[1] // HEAD_DIM
+    heads = wide_row.shape[1] // HEAD_DIM
     me = member_index()
     queries = c_input[...]
     by_token = columns[:, 128:]
@@ -234,14 +248,15 @@
     values = jnp.zeros((span, 128), jnp.float32)
     for j in range(GROUP):
         part = lax.bitwise_xor(me, j)
-        lanes = pl.ds(pl.multiple_of(part * wide, wide), wide)
+        half = pl.ds(pl.multiple_of(lax.rem(part, GROUP // 2) * wide, wide), wide)
         value = entering[j][...]
         high = value.astype(jnp.bfloat16)
         low = (value - high.astype(jnp.float32)).astype(jnp.bfloat16)
         carried = dot(queries, high) + dot(queries, low)
         decay = dot(by_token, selector(heads, 128, part * (heads // GROUP), wide))
-        mixed = inside[:, lanes] + carried * decay
-        readout = weight[:, lanes] * gain[:, lanes]
+        inside = jnp.where(part < GROUP // 2, first_half[:, half], second_half[:, half])
+        mixed = inside + carried * decay
+        readout = wide_row[0:1, pl.ds(pl.multiple_of(part * wide, wide), wide)]
         squared, read = mixed * mixed, mixed * readout
         for k in range(0, wide, 128):
             squares = squares + squared[:, k : k + 128]
@@ -250,18 +265,34 @@
     out[1:2, :] = jnp.sum(values.T, axis=0, keepdims=True)
 
 
-def call(kernel, shapes, name, *args):
-    single = not isinstance(shapes, (list, tuple))
-    structs = [jax.ShapeDtypeStruct(s, d) for s, d in ([shapes] if single else shapes)]
-    result = pl.pallas_call(
+def last_kernel(channels, mine, other, suffix, carry, values_out, advantages_out, values, advantages, sems):
+    sums = mine[...] + other[...]
+    value = sums[1:2] / jnp.sqrt(sums[0:1] / channels + NORM_EPSILON)
+    values[...] = value
+    advantages[...] = suffix[0:1, :] + suffix[1:2, :] * carry[0:1, 0:1] - value
+    copies = [
+        pltpu.make_async_copy(values, values_out, sems.at[0]),
+        pltpu.make_async_copy(advantages, advantages_out, sems.at[1]),
+    ]
+    for copy in copies:
+        copy.start()
+    for copy in copies:
+        copy.wait()
+
+
+def call(kernel, shapes, name, *args, hbm_in=False, hbm_out=False, scratch=()):
+    near, far = pl.BlockSpec(memory_space=pltpu.VMEM), pl.BlockSpec(memory_space=pltpu.HBM)
+    if hbm_in:
+        args = [pltpu.with_memory_space_constraint(arg, pltpu.HBM) for arg in args]
+    return pl.pallas_call(
         kernel,
-        out_shape=structs,
-        in_specs=[pl.BlockSpec(memory_space=pltpu.VMEM)] * len(args),
-        out_specs=[pl.BlockSpec(memory_space=pltpu.VMEM)] * len(structs),
+        out_shape=[jax.ShapeDtypeStruct(*shape) for shape in shapes],
+        in_specs=[far if hbm_in else near] * len(args),
+        out_specs=[far if hbm_out else near] * len(shapes),
+        scratch_shapes=scratch,
         compiler_params=pltpu.CompilerParams(vmem_limit_bytes=VMEM_BYTES),
         name=name,
     )(*args)
-    return result
 
 
 def swap(value, axis, mask):
@@ -292,35 +323,55 @@
     f32, bf16 = jnp.float32, jnp.bfloat16
     piece = ((state + EXTRA, wide), f32)
 
+    i32 = jnp.int32
     made = call(
         state_kernel,
         [piece] * GROUP
-        + [((heads, span), f32), ((heads, span), f32), ((span, 256), bf16), ((8, span), f32)],
+        + [
+            ((span, width), bf16),
+            ((span, state), bf16),
+            ((span, state), bf16),
+            ((heads, span), f32),
+            ((heads, span), f32),
+            ((span, 256), bf16),
+            ((8, span), f32),
+            ((2, width), f32),
+        ],
         "block_states",
         step_input,
         decay_log[None, :],
-        features,
-        b_input,
         rewards[None, :],
         reward_keep_mask[None, :],
         episode_end[None, :],
-    )
-    pieces, (cum, step, columns, rows) = made[:GROUP], made[GROUP:]
-    got = [pieces[0]] + [swap(pieces[j], "ctx", j) for j in range(1, GROUP)]
-    inside, suffix = call(
-        intra_kernel,
-        [((span, width), f32), ((8, span), f32)],
-        "inside_block",
         features,
         b_input,
         c_input,
-        cum,
-        step,
-        columns,
-        rows,
         skip_gain[None, :],
-    )
-    (total,) = call(total_kernel, [piece], "group_total", *got)
+        norm_gain[None, :],
+        value_weight[None, :],
+        hbm_in=True,
+        scratch=[
+            pltpu.VMEM((heads, span), f32),
+            pltpu.VMEM((1, heads), f32),
+            pltpu.VMEM((1, heads), f32),
+            pltpu.VMEM((1, width), f32),
+            pltpu.VMEM((1, width), f32),
+            pltpu.VMEM((1, span), f32),
+            pltpu.VMEM((1, span), i32),
+            pltpu.VMEM((1, span), i32),
+            pltpu.SemaphoreType.DMA((11,)),
+        ],
+    )
+    pieces, near = made[:GROUP], made[GROUP:]
+    queries, columns, wide_row = near[2], near[5], near[7]
+    got = [pieces[0]] + [swap(pieces[j], "ctx", j) for j in range(1, GROUP)]
+    head_groups = heads * HEAD_DIM // 128
+    half = head_groups // 2
+    half_shape = ((span, width // 2), f32)
+    first_half, suffix = call(
+        functools.partial(intra_kernel, 0, half), [half_shape, ((8, span), f32)], "inside_first", *near
+    )
+    (total,) = call(total_kernel, [piece], "group_total", *got, suffix)
     past = None
     bit = 1
     while bit * 2 < groups:
@@ -333,6 +384,9 @@
         )
         bit *= 2
     other = swap(total, "ctx", GROUP * bit)
+    (second_half,) = call(
+        functools.partial(intra_kernel, half, head_groups), [half_shape], "inside_second", *near
+    )
     made = call(
         functools.partial(entering_kernel, bit, past is not None),
         [((state, wide), f32)] * GROUP + [((8, wide), f32)],
@@ -340,25 +394,25 @@
         *got,
         other,
         *([] if past is None else [past]),
+        second_half,
     )
     entering, carry = made[:GROUP], made[GROUP]
     arrived = [entering[0]] + [swap(entering[j], "ctx", j) for j in range(1, GROUP)]
     (sums,) = call(
-        readout_kernel,
-        [((2, span), f32)],
-        "readout",
-        *arrived,
-        c_input,
-        columns,
-        inside,
-        value_weight[None, :],
-        norm_gain[None, :],
-    )
-    sums = sums + swap(sums, "head", 1)
-    mean_square = sums[0] / (width * lax.axis_size("head"))
-    values = sums[1] / jnp.sqrt(mean_square + NORM_EPSILON)
-    returns = suffix[0] + suffix[1] * carry[0, 0]
-    return (values, returns - values)
+        readout_kernel, [((2, span), f32)], "readout", *arrived, queries, columns, first_half, second_half, wide_row
+    )
+    values, advantages = call(
+        functools.partial(last_kernel, width * lax.axis_size("head")),
+        [((1, span), f32)] * 2,
+        "values_and_advantages",
+        sums,
+        swap(sums, "head", 1),
+        suffix,
+        carry,
+        hbm_out=True,
+        scratch=[pltpu.VMEM((1, span), f32), pltpu.VMEM((1, span), f32), pltpu.SemaphoreType.DMA((2,))],
+    )
+    return (values[0], advantages[0])
 
 
 def solution(mesh):

time: 38.7 us -> 34.2 us (0.88)
  local copies, waits for them, and re-layouts: 5.72 us -> 0 us
  Pallas kernels: 6.8 us -> 8.58 us
  other arithmetic: 1.23 us -> 0 us
  waiting for transfers between devices: 12.8 us -> 13.8 us
    unnamed x28 -> x0, local copies, waits for them, and re-layouts: 5.21 us -> none
    pallas_call x5 -> x7, Pallas kernels: 6.8 us -> 8.58 us  [call(): pl.pallas_call(kernel, out_shape=[jax.ShapeDtypeStruct(*shape) for shape...]
    ppermute x8, waiting for transfers between devices: 12.8 us -> 13.8 us  [swap(): return lax.ppermute(value, axis, [(k, k ^ mask) for k in range(count)])]
    add x2 -> x0, other arithmetic: 0.66 us -> none  [the longest x1 0.65 us: local(): returns = suffix[0] + suffix[1] * carry[0, 0]]
    sub x1 -> x0, other arithmetic: 0.56 us -> none  [local(): return (values, returns - values)]
    slice x1 -> x0, local copies, waits for them, and re-layouts: 0.51 us -> none  [local(): returns = suffix[0] + suffix[1] * carry[0, 0]]
  transfers between devices with their start and end apart: 8 -> 8, of which waited for: 5 -> 7; matrix products, arithmetic and copies ran while one was open for 3% -> 0% of each run, Pallas kernels for 12% -> 14%
where the time goes in v2:
time: 34.2 us; the launch traced here: 34.1 us
  waiting for transfers between devices  13.8 us (40%)
  starting transfers between devices  11 us (32%)
  Pallas kernels  8.58 us (25%)
  between operations  0.7 us (2%)
    ppermute x8, waiting for transfers between devices, swap(): return lax.ppermute(value, axis, [(k, k ^ mask) for k in range(count)])  13.8 us
    ppermute x8, starting transfers between devices, swap(): return lax.ppermute(value, axis, [(k, k ^ mask) for k in range(count)])  11 us
    pallas_call x7, Pallas kernels, call(): pl.pallas_call(kernel, out_shape=[jax.ShapeDtypeStruct(*shape) for shape...  8.58 us
  transfers between devices with their start and end apart: 8, of which 7 were waited for; matrix products, arithmetic and copies ran while one was open for 0% of the time, Pallas kernels for 14%

profile of v2, /device:TPU:0, one launch (start us, length us, event | category | flops | bytes accessed | tf_op | source)
XLA Modules:
  0.0 34.1 jit_solution(7838459973482076357)
XLA Ops:
  0.6 2.2 %block_states.1 = (f32[136,256]{1,0:T(8,128)S(1)}, f32[136,256]{1,0:T(8,128)S(1)}, f32[136,256]{1,0:T(8,128)S(1)}, f32[136,256]{1,0:T(8,128)S(1)}, bf16[256,1024...) custom-call(f32[32,256]{1,0:T(8,128)} %refs_0_.1, ...), custom_call_target="tpu_custom_call" | custom-call | tf_op jit(solution)/shard_map/block_states/pallas_call | solution.py:287
  2.8 3.0 %collective-permute-start = (f32[136,256]{1,0:T(8,128)S(1)}, f32[136,256]{1,0:T(8,128)S(1)}, u32[]{:S(2)}, u32[]{:S(2)}) collective-permute-start(f32[136,256]{1,0:T(8,128)S(1)} %get-tuple-element.24), channel_id=1, source_target_pairs={{0,2},{2,0},{4,6},{6,4},{8,10},{10,8},{12,14},{14,12},{1,3},{3,1},... | collective-permute-start | bytes 417800 | tf_op jit(solution)/shard_map/ppermute | solution.py:300
  5.8 1.6 %collective-permute-start.1 = (f32[136,256]{1,0:T(8,128)S(1)}, f32[136,256]{1,0:T(8,128)S(1)}, u32[]{:S(2)}, u32[]{:S(2)}) collective-permute-start(f32[136,256]{1,0:T(8,128)S(1)} %get-tuple-element.25), channel_id=1, source_target_pairs={{0,4},{2,6},{4,0},{6,2},{8,12},{10,14},{12,8},{14,10},{1,5},{3,7},... | collective-permute-start | bytes 417800 | tf_op jit(solution)/shard_map/ppermute | solution.py:300
  7.4 0.0 collective-permute-start.2
  7.4 2.5 %inside_first.1 = (f32[256,512]{1,0:T(8,128)S(1)}, f32[8,256]{1,0:T(8,128)S(1)}) custom-call(bf16[256,1024]{1,0:T(8,128)(2,1)S(1)} %get-tuple-element.27.features, bf16[256,128]{1,0:T(8,128)(2,1)S(1)} %get-tuple-element.28.b_input, bf16[256,128]{1,0:T(8,128)(2,1)S(1)} %get-tuple-element.29.c_input.refs_4_, f32[32,256]{1,0:T(8,128)S(1)} %get-tuple-element.30.cum_ref, ...), custom_call_target="tpu_custom_call" | custom-call | tf_op jit(solution)/shard_map/inside_first/pallas_call | solution.py:287
  9.9 0.0 collective-permute-done.refs_1_
  9.9 2.5 %collective-permute-done.1.refs_2_ = f32[136,256]{1,0:T(8,128)S(1)} collective-permute-done((f32[136,256]{1,0:T(8,128)S(1)}, f32[136,256]{1,0:T(8,128)S(1)}, u32[]{:S(2)}, u32[]{:S(2)}) %collective-permute-start.1) | collective-permute-done | bytes 139296 | tf_op jit(solution)/shard_map/ppermute | solution.py:300
  12.4 1.3 %collective-permute-done.2.refs_3_ = f32[136,256]{1,0:T(8,128)S(1)} collective-permute-done((f32[136,256]{1,0:T(8,128)S(1)}, f32[136,256]{1,0:T(8,128)S(1)}, u32[]{:S(2)}, u32[]{:S(2)}) %collective-permute-start.2) | collective-permute-done | bytes 139296 | tf_op jit(solution)/shard_map/ppermute | solution.py:300
  13.7 0.1 group_total.1
  13.8 2.8 %collective-permute-start.3 = (f32[136,256]{1,0:T(8,128)S(1)}, f32[136,256]{1,0:T(8,128)S(1)}, u32[]{:S(2)}, u32[]{:S(2)}) collective-permute-start(f32[136,256]{1,0:T(8,128)S(1)} %group_total.1), channel_id=1, source_target_pairs={{0,8},{2,10},{4,12},{6,14},{8,0},{10,2},{12,4},{14,6},{1,9},{3,11}... | collective-permute-start | bytes 417800 | tf_op jit(solution)/shard_map/ppermute | solution.py:300
  16.6 2.4 %inside_second.1.refs_5_.refs_7_ = f32[256,512]{1,0:T(8,128)S(1)} custom-call(bf16[256,1024]{1,0:T(8,128)(2,1)S(1)} %get-tuple-element.27.features, bf16[256,128]{1,0:T(8,128)(2,1)S(1)} %get-tuple-element.28.b_input, bf16[256,128]{1,0:T(8,128)(2,1)S(1)} %get-tuple-element.29.c_input.refs_4_, f32[32,256]{1,0:T(8,128)S(1)} %get-tuple-element.30.cum_ref, ...), custom_call_target="tpu_custom_call" | custom-call | tf_op jit(solution)/shard_map/inside_second/pallas_call | solution.py:287
  19.0 3.5 %collective-permute-done.3.refs_4_ = f32[136,256]{1,0:T(8,128)S(1)} collective-permute-done((f32[136,256]{1,0:T(8,128)S(1)}, f32[136,256]{1,0:T(8,128)S(1)}, u32[]{:S(2)}, u32[]{:S(2)}) %collective-permute-start.3) | collective-permute-done | bytes 139296 | tf_op jit(solution)/shard_map/ppermute | solution.py:300
  22.6 0.1 entering_states.1
  22.6 1.1 %collective-permute-start.4 = (f32[128,256]{1,0:T(8,128)S(1)}, f32[128,256]{1,0:T(8,128)S(1)}, u32[]{:S(2)}, u32[]{:S(2)}) collective-permute-start(f32[128,256]{1,0:T(8,128)S(1)} %get-tuple-element.37), channel_id=1, source_target_pairs={{0,2},{2,0},{4,6},{6,4},{8,10},{10,8},{12,14},{14,12},{1,3},{3,1},... | collective-permute-start | bytes 393224 | tf_op jit(solution)/shard_map/ppermute | solution.py:300
  23.8 0.7 %collective-permute-start.5 = (f32[128,256]{1,0:T(8,128)S(1)}, f32[128,256]{1,0:T(8,128)S(1)}, u32[]{:S(2)}, u32[]{:S(2)}) collective-permute-start(f32[128,256]{1,0:T(8,128)S(1)} %get-tuple-element.38), channel_id=1, source_target_pairs={{0,4},{2,6},{4,0},{6,2},{8,12},{10,14},{12,8},{14,10},{1,5},{3,7},... | collective-permute-start | bytes 393224 | tf_op jit(solution)/shard_map/ppermute | solution.py:300
  24.4 1.8 %collective-permute-start.6 = (f32[128,256]{1,0:T(8,128)S(1)}, f32[128,256]{1,0:T(8,128)S(1)}, u32[]{:S(2)}, u32[]{:S(2)}) collective-permute-start(f32[128,256]{1,0:T(8,128)S(1)} %get-tuple-element.39), channel_id=1, source_target_pairs={{0,6},{2,4},{4,2},{6,0},{8,14},{10,12},{12,10},{14,8},{1,7},{3,5},... | collective-permute-start | bytes 393224 | tf_op jit(solution)/shard_map/ppermute | solution.py:300
  26.2 2.4 %collective-permute-done.4.refs_1_ = f32[128,256]{1,0:T(8,128)S(1)} collective-permute-done((f32[128,256]{1,0:T(8,128)S(1)}, f32[128,256]{1,0:T(8,128)S(1)}, u32[]{:S(2)}, u32[]{:S(2)}) %collective-permute-start.4) | collective-permute-done | bytes 131104 | tf_op jit(solution)/shard_map/ppermute | solution.py:300
  28.6 0.4 %collective-permute-done.5.refs_2_ = f32[128,256]{1,0:T(8,128)S(1)} collective-permute-done((f32[128,256]{1,0:T(8,128)S(1)}, f32[128,256]{1,0:T(8,128)S(1)}, u32[]{:S(2)}, u32[]{:S(2)}) %collective-permute-start.5) | collective-permute-done | bytes 131104 | tf_op jit(solution)/shard_map/ppermute | solution.py:300
  29.0 2.5 %collective-permute-done.6.refs_3_ = f32[128,256]{1,0:T(8,128)S(1)} collective-permute-done((f32[128,256]{1,0:T(8,128)S(1)}, f32[128,256]{1,0:T(8,128)S(1)}, u32[]{:S(2)}, u32[]{:S(2)}) %collective-permute-start.6) | collective-permute-done | bytes 131104 | tf_op jit(solution)/shard_map/ppermute | solution.py:300
  31.5 0.7 %readout.1.mine = f32[2,256]{1,0:T(2,128)S(1)} custom-call(f32[128,256]{1,0:T(8,128)S(1)} %get-tuple-element.36.refs_0_, f32[128,256]{1,0:T(8,128)S(1)} %collective-permute-done.4.refs_1_, f32[128,256]{1,0:T(8,128)S(1)} %collective-permute-done.5.refs_2_, f32[128,256]{1,0:T(8,128)S(1)} %collective-permute-done.6.refs_3_, ...), custom_call_target="tpu_custom_call" | custom-call | tf_op jit(solution)/shard_map/readout/pallas_call | solution.py:287
  32.2 0.1 collective-permute-start.7
  32.3 1.1 %collective-permute-done.7.other = f32[2,256]{1,0:T(2,128)S(1)} collective-permute-done((f32[2,256]{1,0:T(2,128)S(1)}, f32[2,256]{1,0:T(2,128)S(1)}, u32[]{:S(2)}, u32[]{:S(2)}) %collective-permute-start.7) | collective-permute-done | bytes 2080 | tf_op jit(solution)/shard_map/ppermute | solution.py:300
  33.4 0.7 %values_and_advantages.1 = (f32[1,256]{1,0:T(1,128)}, f32[1,256]{1,0:T(1,128)}) custom-call(f32[2,256]{1,0:T(2,128)S(1)} %readout.1.mine, f32[2,256]{1,0:T(2,128)S(1)} %collective-permute-done.7.other, f32[8,256]{1,0:T(8,128)S(1)} %get-tuple-element.35.refs_4_.suffix, f32[8,256]{1,0:T(8,128)S(1)} %get-tuple-element.41.carry), custom_call_target="tpu_custom_call" | custom-call | tf_op jit(solution)/shard_map/values_and_advantages/pallas_call | solution.py:287
Async XLA Ops:
  2.8 7.1 %collective-permute-start = (f32[136,256]{1,0:T(8,128)S(1)}, f32[136,256]{1,0:T(8,128)S(1)}, u32[]{:S(2)}, u32[]{:S(2)}) collective-permute-start(f32[136,256]{1,0:T(8,128)S(1)} %get-tuple-element.24), channel_id=1, source_target_pairs={{0,2},{2,0},{4,6},{6,4},{8,10},{10,8},{12,14},{14,12},{1,3},{3,1},... | collective-permute-start | bytes 417800 | tf_op jit(solution)/shard_map/ppermute | solution.py:300
  5.8 6.6 %collective-permute-start.1 = (f32[136,256]{1,0:T(8,128)S(1)}, f32[136,256]{1,0:T(8,128)S(1)}, u32[]{:S(2)}, u32[]{:S(2)}) collective-permute-start(f32[136,256]{1,0:T(8,128)S(1)} %get-tuple-element.25), channel_id=1, source_target_pairs={{0,4},{2,6},{4,0},{6,2},{8,12},{10,14},{12,8},{14,10},{1,5},{3,7},... | collective-permute-start | bytes 417800 | tf_op jit(solution)/shard_map/ppermute | solution.py:300
  7.4 6.3 %collective-permute-start.2 = (f32[136,256]{1,0:T(8,128)S(1)}, f32[136,256]{1,0:T(8,128)S(1)}, u32[]{:S(2)}, u32[]{:S(2)}) collective-permute-start(f32[136,256]{1,0:T(8,128)S(1)} %get-tuple-element.26), channel_id=1, source_target_pairs={{0,6},{2,4},{4,2},{6,0},{8,14},{10,12},{12,10},{14,8},{1,7},{3,5},... | collective-permute-start | bytes 417800 | tf_op jit(solution)/shard_map/ppermute | solution.py:300
  13.8 8.8 %collective-permute-start.3 = (f32[136,256]{1,0:T(8,128)S(1)}, f32[136,256]{1,0:T(8,128)S(1)}, u32[]{:S(2)}, u32[]{:S(2)}) collective-permute-start(f32[136,256]{1,0:T(8,128)S(1)} %group_total.1), channel_id=1, source_target_pairs={{0,8},{2,10},{4,12},{6,14},{8,0},{10,2},{12,4},{14,6},{1,9},{3,11}... | collective-permute-start | bytes 417800 | tf_op jit(solution)/shard_map/ppermute | solution.py:300
  22.6 6.0 %collective-permute-start.4 = (f32[128,256]{1,0:T(8,128)S(1)}, f32[128,256]{1,0:T(8,128)S(1)}, u32[]{:S(2)}, u32[]{:S(2)}) collective-permute-start(f32[128,256]{1,0:T(8,128)S(1)} %get-tuple-element.37), channel_id=1, source_target_pairs={{0,2},{2,0},{4,6},{6,4},{8,10},{10,8},{12,14},{14,12},{1,3},{3,1},... | collective-permute-start | bytes 393224 | tf_op jit(solution)/shard_map/ppermute | solution.py:300
  23.8 5.2 %collective-permute-start.5 = (f32[128,256]{1,0:T(8,128)S(1)}, f32[128,256]{1,0:T(8,128)S(1)}, u32[]{:S(2)}, u32[]{:S(2)}) collective-permute-start(f32[128,256]{1,0:T(8,128)S(1)} %get-tuple-element.38), channel_id=1, source_target_pairs={{0,4},{2,6},{4,0},{6,2},{8,12},{10,14},{12,8},{14,10},{1,5},{3,7},... | collective-permute-start | bytes 393224 | tf_op jit(solution)/shard_map/ppermute | solution.py:300
  24.4 7.0 %collective-permute-start.6 = (f32[128,256]{1,0:T(8,128)S(1)}, f32[128,256]{1,0:T(8,128)S(1)}, u32[]{:S(2)}, u32[]{:S(2)}) collective-permute-start(f32[128,256]{1,0:T(8,128)S(1)} %get-tuple-element.39), channel_id=1, source_target_pairs={{0,6},{2,4},{4,2},{6,0},{8,14},{10,12},{12,10},{14,8},{1,7},{3,5},... | collective-permute-start | bytes 393224 | tf_op jit(solution)/shard_map/ppermute | solution.py:300
  32.2 1.2 %collective-permute-start.7 = (f32[2,256]{1,0:T(2,128)S(1)}, f32[2,256]{1,0:T(2,128)S(1)}, u32[]{:S(2)}, u32[]{:S(2)}) collective-permute-start(f32[2,256]{1,0:T(2,128)S(1)} %readout.1.mine), channel_id=1, source_target_pairs={{0,1},{1,0},{2,3},{3,2},{4,5},{5,4},{6,7},{7,6},{8,9},{9,8},{10,11... | collective-permute-start | bytes 6152 | tf_op jit(solution)/shard_map/ppermute | solution.py:300

commit v3 on v2

v3 whole, which is shorter than its diff:
```python
import functools

import jax
import jax.numpy as jnp
from jax import lax
from jax.experimental import pallas as pl
from jax.experimental.pallas import tpu as pltpu
from jax.sharding import PartitionSpec as P

HEAD_DIM = 32
SPAN = 256
GROUP = 4
LANES = 128
LATE = 0
SHARES = ((0, 2, 2, 8, 8), (0, 0, 4, 8, 8))
EXTRA = 8
NORM_EPSILON = 1e-05
VMEM_BYTES = 24 * 1024 * 1024


def split3(value):
    high = value.astype(jnp.bfloat16).astype(jnp.float32)
    rest = value - high
    middle = rest.astype(jnp.bfloat16).astype(jnp.float32)
    return high, middle, (rest - middle).astype(jnp.bfloat16).astype(jnp.float32)


def dot(a, b, contract=((1,), (0,))):
    return lax.dot_general(a, b, (contract, ((), ())), preferred_element_type=jnp.float32)


def iota(shape, dim):
    return lax.broadcasted_iota(jnp.int32, shape, dim)


def column(row):
    n = row.shape[1]
    return jnp.sum(jnp.where(iota((n, n), 0) == iota((n, n), 1), row, 0.0), axis=1, keepdims=True)


def over_channels(per_head, first_head, channels):
    heads = per_head.shape[0]
    match = iota((heads, channels), 0) == first_head + iota((heads, channels), 1) // HEAD_DIM
    return jnp.sum(jnp.where(match, per_head, 0.0), axis=0, keepdims=True)


def selector(heads, rows, first_head, channels):
    row = iota((rows, channels), 0)
    match = (lax.rem(row, heads) == first_head + iota((rows, channels), 1) // HEAD_DIM) & (row < 3 * heads)
    return jnp.where(match, 1.0, 0.0).astype(jnp.bfloat16)


def is_late():
    return lax.axis_index("head") == LATE


def member_index():
    return lax.rem(lax.axis_index("ctx"), GROUP)


def prepare(cum_ref, skip, norm, weight, columns_out, wide_out):
    heads, span = cum_ref.shape
    cum = cum_ref[...]
    pad = jnp.zeros((128 - 3 * heads, span), jnp.float32)
    columns_out[:, :128] = jnp.concatenate(split3(cum) + (jnp.ones_like(pad),), axis=0).T.astype(jnp.bfloat16)
    columns_out[:, 128:] = jnp.concatenate(split3(jnp.exp(cum)) + (pad,), axis=0).T.astype(jnp.bfloat16)
    wide_out[0:1, :] = norm[...] * weight[...]
    wide_out[1:2, :] = over_channels(column(skip[...]), 0, heads * HEAD_DIM)


def state_kernel(*refs):
    sources, refs = refs[:11], refs[11:]
    pieces, refs = refs[:GROUP], refs[GROUP:]
    features, b_input, c_input, cum_out, step_out, rows, skip, norm, weight, columns, wide_row, inside = refs[:12]
    step_in, decay_log, rewards, keep, ends, sems = refs[12:]
    targets = (step_in, decay_log, rewards, keep, ends, features, b_input, c_input, skip, norm, weight)
    copies = [pltpu.make_async_copy(src, dst, sems.at[i]) for i, (src, dst) in enumerate(zip(sources, targets))]
    for copy in copies:
        copy.start()
    heads, span = step_in.shape
    state = b_input.shape[1]
    wide = features.shape[1] // GROUP
    for copy in copies[:5]:
        copy.wait()
    raw = step_in[...]
    step = jnp.maximum(raw, 0.0) + jnp.log1p(jnp.exp(-jnp.abs(raw)))
    log_decay = -jnp.exp(column(decay_log[...])) * step
    ends_row = ends[...].astype(jnp.float32)
    live = keep[...].astype(jnp.float32) * rewards[...]
    upper = jnp.where(iota((span, span), 0) <= iota((span, span), 1), 1.0, 0.0).astype(jnp.bfloat16)
    stacked = jnp.concatenate(split3(log_decay) + (jnp.broadcast_to(ends_row, (16, span)),), axis=0)
    summed = dot(stacked.astype(jnp.bfloat16), upper)
    cum = summed[:heads] + summed[heads : 2 * heads] + summed[2 * heads : 3 * heads]
    through = summed[3 * heads : 3 * heads + 1]
    before = through - ends_row
    total = cum[:, span - 1 :]
    first_sum = jnp.sum(jnp.where(before == 0.0, live, 0.0), axis=1, keepdims=True)
    still_open = jnp.where(through[:, span - 1 :] == 0.0, 1.0, 0.0)
    coefficient = jnp.exp(total - cum) * step
    pad = jnp.zeros((128 - 3 * heads, span), jnp.float32)
    by_token = jnp.concatenate(split3(coefficient) + (pad,), axis=0).T.astype(jnp.bfloat16)
    cum_out[...] = cum
    step_out[...] = step
    rows[...] = jnp.concatenate([live, through, before, jnp.zeros((5, span), jnp.float32)], axis=0)
    for copy in copies[5:]:
        copy.wait()

    @pl.when(is_late())
    def _():
        prepare(cum_out, skip, norm, weight, columns, wide_row)
        intra_groups(0, features, b_input, c_input, cum_out, step_out, columns, wide_row, inside)

    keys = b_input[...].T
    me = member_index()
    row = iota((EXTRA, LANES), 0)
    for j in (1, 2, 3, 0):
        part = lax.bitwise_xor(me, j)
        first_head = part * (heads // GROUP)
        feat = features[:, pl.ds(pl.multiple_of(part * wide, wide), wide)]
        spread = dot(by_token, selector(heads, 128, first_head, wide))
        scaled = (spread * feat.astype(jnp.float32)).astype(jnp.bfloat16)
        states = dot(keys, scaled)
        decay = over_channels(total, first_head, wide)
        extra = jnp.where(row == wide // LANES, still_open, first_sum)
        for k in range(wide // LANES):
            pieces[j][k * state : (k + 1) * state, :] = states[:, k * LANES : (k + 1) * LANES]
            extra = jnp.where(row == k, decay[:, k * LANES : (k + 1) * LANES], extra)
        pieces[j][wide // LANES * state :, :] = extra


def intra_groups(stage, features, b_input, c_input, cum_ref, step_ref, columns, wide_row, out):
    start, stop = (jnp.where(is_late(), SHARES[0][k], SHARES[1][k]) for k in (stage, stage + 1))
    heads, span = cum_ref.shape
    at_once = 128 // HEAD_DIM
    t, s = iota((span, span), 0), iota((span, span), 1)
    scores = jnp.where(t >= s, dot(c_input[...], b_input[...], ((1,), (1,))), 0.0)
    by_token = columns[:, :128]
    row = iota((128, span), 0)

    def some_heads(index, carry):
        first = index * at_once
        lanes = pl.ds(pl.multiple_of(index * 128, 128), 128)
        feat = features[:, lanes]
        total = feat.astype(jnp.float32) * wide_row[1:2, lanes]
        owner = iota((span, 128), 1) // HEAD_DIM
        for j in range(at_once):
            head = first + j
            cum = cum_ref[pl.ds(head, 1), :]
            high, middle, low = split3(cum)
            other = jnp.where(
                row < 3 * heads,
                jnp.where(lax.rem(row, heads) == head, 1.0, 0.0),
                jnp.where(
                    row == 3 * heads,
                    -high,
                    jnp.where(row == 3 * heads + 1, -middle, jnp.where(row == 3 * heads + 2, -low, 0.0)),
                ),
            ).astype(jnp.bfloat16)
            gap = jnp.minimum(dot(by_token, other), 0.0)
            weights = (scores * jnp.exp(gap) * step_ref[pl.ds(head, 1), :]).astype(jnp.bfloat16)
            total = total + dot(weights, jnp.where(owner == j, feat, jnp.zeros_like(feat)))
        out[:, lanes] = total
        return carry

    lax.fori_loop(start, stop, some_heads, 0)


def first_kernel(
    features, b_input, c_input, cum_ref, step_ref, rows, skip, norm, weight, _0, _1, _2, columns, wide_row, out, suffix
):
    @pl.when(jnp.logical_not(is_late()))
    def _():
        prepare(cum_ref, skip, norm, weight, columns, wide_row)

    intra_groups(1, features, b_input, c_input, cum_ref, step_ref, columns, wide_row, out)

    span = cum_ref.shape[1]
    t, s = iota((span, span), 0), iota((span, span), 1)
    live, through, before = rows[0:1, :], rows[1:2, :], rows[2:3, :]
    reach = jnp.where((t >= s) & (column(before) == before), column(live), 0.0)
    sums = jnp.sum(reach, axis=0, keepdims=True)
    open_end = jnp.where(before == through[:, span - 1 :], 1.0, 0.0)
    suffix[...] = jnp.concatenate([sums, open_end, jnp.zeros((6, span), jnp.float32)], axis=0)


def second_kernel(features, b_input, c_input, cum_ref, step_ref, columns, wide_row, _, out):
    intra_groups(2, features, b_input, c_input, cum_ref, step_ref, columns, wide_row, out)


def in_order(pieces, me_static):
    return [pieces[me_static ^ m] for m in range(GROUP)]


def parts_of(piece):
    halves = 2
    size = (piece.shape[0] - EXTRA) // halves
    extra = piece[halves * size :, :]
    return (
        [piece[k * size : (k + 1) * size, :] for k in range(halves)],
        [extra[k : k + 1] for k in range(halves)],
        extra[halves : halves + 1],
        extra[halves + 1 : halves + 2],
    )


def write_piece(out, states, decays, keeps, amount):
    size = states[0].shape[0]
    for k, state in enumerate(states):
        out[k * size : (k + 1) * size, :] = state
    row = iota((EXTRA, LANES), 0)
    extra = jnp.where(row == len(states), keeps, amount)
    for k, decay in enumerate(decays):
        extra = jnp.where(row == k, decay, extra)
    out[len(states) * size :, :] = extra


def carry_on(states, piece):
    return [jnp.exp(decay) * old + new for old, new, decay in zip(states, piece[0], piece[1])]


def add(first, second):
    return [one + other for one, other in zip(first, second)]


def total_kernel(*refs):
    pieces, out = refs[:GROUP], refs[-1]
    me = member_index()
    for v in range(GROUP):

        @pl.when(me == v)
        def _():
            members = [parts_of(piece) for piece in in_order(pieces, v)]
            states, decays, keeps, _ = members[0]
            for member in members[1:]:
                states = carry_on(states, member)
                decays = add(decays, member[1])
                keeps = keeps * member[2]
            amount = members[-1][3]
            for member in members[-2::-1]:
                amount = member[3] + member[2] * amount
            write_piece(out, states, decays, keeps, amount)


def round_kernel(bit, *refs):
    total, got, before, total_out, before_out = refs
    group = lax.axis_index("ctx") // GROUP
    mine, theirs, past = parts_of(total), parts_of(got), parts_of(before)
    decays, keeps = add(mine[1], theirs[1]), mine[2] * theirs[2]

    @pl.when(lax.rem(group // bit, 2) == 1)
    def _():
        write_piece(before_out, carry_on(theirs[0], past), add(past[1], theirs[1]), past[2], past[3])
        write_piece(total_out, carry_on(theirs[0], mine), decays, keeps, theirs[3] + theirs[2] * mine[3])

    @pl.when(lax.rem(group // bit, 2) == 0)
    def _():
        write_piece(before_out, past[0], past[1], past[2] * theirs[2], past[3] + past[2] * theirs[3])
        write_piece(total_out, carry_on(mine[0], theirs), decays, keeps, mine[3] + mine[2] * theirs[3])


def entering_kernel(bit, has_past, *refs):
    pieces, got = refs[:GROUP], refs[GROUP]
    past = refs[GROUP + 1] if has_past else None
    outs, carry_out, inside = refs[-GROUP - 2 : -2], refs[-2], refs[-1]
    near = refs[GROUP + 1 + has_past : GROUP + 8 + has_past]
    intra_groups(3, *near, inside)
    ctx = lax.axis_index("ctx")
    me = lax.rem(ctx, GROUP)
    is_later = lax.rem(ctx // GROUP // bit, 2) == 1
    theirs = parts_of(got)
    for v in range(GROUP):

        @pl.when(me == v)
        def _():
            members = [parts_of(piece) for piece in in_order(pieces, v)]
            arriving = [jnp.where(is_later, state, 0.0) for state in theirs[0]]
            amount = jnp.where(is_later, 0.0, theirs[3])
            if has_past:
                old = parts_of(past)
                arriving = carry_on(arriving, old)
                amount = old[3] + old[2] * amount
            size = arriving[0].shape[0]
            for m in range(GROUP):
                for k, state in enumerate(arriving):
                    outs[v ^ m][k * size : (k + 1) * size, :] = state
                if m < GROUP - 1:
                    arriving = carry_on(arriving, members[m])
            for m in range(GROUP - 1, v, -1):
                amount = members[m][3] + members[m][2] * amount
            carry_out[...] = jnp.broadcast_to(amount, carry_out.shape)


def readout_kernel(*refs):
    entering, (c_input, columns, inside, wide_row, out) = refs[:GROUP], refs[GROUP:]
    span, state = c_input.shape
    heads = wide_row.shape[1] // HEAD_DIM
    wide = wide_row.shape[1] // GROUP
    me = member_index()
    queries = c_input[...]
    by_token = columns[:, 128:]
    squares = jnp.zeros((span, 128), jnp.float32)
    values = jnp.zeros((span, 128), jnp.float32)
    for j in range(GROUP):
        part = lax.bitwise_xor(me, j)
        lanes = pl.ds(pl.multiple_of(part * wide, wide), wide)
        value = jnp.concatenate([entering[j][:state, :], entering[j][state:, :]], axis=1)
        high = value.astype(jnp.bfloat16)
        low = (value - high.astype(jnp.float32)).astype(jnp.bfloat16)
        carried = dot(queries, high) + dot(queries, low)
        decay = dot(by_token, selector(heads, 128, part * (heads // GROUP), wide))
        mixed = inside[:, lanes] + carried * decay
        readout = wide_row[0:1, lanes]
        squared, read = mixed * mixed, mixed * readout
        for k in range(0, wide, 128):
            squares = squares + squared[:, k : k + 128]
            values = values + read[:, k : k + 128]
    out[0:1, :] = jnp.sum(squares.T, axis=0, keepdims=True)
    out[1:2, :] = jnp.sum(values.T, axis=0, keepdims=True)


def last_kernel(channels, mine, other, suffix, carry, values_out, advantages_out, values, advantages, sems):
    sums = mine[...] + other[...]
    value = sums[1:2] / jnp.sqrt(sums[0:1] / channels + NORM_EPSILON)
    values[...] = value
    advantages[...] = suffix[0:1, :] + suffix[1:2, :] * carry[0:1, 0:1] - value
    copies = [
        pltpu.make_async_copy(values, values_out, sems.at[0]),
        pltpu.make_async_copy(advantages, advantages_out, sems.at[1]),
    ]
    for copy in copies:
        copy.start()
    for copy in copies:
        copy.wait()


def call(kernel, shapes, name, *args, hbm_in=False, hbm_out=False, scratch=(), aliases=None):
    near, far = pl.BlockSpec(memory_space=pltpu.VMEM), pl.BlockSpec(memory_space=pltpu.HBM)
    if hbm_in:
        args = [pltpu.with_memory_space_constraint(arg, pltpu.HBM) for arg in args]
    return pl.pallas_call(
        kernel,
        out_shape=[jax.ShapeDtypeStruct(*shape) for shape in shapes],
        in_specs=[far if hbm_in else near] * len(args),
        out_specs=[far if hbm_out else near] * len(shapes),
        scratch_shapes=scratch,
        input_output_aliases=aliases or {},
        compiler_params=pltpu.CompilerParams(vmem_limit_bytes=VMEM_BYTES),
        name=name,
    )(*args)


def swap(value, axis, mask):
    count = lax.axis_size(axis)
    return lax.ppermute(value, axis, [(k, k ^ mask) for k in range(count)])


def local(
    features,
    b_input,
    c_input,
    step_input,
    decay_log,
    skip_gain,
    norm_gain,
    value_weight,
    rewards,
    reward_keep_mask,
    episode_end,
):
    span, width = features.shape
    heads = step_input.shape[0]
    state = b_input.shape[1]
    halves = width // GROUP // LANES
    count = lax.axis_size("ctx")
    groups = count // GROUP
    assert span == SPAN and count == groups * GROUP and groups > 1 and groups & (groups - 1) == 0 and halves == 2
    f32, bf16, i32 = jnp.float32, jnp.bfloat16, jnp.int32
    piece = ((halves * state + EXTRA, LANES), f32)
    states = ((halves * state, LANES), f32)
    columns_shape, wide_shape, inside_shape = ((span, 256), bf16), ((2, width), f32), ((span, width), f32)

    made = call(
        state_kernel,
        [piece] * GROUP
        + [
            ((span, width), bf16),
            ((span, state), bf16),
            ((span, state), bf16),
            ((heads, span), f32),
            ((heads, span), f32),
            ((8, span), f32),
            ((1, heads), f32),
            ((1, width), f32),
            ((1, width), f32),
            columns_shape,
            wide_shape,
            inside_shape,
        ],
        "block_states",
        step_input,
        decay_log[None, :],
        rewards[None, :],
        reward_keep_mask[None, :],
        episode_end[None, :],
        features,
        b_input,
        c_input,
        skip_gain[None, :],
        norm_gain[None, :],
        value_weight[None, :],
        hbm_in=True,
        scratch=[
            pltpu.VMEM((heads, span), f32),
            pltpu.VMEM((1, heads), f32),
            pltpu.VMEM((1, span), f32),
            pltpu.VMEM((1, span), i32),
            pltpu.VMEM((1, span), i32),
            pltpu.SemaphoreType.DMA((11,)),
        ],
    )
    pieces, made = made[:GROUP], made[GROUP:]
    got = [pieces[0]] + [swap(pieces[j], "ctx", j) for j in range(1, GROUP)]
    columns, wide_row, inside, suffix = call(
        first_kernel,
        [columns_shape, wide_shape, inside_shape, ((8, span), f32)],
        "inside_first",
        *made,
        aliases={9: 0, 10: 1, 11: 2},
    )
    near = (*made[:5], columns, wide_row)
    queries = made[2]
    (total,) = call(total_kernel, [piece], "group_total", *got, suffix)
    past = None
    bit = 1
    while bit * 2 < groups:
        other = swap(total, "ctx", GROUP * bit)
        if past is None:
            row = jnp.arange(piece[0][0])[:, None]
            past = jnp.where(row == halves * (state + 1), 1.0, 0.0).astype(f32) * jnp.ones((1, LANES), f32)
        total, past = call(
            functools.partial(round_kernel, bit), [piece, piece], "scan_round", total, other, past
        )
        bit *= 2
    other = swap(total, "ctx", GROUP * bit)
    (inside,) = call(second_kernel, [inside_shape], "inside_second", *near, inside, aliases={len(near): 0})
    operands = (*got, other, *([] if past is None else [past]), *near, inside)
    made = call(
        functools.partial(entering_kernel, bit, past is not None),
        [states] * GROUP + [((8, LANES), f32), inside_shape],
        "entering_states",
        *operands,
        aliases={len(operands) - 1: GROUP + 1},
    )
    entering, carry, inside = made[:GROUP], made[GROUP], made[GROUP + 1]
    arrived = [entering[0]] + [swap(entering[j], "ctx", j) for j in range(1, GROUP)]
    (sums,) = call(readout_kernel, [((2, span), f32)], "readout", *arrived, queries, columns, inside, wide_row)
    values, advantages = call(
        functools.partial(last_kernel, width * lax.axis_size("head")),
        [((1, span), f32)] * 2,
        "values_and_advantages",
        sums,
        swap(sums, "head", 1),
        suffix,
        carry,
        hbm_out=True,
        scratch=[pltpu.VMEM((1, span), f32), pltpu.VMEM((1, span), f32), pltpu.SemaphoreType.DMA((2,))],
    )
    return (values[0], advantages[0])


def solution(mesh):
    placed = (
        P(("traj", "ctx"), "head"),
        P(("traj", "ctx"), None),
        P(("traj", "ctx"), None),
        P("head", ("traj", "ctx")),
        P("head"),
        P("head"),
        P("head"),
        P("head"),
        P(("traj", "ctx")),
        P(("traj", "ctx")),
        P(("traj", "ctx")),
    )
    return jax.shard_map(
        local,
        mesh=mesh,
        in_specs=placed,
        out_specs=(P(("traj", "ctx")), P(("traj", "ctx"))),
        check_vma=False,
    )
```

time: 34.2 us -> 33 us (0.965)
  waiting for transfers between devices: 13.8 us -> 12.2 us
    ppermute x8, waiting for transfers between devices: 13.8 us -> 12.2 us  [swap(): return lax.ppermute(value, axis, [(k, k ^ mask) for k in range(count)])]
  transfers between devices with their start and end apart: 8 -> 8, of which waited for: 7 -> 8; matrix products, arithmetic and copies ran while one was open for 0% -> 0% of each run, Pallas kernels for 14% -> 12%
where the time goes in v3:
time: 33 us; the launch traced here: 32.8 us
  waiting for transfers between devices  12.2 us (37%)
  starting transfers between devices  11 us (33%)
  Pallas kernels  8.91 us (27%)
  between operations  0.69 us (2%)
    ppermute x8, waiting for transfers between devices, swap(): return lax.ppermute(value, axis, [(k, k ^ mask) for k in range(count)])  12.2 us
    ppermute x8, starting transfers between devices, swap(): return lax.ppermute(value, axis, [(k, k ^ mask) for k in range(count)])  11 us
    pallas_call x7, Pallas kernels, call(): pl.pallas_call(kernel, out_shape=[jax.ShapeDtypeStruct(*shape) for shape...  8.91 us
  transfers between devices with their start and end apart: 8, of which 8 were waited for; matrix products, arithmetic and copies ran while one was open for 0% of the time, Pallas kernels for 12%

profile of v3, /device:TPU:0, one launch (start us, length us, event | category | flops | bytes accessed | tf_op | source)
XLA Modules:
  0.0 32.8 jit_solution(3552942546257456695)
XLA Ops:
  0.6 3.6 %block_states.1 = (f32[264,128]{1,0:T(8,128)S(1)}, f32[264,128]{1,0:T(8,128)S(1)}, f32[264,128]{1,0:T(8,128)S(1)}, f32[264,128]{1,0:T(8,128)S(1)}, bf16[256,1024...) custom-call(f32[32,256]{1,0:T(8,128)} %refs_0_.1, ...), custom_call_target="tpu_custom_call" | custom-call | tf_op jit(solution)/shard_map/block_states/pallas_call | solution.py:340
  4.2 3.0 %collective-permute-start = (f32[264,128]{1,0:T(8,128)S(1)}, f32[264,128]{1,0:T(8,128)S(1)}, u32[]{:S(2)}, u32[]{:S(2)}) collective-permute-start(f32[264,128]{1,0:T(8,128)S(1)} %get-tuple-element.31), channel_id=1, source_target_pairs={{0,2},{2,0},{4,6},{6,4},{8,10},{10,8},{12,14},{14,12},{1,3},{3,1},... | collective-permute-start | bytes 405512 | tf_op jit(solution)/shard_map/ppermute | solution.py:354
  7.2 1.6 %collective-permute-start.1 = (f32[264,128]{1,0:T(8,128)S(1)}, f32[264,128]{1,0:T(8,128)S(1)}, u32[]{:S(2)}, u32[]{:S(2)}) collective-permute-start(f32[264,128]{1,0:T(8,128)S(1)} %get-tuple-element.32), channel_id=1, source_target_pairs={{0,4},{2,6},{4,0},{6,2},{8,12},{10,14},{12,8},{14,10},{1,5},{3,7},... | collective-permute-start | bytes 405512 | tf_op jit(solution)/shard_map/ppermute | solution.py:354
  8.8 0.0 collective-permute-start.2
  8.8 0.4 %inside_first.1 = (bf16[256,256]{1,0:T(8,128)(2,1)S(1)}, f32[2,1024]{1,0:T(2,128)S(1)}, f32[256,1024]{1,0:T(8,128)S(1)}, f32[8,256]{1,0:T(8,128)S(1)}) custom-call(bf16[256,1024]{1,0:T(8,128)(2,1)S(1)} %get-tuple-element.34.features.refs_5_, ...), custom_call_target="tpu_custom_call", output_to_operand_aliasing={{0}: (9, {}), {1}: (10, {}), {2}: (11, {})} | custom-call | tf_op jit(solution)/shard_map/inside_first/pallas_call | solution.py:340
  9.2 2.0 %collective-permute-done.refs_1_ = f32[264,128]{1,0:T(8,128)S(1)} collective-permute-done((f32[264,128]{1,0:T(8,128)S(1)}, f32[264,128]{1,0:T(8,128)S(1)}, u32[]{:S(2)}, u32[]{:S(2)}) %collective-permute-start) | collective-permute-done | bytes 135200 | tf_op jit(solution)/shard_map/ppermute | solution.py:354
  11.2 1.3 %collective-permute-done.1.refs_2_ = f32[264,128]{1,0:T(8,128)S(1)} collective-permute-done((f32[264,128]{1,0:T(8,128)S(1)}, f32[264,128]{1,0:T(8,128)S(1)}, u32[]{:S(2)}, u32[]{:S(2)}) %collective-permute-start.1) | collective-permute-done | bytes 135200 | tf_op jit(solution)/shard_map/ppermute | solution.py:354
  12.5 2.2 %collective-permute-done.2.refs_3_ = f32[264,128]{1,0:T(8,128)S(1)} collective-permute-done((f32[264,128]{1,0:T(8,128)S(1)}, f32[264,128]{1,0:T(8,128)S(1)}, u32[]{:S(2)}, u32[]{:S(2)}) %collective-permute-start.2) | collective-permute-done | bytes 135200 | tf_op jit(solution)/shard_map/ppermute | solution.py:354
  14.7 0.1 group_total.1
  14.8 2.8 %collective-permute-start.3 = (f32[264,128]{1,0:T(8,128)S(1)}, f32[264,128]{1,0:T(8,128)S(1)}, u32[]{:S(2)}, u32[]{:S(2)}) collective-permute-start(f32[264,128]{1,0:T(8,128)S(1)} %group_total.1), channel_id=1, source_target_pairs={{0,8},{2,10},{4,12},{6,14},{8,0},{10,2},{12,4},{14,6},{1,9},{3,11}... | collective-permute-start | bytes 405512 | tf_op jit(solution)/shard_map/ppermute | solution.py:354
  17.6 3.5 %inside_second.1.refs_12_ = f32[256,1024]{1,0:T(8,128)S(1)} custom-call(bf16[256,1024]{1,0:T(8,128)(2,1)S(1)} %get-tuple-element.34.features.refs_5_, bf16[256,128]{1,0:T(8,128)(2,1)S(1)} %get-tuple-element.35.b_input.refs_6_, bf16[256,128]{1,0:T(8,128)(2,1)S(1)} %get-tuple-element.36.c_input.refs_7_.refs_4_, ...), custom_call_target="tpu_custom_call", output_to_operand_aliasing={{}: (7, {})} | custom-call | tf_op jit(solution)/shard_map/inside_second/pallas_call | solution.py:340
  21.1 1.2 %collective-permute-done.3.refs_4_ = f32[264,128]{1,0:T(8,128)S(1)} collective-permute-done((f32[264,128]{1,0:T(8,128)S(1)}, f32[264,128]{1,0:T(8,128)S(1)}, u32[]{:S(2)}, u32[]{:S(2)}) %collective-permute-start.3) | collective-permute-done | bytes 135200 | tf_op jit(solution)/shard_map/ppermute | solution.py:354
  22.3 0.1 entering_states.1
  22.4 0.6 %collective-permute-start.4 = (f32[256,128]{1,0:T(8,128)S(1)}, f32[256,128]{1,0:T(8,128)S(1)}, u32[]{:S(2)}, u32[]{:S(2)}) collective-permute-start(f32[256,128]{1,0:T(8,128)S(1)} %get-tuple-element.51), channel_id=1, source_target_pairs={{0,2},{2,0},{4,6},{6,4},{8,10},{10,8},{12,14},{14,12},{1,3},{3,1},... | collective-permute-start | bytes 393224 | tf_op jit(solution)/shard_map/ppermute | solution.py:354
  23.0 0.8 %collective-permute-start.5 = (f32[256,128]{1,0:T(8,128)S(1)}, f32[256,128]{1,0:T(8,128)S(1)}, u32[]{:S(2)}, u32[]{:S(2)}) collective-permute-start(f32[256,128]{1,0:T(8,128)S(1)} %get-tuple-element.52), channel_id=1, source_target_pairs={{0,4},{2,6},{4,0},{6,2},{8,12},{10,14},{12,8},{14,10},{1,5},{3,7},... | collective-permute-start | bytes 393224 | tf_op jit(solution)/shard_map/ppermute | solution.py:354
  23.8 2.1 %collective-permute-start.6 = (f32[256,128]{1,0:T(8,128)S(1)}, f32[256,128]{1,0:T(8,128)S(1)}, u32[]{:S(2)}, u32[]{:S(2)}) collective-permute-start(f32[256,128]{1,0:T(8,128)S(1)} %get-tuple-element.53), channel_id=1, source_target_pairs={{0,6},{2,4},{4,2},{6,0},{8,14},{10,12},{12,10},{14,8},{1,7},{3,5},... | collective-permute-start | bytes 393224 | tf_op jit(solution)/shard_map/ppermute | solution.py:354
  25.9 1.5 %collective-permute-done.4.refs_1_ = f32[256,128]{1,0:T(8,128)S(1)} collective-permute-done((f32[256,128]{1,0:T(8,128)S(1)}, f32[256,128]{1,0:T(8,128)S(1)}, u32[]{:S(2)}, u32[]{:S(2)}) %collective-permute-start.4) | collective-permute-done | bytes 131104 | tf_op jit(solution)/shard_map/ppermute | solution.py:354
  27.4 0.6 %collective-permute-done.5.refs_2_ = f32[256,128]{1,0:T(8,128)S(1)} collective-permute-done((f32[256,128]{1,0:T(8,128)S(1)}, f32[256,128]{1,0:T(8,128)S(1)}, u32[]{:S(2)}, u32[]{:S(2)}) %collective-permute-start.5) | collective-permute-done | bytes 131104 | tf_op jit(solution)/shard_map/ppermute | solution.py:354
  28.0 2.3 %collective-permute-done.6.refs_3_ = f32[256,128]{1,0:T(8,128)S(1)} collective-permute-done((f32[256,128]{1,0:T(8,128)S(1)}, f32[256,128]{1,0:T(8,128)S(1)}, u32[]{:S(2)}, u32[]{:S(2)}) %collective-permute-start.6) | collective-permute-done | bytes 131104 | tf_op jit(solution)/shard_map/ppermute | solution.py:354
  30.3 0.7 %readout.1.mine = f32[2,256]{1,0:T(2,128)S(1)} custom-call(f32[256,128]{1,0:T(8,128)S(1)} %get-tuple-element.50.refs_0_, f32[256,128]{1,0:T(8,128)S(1)} %collective-permute-done.4.refs_1_, f32[256,128]{1,0:T(8,128)S(1)} %collective-permute-done.5.refs_2_, f32[256,128]{1,0:T(8,128)S(1)} %collective-permute-done.6.refs_3_, ...), custom_call_target="tpu_custom_call" | custom-call | tf_op jit(solution)/shard_map/readout/pallas_call | solution.py:340
  31.0 0.1 collective-permute-start.7
  31.1 1.1 %collective-permute-done.7.other = f32[2,256]{1,0:T(2,128)S(1)} collective-permute-done((f32[2,256]{1,0:T(2,128)S(1)}, f32[2,256]{1,0:T(2,128)S(1)}, u32[]{:S(2)}, u32[]{:S(2)}) %collective-permute-start.7) | collective-permute-done | bytes 2080 | tf_op jit(solution)/shard_map/ppermute | solution.py:354
  32.2 0.7 %values_and_advantages.1 = (f32[1,256]{1,0:T(1,128)}, f32[1,256]{1,0:T(1,128)}) custom-call(f32[2,256]{1,0:T(2,128)S(1)} %readout.1.mine, f32[2,256]{1,0:T(2,128)S(1)} %collective-permute-done.7.other, f32[8,256]{1,0:T(8,128)S(1)} %get-tuple-element.46.refs_4_.suffix, f32[8,128]{1,0:T(8,128)S(1)} %get-tuple-element.55.carry), custom_call_target="tpu_custom_call" | custom-call | tf_op jit(solution)/shard_map/values_and_advantages/pallas_call | solution.py:340
Async XLA Ops:
  4.2 7.0 %collective-permute-start = (f32[264,128]{1,0:T(8,128)S(1)}, f32[264,128]{1,0:T(8,128)S(1)}, u32[]{:S(2)}, u32[]{:S(2)}) collective-permute-start(f32[264,128]{1,0:T(8,128)S(1)} %get-tuple-element.31), channel_id=1, source_target_pairs={{0,2},{2,0},{4,6},{6,4},{8,10},{10,8},{12,14},{14,12},{1,3},{3,1},... | collective-permute-start | bytes 405512 | tf_op jit(solution)/shard_map/ppermute | solution.py:354
  7.2 5.2 %collective-permute-start.1 = (f32[264,128]{1,0:T(8,128)S(1)}, f32[264,128]{1,0:T(8,128)S(1)}, u32[]{:S(2)}, u32[]{:S(2)}) collective-permute-start(f32[264,128]{1,0:T(8,128)S(1)} %get-tuple-element.32), channel_id=1, source_target_pairs={{0,4},{2,6},{4,0},{6,2},{8,12},{10,14},{12,8},{14,10},{1,5},{3,7},... | collective-permute-start | bytes 405512 | tf_op jit(solution)/shard_map/ppermute | solution.py:354
  8.8 5.9 %collective-permute-start.2 = (f32[264,128]{1,0:T(8,128)S(1)}, f32[264,128]{1,0:T(8,128)S(1)}, u32[]{:S(2)}, u32[]{:S(2)}) collective-permute-start(f32[264,128]{1,0:T(8,128)S(1)} %get-tuple-element.33), channel_id=1, source_target_pairs={{0,6},{2,4},{4,2},{6,0},{8,14},{10,12},{12,10},{14,8},{1,7},{3,5},... | collective-permute-start | bytes 405512 | tf_op jit(solution)/shard_map/ppermute | solution.py:354
  14.8 7.5 %collective-permute-start.3 = (f32[264,128]{1,0:T(8,128)S(1)}, f32[264,128]{1,0:T(8,128)S(1)}, u32[]{:S(2)}, u32[]{:S(2)}) collective-permute-start(f32[264,128]{1,0:T(8,128)S(1)} %group_total.1), channel_id=1, source_target_pairs={{0,8},{2,10},{4,12},{6,14},{8,0},{10,2},{12,4},{14,6},{1,9},{3,11}... | collective-permute-start | bytes 405512 | tf_op jit(solution)/shard_map/ppermute | solution.py:354
  22.4 5.0 %collective-permute-start.4 = (f32[256,128]{1,0:T(8,128)S(1)}, f32[256,128]{1,0:T(8,128)S(1)}, u32[]{:S(2)}, u32[]{:S(2)}) collective-permute-start(f32[256,128]{1,0:T(8,128)S(1)} %get-tuple-element.51), channel_id=1, source_target_pairs={{0,2},{2,0},{4,6},{6,4},{8,10},{10,8},{12,14},{14,12},{1,3},{3,1},... | collective-permute-start | bytes 393224 | tf_op jit(solution)/shard_map/ppermute | solution.py:354
  23.0 5.0 %collective-permute-start.5 = (f32[256,128]{1,0:T(8,128)S(1)}, f32[256,128]{1,0:T(8,128)S(1)}, u32[]{:S(2)}, u32[]{:S(2)}) collective-permute-start(f32[256,128]{1,0:T(8,128)S(1)} %get-tuple-element.52), channel_id=1, source_target_pairs={{0,4},{2,6},{4,0},{6,2},{8,12},{10,14},{12,8},{14,10},{1,5},{3,7},... | collective-permute-start | bytes 393224 | tf_op jit(solution)/shard_map/ppermute | solution.py:354
  23.8 6.4 %collective-permute-start.6 = (f32[256,128]{1,0:T(8,128)S(1)}, f32[256,128]{1,0:T(8,128)S(1)}, u32[]{:S(2)}, u32[]{:S(2)}) collective-permute-start(f32[256,128]{1,0:T(8,128)S(1)} %get-tuple-element.53), channel_id=1, source_target_pairs={{0,6},{2,4},{4,2},{6,0},{8,14},{10,12},{12,10},{14,8},{1,7},{3,5},... | collective-permute-start | bytes 393224 | tf_op jit(solution)/shard_map/ppermute | solution.py:354
  31.0 1.2 %collective-permute-start.7 = (f32[2,256]{1,0:T(2,128)S(1)}, f32[2,256]{1,0:T(2,128)S(1)}, u32[]{:S(2)}, u32[]{:S(2)}) collective-permute-start(f32[2,256]{1,0:T(2,128)S(1)} %readout.1.mine), channel_id=1, source_target_pairs={{0,1},{1,0},{2,3},{3,2},{4,5},{5,4},{6,7},{7,6},{8,9},{9,8},{10,11... | collective-permute-start | bytes 6152 | tf_op jit(solution)/shard_map/ppermute | solution.py:354

commit v4 on v3

--- a/solution.py
+++ b/solution.py
@@ -12,7 +12,9 @@
 GROUP = 4
 LANES = 128
 LATE = 0
-SHARES = ((0, 2, 2, 8, 8), (0, 0, 4, 8, 8))
+FIRST_ORDERS = ((0, 1, 2, 3), (0, 2, 1, 3))
+LAST_ORDERS = ((0, 3, 1, 2), (0, 1, 2, 3))
+SHARES = ((0, 2, 4, 8), (0, 0, 4, 8))
 EXTRA = 8
 NORM_EPSILON = 1e-05
 VMEM_BYTES = 24 * 1024 * 1024
@@ -56,6 +58,19 @@
 
 def member_index():
     return lax.rem(lax.axis_index("ctx"), GROUP)
+
+
+def partner_index(orders, slot):
+    return lax.bitwise_xor(member_index(), jnp.where(lax.axis_index("head") == 0, orders[0][slot], orders[1][slot]))
+
+
+def each_place(body):
+    for core in range(len(FIRST_ORDERS)):
+        for v in range(GROUP):
+
+            @pl.when((member_index() == v) & (lax.axis_index("head") == core))
+            def _():
+                body(v, *([orders[core].index(v ^ m) for m in range(GROUP)] for orders in (FIRST_ORDERS, LAST_ORDERS)))
 
 
 def prepare(cum_ref, skip, norm, weight, columns_out, wide_out):
@@ -111,10 +126,9 @@
         intra_groups(0, features, b_input, c_input, cum_out, step_out, columns, wide_row, inside)
 
     keys = b_input[...].T
-    me = member_index()
     row = iota((EXTRA, LANES), 0)
     for j in (1, 2, 3, 0):
-        part = lax.bitwise_xor(me, j)
+        part = partner_index(FIRST_ORDERS, j)
         first_head = part * (heads // GROUP)
         feat = features[:, pl.ds(pl.multiple_of(part * wide, wide), wide)]
         spread = dot(by_token, selector(heads, 128, first_head, wide))
@@ -187,10 +201,6 @@
     intra_groups(2, features, b_input, c_input, cum_ref, step_ref, columns, wide_row, out)
 
 
-def in_order(pieces, me_static):
-    return [pieces[me_static ^ m] for m in range(GROUP)]
-
-
 def parts_of(piece):
     halves = 2
     size = (piece.shape[0] - EXTRA) // halves
@@ -224,21 +234,19 @@
 
 def total_kernel(*refs):
     pieces, out = refs[:GROUP], refs[-1]
-    me = member_index()
-    for v in range(GROUP):
-
-        @pl.when(me == v)
-        def _():
-            members = [parts_of(piece) for piece in in_order(pieces, v)]
-            states, decays, keeps, _ = members[0]
-            for member in members[1:]:
-                states = carry_on(states, member)
-                decays = add(decays, member[1])
-                keeps = keeps * member[2]
-            amount = members[-1][3]
-            for member in members[-2::-1]:
-                amount = member[3] + member[2] * amount
-            write_piece(out, states, decays, keeps, amount)
+
+    @each_place
+    def _(me, first, last):
+        members = [parts_of(pieces[slot]) for slot in first]
+        states, decays, keeps, _ = members[0]
+        for member in members[1:]:
+            states = carry_on(states, member)
+            decays = add(decays, member[1])
+            keeps = keeps * member[2]
+        amount = members[-1][3]
+        for member in members[-2::-1]:
+            amount = member[3] + member[2] * amount
+        write_piece(out, states, decays, keeps, amount)
 
 
 def round_kernel(bit, *refs):
@@ -258,36 +266,38 @@
         write_piece(total_out, carry_on(mine[0], theirs), decays, keeps, mine[3] + mine[2] * theirs[3])
 
 
-def entering_kernel(bit, has_past, *refs):
-    pieces, got = refs[:GROUP], refs[GROUP]
-    past = refs[GROUP + 1] if has_past else None
-    outs, carry_out, inside = refs[-GROUP - 2 : -2], refs[-2], refs[-1]
-    near = refs[GROUP + 1 + has_past : GROUP + 8 + has_past]
-    intra_groups(3, *near, inside)
-    ctx = lax.axis_index("ctx")
-    me = lax.rem(ctx, GROUP)
-    is_later = lax.rem(ctx // GROUP // bit, 2) == 1
-    theirs = parts_of(got)
-    for v in range(GROUP):
-
-        @pl.when(me == v)
-        def _():
-            members = [parts_of(piece) for piece in in_order(pieces, v)]
+def entering_kernel(bit, has_got, has_past, *refs):
+    pieces, refs = refs[:GROUP], refs[GROUP:]
+    got, refs = (refs[0], refs[1:]) if has_got else (None, refs)
+    past, refs = (refs[0], refs[1:]) if has_past else (None, refs)
+    outs, carry_out = refs[-GROUP - 1 : -1], refs[-1]
+    is_later = lax.rem(lax.axis_index("ctx") // GROUP // bit, 2) == 1
+
+    @each_place
+    def _(me, first, last):
+        members = [parts_of(pieces[slot]) for slot in first]
+        size = members[0][0][0].shape
+        arriving = [jnp.zeros(size, jnp.float32)] * 2
+        keeps, amount = jnp.ones((1, LANES), jnp.float32), jnp.zeros((1, LANES), jnp.float32)
+        if has_got:
+            theirs = parts_of(got)
             arriving = [jnp.where(is_later, state, 0.0) for state in theirs[0]]
-            amount = jnp.where(is_later, 0.0, theirs[3])
-            if has_past:
-                old = parts_of(past)
-                arriving = carry_on(arriving, old)
-                amount = old[3] + old[2] * amount
-            size = arriving[0].shape[0]
-            for m in range(GROUP):
-                for k, state in enumerate(arriving):
-                    outs[v ^ m][k * size : (k + 1) * size, :] = state
-                if m < GROUP - 1:
-                    arriving = carry_on(arriving, members[m])
-            for m in range(GROUP - 1, v, -1):
-                amount = members[m][3] + members[m][2] * amount
-            carry_out[...] = jnp.broadcast_to(amount, carry_out.shape)
+            keeps = jnp.where(is_later, keeps, theirs[2])
+            amount = jnp.where(is_later, amount, theirs[3])
+        if has_past:
+            old = parts_of(past)
+            arriving = carry_on(arriving, old)
+            amount = old[3] + old[2] * amount
+        for m in range(GROUP):
+            for k, state in enumerate(arriving):
+                outs[last[m]][k * size[0] : (k + 1) * size[0], :] = state
+            if m < GROUP - 1:
+                arriving = carry_on(arriving, members[m])
+        for m in range(GROUP - 1, me, -1):
+            amount = members[m][3] + members[m][2] * amount
+            keeps = keeps * members[m][2]
+        row = iota(carry_out.shape, 0)
+        carry_out[...] = jnp.where(row == 0, amount, keeps)
 
 
 def readout_kernel(*refs):
@@ -295,13 +305,12 @@
     span, state = c_input.shape
     heads = wide_row.shape[1] // HEAD_DIM
     wide = wide_row.shape[1] // GROUP
-    me = member_index()
     queries = c_input[...]
     by_token = columns[:, 128:]
     squares = jnp.zeros((span, 128), jnp.float32)
     values = jnp.zeros((span, 128), jnp.float32)
     for j in range(GROUP):
-        part = lax.bitwise_xor(me, j)
+        part = partner_index(LAST_ORDERS, j)
         lanes = pl.ds(pl.multiple_of(part * wide, wide), wide)
         value = jnp.concatenate([entering[j][:state, :], entering[j][state:, :]], axis=1)
         high = value.astype(jnp.bfloat16)
@@ -318,11 +327,15 @@
     out[1:2, :] = jnp.sum(values.T, axis=0, keepdims=True)
 
 
-def last_kernel(channels, mine, other, suffix, carry, values_out, advantages_out, values, advantages, sems):
+def last_kernel(channels, first_group_early, mine, other, suffix, carry, got, values_out, advantages_out, values, advantages, sems):
     sums = mine[...] + other[...]
     value = sums[1:2] / jnp.sqrt(sums[0:1] / channels + NORM_EPSILON)
     values[...] = value
-    advantages[...] = suffix[0:1, :] + suffix[1:2, :] * carry[0:1, 0:1] - value
+    amount = carry[0:1, 0:1]
+    if first_group_early:
+        later = jnp.where(lax.axis_index("ctx") < GROUP, parts_of(got)[3][:, 0:1], 0.0)
+        amount = amount + carry[1:2, 0:1] * later
+    advantages[...] = suffix[0:1, :] + suffix[1:2, :] * amount - value
     copies = [
         pltpu.make_async_copy(values, values_out, sems.at[0]),
         pltpu.make_async_copy(advantages, advantages_out, sems.at[1]),
@@ -352,6 +365,16 @@
 def swap(value, axis, mask):
     count = lax.axis_size(axis)
     return lax.ppermute(value, axis, [(k, k ^ mask) for k in range(count)])
+
+
+def swap_slots(orders, pieces):
+    cores = lax.axis_size("head")
+    assert cores == len(orders)
+    pairs = [
+        [(k * cores + core, (k ^ orders[core][slot]) * cores + core) for k in range(lax.axis_size("ctx")) for core in range(cores)]
+        for slot in range(1, GROUP)
+    ]
+    return [pieces[0]] + [lax.ppermute(piece, ("ctx", "head"), pair) for piece, pair in zip(pieces[1:], pairs)]
 
 
 def local(
@@ -419,7 +442,7 @@
         ],
     )
     pieces, made = made[:GROUP], made[GROUP:]
-    got = [pieces[0]] + [swap(pieces[j], "ctx", j) for j in range(1, GROUP)]
+    got = swap_slots(FIRST_ORDERS, pieces)
     columns, wide_row, inside, suffix = call(
         first_kernel,
         [columns_shape, wide_shape, inside_shape, ((8, span), f32)],
@@ -443,25 +466,37 @@
         bit *= 2
     other = swap(total, "ctx", GROUP * bit)
     (inside,) = call(second_kernel, [inside_shape], "inside_second", *near, inside, aliases={len(near): 0})
-    operands = (*got, other, *([] if past is None else [past]), *near, inside)
-    made = call(
-        functools.partial(entering_kernel, bit, past is not None),
-        [states] * GROUP + [((8, LANES), f32), inside_shape],
-        "entering_states",
-        *operands,
-        aliases={len(operands) - 1: GROUP + 1},
-    )
-    entering, carry, inside = made[:GROUP], made[GROUP], made[GROUP + 1]
-    arrived = [entering[0]] + [swap(entering[j], "ctx", j) for j in range(1, GROUP)]
-    (sums,) = call(readout_kernel, [((2, span), f32)], "readout", *arrived, queries, columns, inside, wide_row)
+
+    def finish(has_got):
+        operands = (*got, *([other] if has_got else []), *([] if past is None else [past]))
+        made = call(
+            functools.partial(entering_kernel, bit, has_got, past is not None),
+            [states] * GROUP + [((8, LANES), f32)],
+            "entering_states",
+            *operands,
+            *([] if past is None else [inside]),
+        )
+        arrived = swap_slots(LAST_ORDERS, made[:GROUP])
+        (sums,) = call(readout_kernel, [((2, span), f32)], "readout", *arrived, queries, columns, inside, wide_row)
+        return sums, made[GROUP]
+
+    first_group_early = groups == 2
+    if first_group_early:
+        is_first = lax.axis_index("ctx") < GROUP
+        nothing = lambda: (jnp.zeros((2, span), f32), jnp.zeros((8, LANES), f32))
+        early = lax.cond(is_first, lambda: finish(False), nothing)
+        sums, carry = lax.cond(is_first, lambda: early, lambda: finish(True))
+    else:
+        sums, carry = finish(True)
     values, advantages = call(
-        functools.partial(last_kernel, width * lax.axis_size("head")),
+        functools.partial(last_kernel, width * lax.axis_size("head"), first_group_early),
         [((1, span), f32)] * 2,
         "values_and_advantages",
         sums,
         swap(sums, "head", 1),
         suffix,
         carry,
+        other,
         hbm_out=True,
         scratch=[pltpu.VMEM((1, span), f32), pltpu.VMEM((1, span), f32), pltpu.SemaphoreType.DMA((2,))],
     )

time: 33 us -> 31.4 us (0.952)
  the two profiles are of different devices: /device:TPU:0 before, /device:TPU:21 now
where the time goes in v4:
time: 31.4 us; the launch traced here: 31.2 us
  starting transfers between devices  11.8 us (38%)
  waiting for transfers between devices  9.81 us (31%)
  Pallas kernels  8.85 us (28%)
  between operations  0.69 us (2%)
    pallas_call x7, Pallas kernels, call(): pl.pallas_call(kernel, out_shape=[jax.ShapeDtypeStruct(*shape) for shape...  8.85 us
    ppermute x6, waiting for transfers between devices, swap_slots(): lax.ppermute(piece, ('ctx', 'head'), pair)  6.72 us
    ppermute x2, starting transfers between devices, swap(): return lax.ppermute(value, axis, [(k, k ^ mask) for k in range(count)])  6.39 us
    ppermute x6, starting transfers between devices, swap_slots(): lax.ppermute(piece, ('ctx', 'head'), pair)  5.43 us
    ppermute x2, waiting for transfers between devices, swap(): return lax.ppermute(value, axis, [(k, k ^ mask) for k in range(count)])  3.09 us
  transfers between devices with their start and end apart: 8, of which 7 were waited for; matrix products, arithmetic and copies ran while one was open for 0% of the time, Pallas kernels for 16%

profile of v4, /device:TPU:21, one launch (start us, length us, event | category | flops | bytes accessed | tf_op | source)
XLA Modules:
  0.0 31.2 jit_solution(3930281098637405457)
XLA Ops:
  0.6 2.3 %block_states.1 = (f32[264,128]{1,0:T(8,128)S(1)}, f32[264,128]{1,0:T(8,128)S(1)}, f32[264,128]{1,0:T(8,128)S(1)}, f32[264,128]{1,0:T(8,128)S(1)}, bf16[256,1024...) custom-call(f32[32,256]{1,0:T(8,128)} %refs_0_.1, ...), custom_call_target="tpu_custom_call" | custom-call | tf_op jit(solution)/shard_map/block_states/pallas_call | solution.py:353
  2.9 1.4 %collective-permute-start.6 = (f32[264,128]{1,0:T(8,128)S(1)}, f32[264,128]{1,0:T(8,128)S(1)}, u32[]{:S(2)}, u32[]{:S(2)}) collective-permute-start(f32[264,128]{1,0:T(8,128)S(1)} %get-tuple-element.92), channel_id=1, source_target_pairs={{0,2},{1,5},{2,0},{3,7},{4,6},{5,1},{6,4},{7,3},{8,10},{9,13},{10,... | collective-permute-start | bytes 405512 | tf_op jit(solution)/shard_map/ppermute | solution.py:377
  4.3 1.2 %collective-permute-start.7 = (f32[264,128]{1,0:T(8,128)S(1)}, f32[264,128]{1,0:T(8,128)S(1)}, u32[]{:S(2)}, u32[]{:S(2)}) collective-permute-start(f32[264,128]{1,0:T(8,128)S(1)} %get-tuple-element.93), channel_id=1, source_target_pairs={{0,4},{1,3},{2,6},{3,1},{4,0},{5,7},{6,2},{7,5},{8,12},{9,11},{10,... | collective-permute-start | bytes 405512 | tf_op jit(solution)/shard_map/ppermute | solution.py:377
  5.5 0.1 collective-permute-start.8
  5.7 2.7 %inside_first.1 = (bf16[256,256]{1,0:T(8,128)(2,1)S(1)}, f32[2,1024]{1,0:T(2,128)S(1)}, f32[256,1024]{1,0:T(8,128)S(1)}, f32[8,256]{1,0:T(8,128)S(1)}) custom-call(bf16[256,1024]{1,0:T(8,128)(2,1)S(1)} %get-tuple-element.95.features, bf16[256,128]{1,0:T(8,128)(2,1)S(1)} %get-tuple-element.96.b_input, ...), custom_call_target="tpu_custom_call", output_to_operand_aliasing={{0}: (9, {}), {1}: (10, {}), {2}: (11, {})} | custom-call | tf_op jit(solution)/shard_map/inside_first/pallas_call | solution.py:353
  8.3 0.0 collective-permute-done.6.refs_1_
  8.3 0.7 %collective-permute-done.7.refs_2_ = f32[264,128]{1,0:T(8,128)S(1)} collective-permute-done((f32[264,128]{1,0:T(8,128)S(1)}, f32[264,128]{1,0:T(8,128)S(1)}, u32[]{:S(2)}, u32[]{:S(2)}) %collective-permute-start.7) | collective-permute-done | bytes 135200 | tf_op jit(solution)/shard_map/ppermute | solution.py:377
  9.1 2.2 %collective-permute-done.8.refs_3_ = f32[264,128]{1,0:T(8,128)S(1)} collective-permute-done((f32[264,128]{1,0:T(8,128)S(1)}, f32[264,128]{1,0:T(8,128)S(1)}, u32[]{:S(2)}, u32[]{:S(2)}) %collective-permute-start.8) | collective-permute-done | bytes 135200 | tf_op jit(solution)/shard_map/ppermute | solution.py:377
  11.3 0.1 group_total.1
  11.4 0.1 collective-permute-start.9
  11.5 2.4 %inside_second.1 = f32[256,1024]{1,0:T(8,128)S(1)} custom-call(bf16[256,1024]{1,0:T(8,128)(2,1)S(1)} %get-tuple-element.95.features, bf16[256,128]{1,0:T(8,128)(2,1)S(1)} %get-tuple-element.96.b_input, bf16[256,128]{1,0:T(8,128)(2,1)S(1)} %get-tuple-element.97.c_input, f32[32,256]{1,0:T(8,128)S(1)} %get-tuple-element.98.cum_ref, ...), custom_call_target="tpu_custom_call", output_to_operand_aliasing={{}: (7, {})} | custom-call | tf_op jit(solution)/shard_map/inside_second/pallas_call | solution.py:353
  13.9 2.3 %collective-permute-done.9.got = f32[264,128]{1,0:T(8,128)S(1)} collective-permute-done((f32[264,128]{1,0:T(8,128)S(1)}, f32[264,128]{1,0:T(8,128)S(1)}, u32[]{:S(2)}, u32[]{:S(2)}) %collective-permute-start.9) | collective-permute-done | bytes 135200 | tf_op jit(solution)/shard_map/ppermute | solution.py:367
  16.2 7.2 %conditional.3 = (f32[2,256]{1,0:T(2,128)S(1)}, f32[8,128]{1,0:T(8,128)S(1)}) conditional(s32[]{:T(128)} %convert_element_type.4, (f32[264,128]{1,0:T(8,128)S(1)}, f32[264,128]{1,0:T(8,128)S(1)}, f32[264,128]{1,0:T(8,128)S(1)}, f32[264,128]{1,0:T(8,128)S(1)}, f32[264,128]{1,0:T(8,128)S(1)}, /*index=5*/bf16[256,128]{1,0:T(8,128)(2,1)S(1)}, ...), branch_computations={%region_2.0_spmd, %region_3.0_spmd} | conditional | bytes 1573000 | solution.py:488
  16.2 0.1 entering_states.3
  16.3 0.3 collective-permute-start.3
  16.5 1.2 %collective-permute-start.4 = (f32[256,128]{1,0:T(8,128)S(1)}, f32[256,128]{1,0:T(8,128)S(1)}, u32[]{:S(2)}, u32[]{:S(2)}) collective-permute-start(f32[256,128]{1,0:T(8,128)S(1)} %get-tuple-element.58), channel_id=1, source_target_pairs={{0,2},{1,5},{2,0},{3,7},{4,6},{5,1},{6,4},{7,3},{8,10},{9,13},{10,... | collective-permute-start | bytes 393224 | tf_op jit(solution)/shard_map/cond/branch_0_fun/ppermute | solution.py:377
  17.8 1.2 %collective-permute-start.5 = (f32[256,128]{1,0:T(8,128)S(1)}, f32[256,128]{1,0:T(8,128)S(1)}, u32[]{:S(2)}, u32[]{:S(2)}) collective-permute-start(f32[256,128]{1,0:T(8,128)S(1)} %get-tuple-element.59), channel_id=1, source_target_pairs={{0,4},{1,7},{2,6},{3,5},{4,0},{5,3},{6,2},{7,1},{8,12},{9,15},{10,... | collective-permute-start | bytes 393224 | tf_op jit(solution)/shard_map/cond/branch_0_fun/ppermute | solution.py:377
  19.0 1.5 %collective-permute-done.3.refs_1_ = f32[256,128]{1,0:T(8,128)S(1)} collective-permute-done((f32[256,128]{1,0:T(8,128)S(1)}, f32[256,128]{1,0:T(8,128)S(1)}, u32[]{:S(2)}, u32[]{:S(2)}) %collective-permute-start.3) | collective-permute-done | bytes 131104 | tf_op jit(solution)/shard_map/cond/branch_0_fun/ppermute | solution.py:377
  20.5 0.2 collective-permute-done.4.refs_2_
  20.7 2.1 %collective-permute-done.5.refs_3_ = f32[256,128]{1,0:T(8,128)S(1)} collective-permute-done((f32[256,128]{1,0:T(8,128)S(1)}, f32[256,128]{1,0:T(8,128)S(1)}, u32[]{:S(2)}, u32[]{:S(2)}) %collective-permute-start.5) | collective-permute-done | bytes 131104 | tf_op jit(solution)/shard_map/cond/branch_0_fun/ppermute | solution.py:377
  22.8 0.7 %readout.3 = f32[2,256]{1,0:T(2,128)S(1)} custom-call(f32[256,128]{1,0:T(8,128)S(1)} %get-tuple-element.56.refs_0_, f32[256,128]{1,0:T(8,128)S(1)} %collective-permute-done.3.refs_1_, f32[256,128]{1,0:T(8,128)S(1)} %collective-permute-done.4.refs_2_, f32[256,128]{1,0:T(8,128)S(1)} %collective-permute-done.5.refs_3_, ...), custom_call_target="tpu_custom_call" | custom-call | tf_op jit(solution)/shard_map/cond/branch_0_fun/readout/pallas_call | solution.py:353
  23.5 6.3 %collective-permute-start.10 = (f32[2,256]{1,0:T(2,128)S(1)}, f32[2,256]{1,0:T(2,128)S(1)}, u32[]{:S(2)}, u32[]{:S(2)}) collective-permute-start(f32[2,256]{1,0:T(2,128)S(1)} %get-tuple-element.111.mine), channel_id=1, source_target_pairs={{0,1},{1,0},{2,3},{3,2},{4,5},{5,4},{6,7},{7,6},{8,9},{9,8},{10,11... | collective-permute-start | bytes 6152 | tf_op jit(solution)/shard_map/ppermute | solution.py:367
  29.7 0.8 %collective-permute-done.10.other = f32[2,256]{1,0:T(2,128)S(1)} collective-permute-done((f32[2,256]{1,0:T(2,128)S(1)}, f32[2,256]{1,0:T(2,128)S(1)}, u32[]{:S(2)}, u32[]{:S(2)}) %collective-permute-start.10) | collective-permute-done | bytes 2080 | tf_op jit(solution)/shard_map/ppermute | solution.py:367
  30.5 0.7 %values_and_advantages.1 = (f32[1,256]{1,0:T(1,128)}, f32[1,256]{1,0:T(1,128)}) custom-call(f32[2,256]{1,0:T(2,128)S(1)} %get-tuple-element.111.mine, f32[2,256]{1,0:T(2,128)S(1)} %collective-permute-done.10.other, f32[8,256]{1,0:T(8,128)S(1)} %get-tuple-element.107.refs_4_.suffix, f32[8,128]{1,0:T(8,128)S(1)} %get-tuple-element.112.carry, ...), custom_call_target="tpu_custom_call" | custom-call | tf_op jit(solution)/shard_map/values_and_advantages/pallas_call | solution.py:353
  (3 shorter events, 0.0 us)
Async XLA Ops:
  2.9 5.4 %collective-permute-start.6 = (f32[264,128]{1,0:T(8,128)S(1)}, f32[264,128]{1,0:T(8,128)S(1)}, u32[]{:S(2)}, u32[]{:S(2)}) collective-permute-start(f32[264,128]{1,0:T(8,128)S(1)} %get-tuple-element.92), channel_id=1, source_target_pairs={{0,2},{1,5},{2,0},{3,7},{4,6},{5,1},{6,4},{7,3},{8,10},{9,13},{10,... | collective-permute-start | bytes 405512 | tf_op jit(solution)/shard_map/ppermute | solution.py:377
  4.3 4.8 %collective-permute-start.7 = (f32[264,128]{1,0:T(8,128)S(1)}, f32[264,128]{1,0:T(8,128)S(1)}, u32[]{:S(2)}, u32[]{:S(2)}) collective-permute-start(f32[264,128]{1,0:T(8,128)S(1)} %get-tuple-element.93), channel_id=1, source_target_pairs={{0,4},{1,3},{2,6},{3,1},{4,0},{5,7},{6,2},{7,5},{8,12},{9,11},{10,... | collective-permute-start | bytes 405512 | tf_op jit(solution)/shard_map/ppermute | solution.py:377
  5.5 5.8 %collective-permute-start.8 = (f32[264,128]{1,0:T(8,128)S(1)}, f32[264,128]{1,0:T(8,128)S(1)}, u32[]{:S(2)}, u32[]{:S(2)}) collective-permute-start(f32[264,128]{1,0:T(8,128)S(1)} %get-tuple-element.94), channel_id=1, source_target_pairs={{0,6},{1,7},{2,4},{3,5},{4,2},{5,3},{6,0},{7,1},{8,14},{9,15},{10,... | collective-permute-start | bytes 405512 | tf_op jit(solution)/shard_map/ppermute | solution.py:377
  11.4 4.8 %collective-permute-start.9 = (f32[264,128]{1,0:T(8,128)S(1)}, f32[264,128]{1,0:T(8,128)S(1)}, u32[]{:S(2)}, u32[]{:S(2)}) collective-permute-start(f32[264,128]{1,0:T(8,128)S(1)} %group_total.1), channel_id=1, source_target_pairs={{0,8},{2,10},{4,12},{6,14},{8,0},{10,2},{12,4},{14,6},{1,9},{3,11}... | collective-permute-start | bytes 405512 | tf_op jit(solution)/shard_map/ppermute | solution.py:367
  16.3 4.2 %collective-permute-start.3 = (f32[256,128]{1,0:T(8,128)S(1)}, f32[256,128]{1,0:T(8,128)S(1)}, u32[]{:S(2)}, u32[]{:S(2)}) collective-permute-start(f32[256,128]{1,0:T(8,128)S(1)} %get-tuple-element.57), channel_id=1, source_target_pairs={{0,6},{1,3},{2,4},{3,1},{4,2},{5,7},{6,0},{7,5},{8,14},{9,11},{10,... | collective-permute-start | bytes 393224 | tf_op jit(solution)/shard_map/cond/branch_0_fun/ppermute | solution.py:377
  16.5 4.1 %collective-permute-start.4 = (f32[256,128]{1,0:T(8,128)S(1)}, f32[256,128]{1,0:T(8,128)S(1)}, u32[]{:S(2)}, u32[]{:S(2)}) collective-permute-start(f32[256,128]{1,0:T(8,128)S(1)} %get-tuple-element.58), channel_id=1, source_target_pairs={{0,2},{1,5},{2,0},{3,7},{4,6},{5,1},{6,4},{7,3},{8,10},{9,13},{10,... | collective-permute-start | bytes 393224 | tf_op jit(solution)/shard_map/cond/branch_0_fun/ppermute | solution.py:377
  17.8 5.0 %collective-permute-start.5 = (f32[256,128]{1,0:T(8,128)S(1)}, f32[256,128]{1,0:T(8,128)S(1)}, u32[]{:S(2)}, u32[]{:S(2)}) collective-permute-start(f32[256,128]{1,0:T(8,128)S(1)} %get-tuple-element.59), channel_id=1, source_target_pairs={{0,4},{1,7},{2,6},{3,5},{4,0},{5,3},{6,2},{7,1},{8,12},{9,15},{10,... | collective-permute-start | bytes 393224 | tf_op jit(solution)/shard_map/cond/branch_0_fun/ppermute | solution.py:377
  23.5 7.1 %collective-permute-start.10 = (f32[2,256]{1,0:T(2,128)S(1)}, f32[2,256]{1,0:T(2,128)S(1)}, u32[]{:S(2)}, u32[]{:S(2)}) collective-permute-start(f32[2,256]{1,0:T(2,128)S(1)} %get-tuple-element.111.mine), channel_id=1, source_target_pairs={{0,1},{1,0},{2,3},{3,2},{4,5},{5,4},{6,7},{7,6},{8,9},{9,8},{10,11... | collective-permute-start | bytes 6152 | tf_op jit(solution)/shard_map/ppermute | solution.py:367

commit v5 on v4

--- a/solution.py
+++ b/solution.py
@@ -11,10 +11,11 @@
 SPAN = 256
 GROUP = 4
 LANES = 128
-LATE = 0
 FIRST_ORDERS = ((0, 1, 2, 3), (0, 2, 1, 3))
+EARLY_ORDERS = ((0, 3, 1, 2), (0, 1, 2, 3))
 LAST_ORDERS = ((0, 3, 1, 2), (0, 1, 2, 3))
-SHARES = ((0, 2, 4, 8), (0, 0, 4, 8))
+READOUTS = ((0, 1, 2, 3),)
+SHARES = (((0, 1, 4, 8), (0, 0, 7, 8)), ((0, 1, 6, 8), (0, 0, 6, 8)))
 EXTRA = 8
 NORM_EPSILON = 1e-05
 VMEM_BYTES = 24 * 1024 * 1024
@@ -52,10 +53,6 @@
     return jnp.where(match, 1.0, 0.0).astype(jnp.bfloat16)
 
 
-def is_late():
-    return lax.axis_index("head") == LATE
-
-
 def member_index():
     return lax.rem(lax.axis_index("ctx"), GROUP)
 
@@ -64,13 +61,13 @@
     return lax.bitwise_xor(member_index(), jnp.where(lax.axis_index("head") == 0, orders[0][slot], orders[1][slot]))
 
 
-def each_place(body):
+def each_place(last_orders, body):
     for core in range(len(FIRST_ORDERS)):
         for v in range(GROUP):
 
             @pl.when((member_index() == v) & (lax.axis_index("head") == core))
             def _():
-                body(v, *([orders[core].index(v ^ m) for m in range(GROUP)] for orders in (FIRST_ORDERS, LAST_ORDERS)))
+                body(v, *([orders[core].index(v ^ m) for m in range(GROUP)] for orders in (FIRST_ORDERS, last_orders)))
 
 
 def prepare(cum_ref, skip, norm, weight, columns_out, wide_out):
@@ -83,18 +80,38 @@
     wide_out[1:2, :] = over_channels(column(skip[...]), 0, heads * HEAD_DIM)
 
 
+def write_pieces(slots, token, features, b_input, total, still_open, first_sum, outs):
+    keys = b_input[...].T
+    state = keys.shape[0]
+    heads = total.shape[0]
+    wide = features.shape[1] // GROUP
+    row = iota((EXTRA, LANES), 0)
+    by_token = token[...].astype(jnp.bfloat16)
+    for slot, out in zip(slots, outs):
+        part = partner_index(FIRST_ORDERS, slot)
+        first_head = part * (heads // GROUP)
+        feat = features[:, pl.ds(pl.multiple_of(part * wide, wide), wide)]
+        spread = dot(by_token, selector(heads, 128, first_head, wide))
+        scaled = (spread * feat.astype(jnp.float32)).astype(jnp.bfloat16)
+        states = dot(keys, scaled)
+        decay = over_channels(total, first_head, wide)
+        extra = jnp.where(row == wide // LANES, still_open, first_sum)
+        for k in range(wide // LANES):
+            out[k * state : (k + 1) * state, :] = states[:, k * LANES : (k + 1) * LANES]
+            extra = jnp.where(row == k, decay[:, k * LANES : (k + 1) * LANES], extra)
+        out[wide // LANES * state :, :] = extra
+
+
 def state_kernel(*refs):
     sources, refs = refs[:11], refs[11:]
-    pieces, refs = refs[:GROUP], refs[GROUP:]
-    features, b_input, c_input, cum_out, step_out, rows, skip, norm, weight, columns, wide_row, inside = refs[:12]
-    step_in, decay_log, rewards, keep, ends, sems = refs[12:]
+    pieces, refs = refs[: GROUP - 1], refs[GROUP - 1 :]
+    features, b_input, c_input, cum_out, step_out, rows, skip, norm, weight, token, columns, wide_row, inside = refs[:13]
+    step_in, decay_log, rewards, keep, ends, sems = refs[13:]
     targets = (step_in, decay_log, rewards, keep, ends, features, b_input, c_input, skip, norm, weight)
     copies = [pltpu.make_async_copy(src, dst, sems.at[i]) for i, (src, dst) in enumerate(zip(sources, targets))]
     for copy in copies:
         copy.start()
     heads, span = step_in.shape
-    state = b_input.shape[1]
-    wide = features.shape[1] // GROUP
     for copy in copies[:5]:
         copy.wait()
     raw = step_in[...]
@@ -113,37 +130,33 @@
     still_open = jnp.where(through[:, span - 1 :] == 0.0, 1.0, 0.0)
     coefficient = jnp.exp(total - cum) * step
     pad = jnp.zeros((128 - 3 * heads, span), jnp.float32)
-    by_token = jnp.concatenate(split3(coefficient) + (pad,), axis=0).T.astype(jnp.bfloat16)
+    token[...] = jnp.concatenate(split3(coefficient) + (pad,), axis=0).T
     cum_out[...] = cum
     step_out[...] = step
-    rows[...] = jnp.concatenate([live, through, before, jnp.zeros((5, span), jnp.float32)], axis=0)
+    flags = [jnp.broadcast_to(value, (1, span)) for value in (still_open, first_sum)]
+    rows[...] = jnp.concatenate([live, through, before, *flags, jnp.zeros((3, span), jnp.float32)], axis=0)
     for copy in copies[5:]:
         copy.wait()
 
-    @pl.when(is_late())
+    @pl.when(share_bound(1) > 0)
     def _():
         prepare(cum_out, skip, norm, weight, columns, wide_row)
         intra_groups(0, features, b_input, c_input, cum_out, step_out, columns, wide_row, inside)
 
-    keys = b_input[...].T
-    row = iota((EXTRA, LANES), 0)
-    for j in (1, 2, 3, 0):
-        part = partner_index(FIRST_ORDERS, j)
-        first_head = part * (heads // GROUP)
-        feat = features[:, pl.ds(pl.multiple_of(part * wide, wide), wide)]
-        spread = dot(by_token, selector(heads, 128, first_head, wide))
-        scaled = (spread * feat.astype(jnp.float32)).astype(jnp.bfloat16)
-        states = dot(keys, scaled)
-        decay = over_channels(total, first_head, wide)
-        extra = jnp.where(row == wide // LANES, still_open, first_sum)
-        for k in range(wide // LANES):
-            pieces[j][k * state : (k + 1) * state, :] = states[:, k * LANES : (k + 1) * LANES]
-            extra = jnp.where(row == k, decay[:, k * LANES : (k + 1) * LANES], extra)
-        pieces[j][wide // LANES * state :, :] = extra
+    write_pieces((1, 2, 3), token, features, b_input, total, still_open, first_sum, pieces)
+
+
+def share_bound(k):
+    first_group, first_core = lax.axis_index("ctx") < GROUP, lax.axis_index("head") == 0
+    return jnp.where(
+        first_group,
+        jnp.where(first_core, SHARES[0][0][k], SHARES[0][1][k]),
+        jnp.where(first_core, SHARES[1][0][k], SHARES[1][1][k]),
+    )
 
 
 def intra_groups(stage, features, b_input, c_input, cum_ref, step_ref, columns, wide_row, out):
-    start, stop = (jnp.where(is_late(), SHARES[0][k], SHARES[1][k]) for k in (stage, stage + 1))
+    start, stop = share_bound(stage), share_bound(stage + 1)
     heads, span = cum_ref.shape
     at_once = 128 // HEAD_DIM
     t, s = iota((span, span), 0), iota((span, span), 1)
@@ -180,15 +193,36 @@
 
 
 def first_kernel(
-    features, b_input, c_input, cum_ref, step_ref, rows, skip, norm, weight, _0, _1, _2, columns, wide_row, out, suffix
+    features,
+    b_input,
+    c_input,
+    cum_ref,
+    step_ref,
+    rows,
+    skip,
+    norm,
+    weight,
+    token,
+    _0,
+    _1,
+    _2,
+    columns,
+    wide_row,
+    out,
+    suffix,
+    own_piece,
 ):
-    @pl.when(jnp.logical_not(is_late()))
+    span = cum_ref.shape[1]
+    write_pieces(
+        (0,), token, features, b_input, cum_ref[:, span - 1 :], rows[3:4, 0:1], rows[4:5, 0:1], (own_piece,)
+    )
+
+    @pl.when(share_bound(1) == 0)
     def _():
         prepare(cum_ref, skip, norm, weight, columns, wide_row)
 
     intra_groups(1, features, b_input, c_input, cum_ref, step_ref, columns, wide_row, out)
 
-    span = cum_ref.shape[1]
     t, s = iota((span, span), 0), iota((span, span), 1)
     live, through, before = rows[0:1, :], rows[1:2, :], rows[2:3, :]
     reach = jnp.where((t >= s) & (column(before) == before), column(live), 0.0)
@@ -235,7 +269,7 @@
 def total_kernel(*refs):
     pieces, out = refs[:GROUP], refs[-1]
 
-    @each_place
+    @functools.partial(each_place, FIRST_ORDERS)
     def _(me, first, last):
         members = [parts_of(pieces[slot]) for slot in first]
         states, decays, keeps, _ = members[0]
@@ -266,14 +300,14 @@
         write_piece(total_out, carry_on(mine[0], theirs), decays, keeps, mine[3] + mine[2] * theirs[3])
 
 
-def entering_kernel(bit, has_got, has_past, *refs):
+def entering_kernel(bit, orders, has_got, has_past, *refs):
     pieces, refs = refs[:GROUP], refs[GROUP:]
     got, refs = (refs[0], refs[1:]) if has_got else (None, refs)
     past, refs = (refs[0], refs[1:]) if has_past else (None, refs)
     outs, carry_out = refs[-GROUP - 1 : -1], refs[-1]
     is_later = lax.rem(lax.axis_index("ctx") // GROUP // bit, 2) == 1
 
-    @each_place
+    @functools.partial(each_place, orders)
     def _(me, first, last):
         members = [parts_of(pieces[slot]) for slot in first]
         size = members[0][0][0].shape
@@ -300,22 +334,23 @@
         carry_out[...] = jnp.where(row == 0, amount, keeps)
 
 
-def readout_kernel(*refs):
-    entering, (c_input, columns, inside, wide_row, out) = refs[:GROUP], refs[GROUP:]
+def readout_kernel(orders, slots, *refs):
+    entering, (c_input, columns, inside, wide_row), refs = refs[: len(slots)], refs[len(slots) :][:4], refs[len(slots) + 4 :]
+    out = refs[-1]
     span, state = c_input.shape
+    wide = wide_row.shape[1] // GROUP
     heads = wide_row.shape[1] // HEAD_DIM
-    wide = wide_row.shape[1] // GROUP
-    queries = c_input[...]
+    queries = jnp.concatenate([c_input[...]] * 2, axis=1)
     by_token = columns[:, 128:]
     squares = jnp.zeros((span, 128), jnp.float32)
     values = jnp.zeros((span, 128), jnp.float32)
-    for j in range(GROUP):
-        part = partner_index(LAST_ORDERS, j)
+    for slot, piece in zip(slots, entering):
+        part = partner_index(orders, slot)
         lanes = pl.ds(pl.multiple_of(part * wide, wide), wide)
-        value = jnp.concatenate([entering[j][:state, :], entering[j][state:, :]], axis=1)
+        value = jnp.concatenate([piece[:state, :], piece[state:, :]], axis=1)
         high = value.astype(jnp.bfloat16)
         low = (value - high.astype(jnp.float32)).astype(jnp.bfloat16)
-        carried = dot(queries, high) + dot(queries, low)
+        carried = dot(queries, jnp.concatenate([high, low], axis=0))
         decay = dot(by_token, selector(heads, 128, part * (heads // GROUP), wide))
         mixed = inside[:, lanes] + carried * decay
         readout = wide_row[0:1, lanes]
@@ -323,8 +358,12 @@
         for k in range(0, wide, 128):
             squares = squares + squared[:, k : k + 128]
             values = values + read[:, k : k + 128]
-    out[0:1, :] = jnp.sum(squares.T, axis=0, keepdims=True)
-    out[1:2, :] = jnp.sum(values.T, axis=0, keepdims=True)
+    squares = jnp.sum(squares.T, axis=0, keepdims=True)
+    values = jnp.sum(values.T, axis=0, keepdims=True)
+    if len(refs) > 1:
+        squares, values = squares + refs[0][0:1, :], values + refs[0][1:2, :]
+    out[0:1, :] = squares
+    out[1:2, :] = values
 
 
 def last_kernel(channels, first_group_early, mine, other, suffix, carry, got, values_out, advantages_out, values, advantages, sems):
@@ -371,10 +410,14 @@
     cores = lax.axis_size("head")
     assert cores == len(orders)
     pairs = [
-        [(k * cores + core, (k ^ orders[core][slot]) * cores + core) for k in range(lax.axis_size("ctx")) for core in range(cores)]
+        [
+            (k * cores + core, (k ^ orders[core][slot]) * cores + core)
+            for k in range(lax.axis_size("ctx"))
+            for core in range(cores)
+        ]
         for slot in range(1, GROUP)
     ]
-    return [pieces[0]] + [lax.ppermute(piece, ("ctx", "head"), pair) for piece, pair in zip(pieces[1:], pairs)]
+    return [lax.ppermute(piece, ("ctx", "head"), pair) for piece, pair in zip(pieces, pairs)]
 
 
 def local(
@@ -404,7 +447,7 @@
 
     made = call(
         state_kernel,
-        [piece] * GROUP
+        [piece] * (GROUP - 1)
         + [
             ((span, width), bf16),
             ((span, state), bf16),
@@ -415,6 +458,7 @@
             ((1, heads), f32),
             ((1, width), f32),
             ((1, width), f32),
+            ((span, 128), f32),
             columns_shape,
             wide_shape,
             inside_shape,
@@ -441,15 +485,16 @@
             pltpu.SemaphoreType.DMA((11,)),
         ],
     )
-    pieces, made = made[:GROUP], made[GROUP:]
-    got = swap_slots(FIRST_ORDERS, pieces)
-    columns, wide_row, inside, suffix = call(
+    pieces, made = made[: GROUP - 1], made[GROUP - 1 :]
+    moved = swap_slots(FIRST_ORDERS, pieces)
+    columns, wide_row, inside, suffix, own_piece = call(
         first_kernel,
-        [columns_shape, wide_shape, inside_shape, ((8, span), f32)],
+        [columns_shape, wide_shape, inside_shape, ((8, span), f32), piece],
         "inside_first",
         *made,
-        aliases={9: 0, 10: 1, 11: 2},
-    )
+        aliases={10: 0, 11: 1, 12: 2},
+    )
+    got = [own_piece, *moved]
     near = (*made[:5], columns, wide_row)
     queries = made[2]
     (total,) = call(total_kernel, [piece], "group_total", *got, suffix)
@@ -468,17 +513,30 @@
     (inside,) = call(second_kernel, [inside_shape], "inside_second", *near, inside, aliases={len(near): 0})
 
     def finish(has_got):
+        orders = LAST_ORDERS if has_got else EARLY_ORDERS
         operands = (*got, *([other] if has_got else []), *([] if past is None else [past]))
         made = call(
-            functools.partial(entering_kernel, bit, has_got, past is not None),
+            functools.partial(entering_kernel, bit, orders, has_got, past is not None),
             [states] * GROUP + [((8, LANES), f32)],
             "entering_states",
             *operands,
             *([] if past is None else [inside]),
         )
-        arrived = swap_slots(LAST_ORDERS, made[:GROUP])
-        (sums,) = call(readout_kernel, [((2, span), f32)], "readout", *arrived, queries, columns, inside, wide_row)
-        return sums, made[GROUP]
+        arrived = [made[0], *swap_slots(orders, made[1:GROUP])]
+        sums = ()
+        for slots in READOUTS:
+            sums = call(
+                functools.partial(readout_kernel, orders, slots),
+                [((2, span), f32)],
+                "readout",
+                *(arrived[slot] for slot in slots),
+                queries,
+                columns,
+                inside,
+                wide_row,
+                *sums,
+            )
+        return sums[0], made[GROUP]
 
     first_group_early = groups == 2
     if first_group_early:

time: 31.4 us -> 30.2 us (0.962)
  the two profiles are of different devices: /device:TPU:21 before, /device:TPU:17 now
where the time goes in v5:
time: 30.2 us; the launch traced here: 30.1 us
  waiting for transfers between devices  10.3 us (34%)
  starting transfers between devices  10.2 us (34%)
  Pallas kernels  8.85 us (29%)
  between operations  0.71 us (2%)
    pallas_call x7, Pallas kernels, call(): pl.pallas_call(kernel, out_shape=[jax.ShapeDtypeStruct(*shape) for shape...  8.85 us
    ppermute x6, waiting for transfers between devices, swap_slots(): lax.ppermute(piece, ('ctx', 'head'), pair)  6.07 us
    ppermute x6, starting transfers between devices, swap_slots(): lax.ppermute(piece, ('ctx', 'head'), pair)  5.43 us
    ppermute x2, starting transfers between devices, swap(): return lax.ppermute(value, axis, [(k, k ^ mask) for k in range(count)])  4.76 us
    ppermute x2, waiting for transfers between devices, swap(): return lax.ppermute(value, axis, [(k, k ^ mask) for k in range(count)])  4.22 us
  transfers between devices with their start and end apart: 8, of which 6 were waited for; matrix products, arithmetic and copies ran while one was open for 0% of the time, Pallas kernels for 18%

profile of v5, /device:TPU:17, one launch (start us, length us, event | category | flops | bytes accessed | tf_op | source)
XLA Modules:
  0.0 30.1 jit_solution(6644989975024795060)
XLA Ops:
  0.6 2.1 %block_states.1 = (f32[264,128]{1,0:T(8,128)S(1)}, f32[264,128]{1,0:T(8,128)S(1)}, f32[264,128]{1,0:T(8,128)S(1)}, bf16[256,1024]{1,0:T(8,128)(2,1)S(1)}, bf16[2...) custom-call(f32[32,256]{1,0:T(8,128)} %refs_0_.1, ...), custom_call_target="tpu_custom_call" | custom-call | tf_op jit(solution)/shard_map/block_states/pallas_call | solution.py:392
  2.7 1.4 %collective-permute-start.6 = (f32[264,128]{1,0:T(8,128)S(1)}, f32[264,128]{1,0:T(8,128)S(1)}, u32[]{:S(2)}, u32[]{:S(2)}) collective-permute-start(f32[264,128]{1,0:T(8,128)S(1)} %get-tuple-element.106), channel_id=1, source_target_pairs={{0,2},{1,5},{2,0},{3,7},{4,6},{5,1},{6,4},{7,3},{8,10},{9,13},{10,... | collective-permute-start | bytes 405512 | tf_op jit(solution)/shard_map/ppermute | solution.py:420
  4.1 1.2 %collective-permute-start.7 = (f32[264,128]{1,0:T(8,128)S(1)}, f32[264,128]{1,0:T(8,128)S(1)}, u32[]{:S(2)}, u32[]{:S(2)}) collective-permute-start(f32[264,128]{1,0:T(8,128)S(1)} %get-tuple-element.107), channel_id=1, source_target_pairs={{0,4},{1,3},{2,6},{3,1},{4,0},{5,7},{6,2},{7,5},{8,12},{9,11},{10,... | collective-permute-start | bytes 405512 | tf_op jit(solution)/shard_map/ppermute | solution.py:420
  5.3 0.1 collective-permute-start.8
  5.4 4.1 %inside_first.1 = (bf16[256,256]{1,0:T(8,128)(2,1)S(1)}, f32[2,1024]{1,0:T(2,128)S(1)}, f32[256,1024]{1,0:T(8,128)S(1)}, f32[8,256]{1,0:T(8,128)S(1)}, f32[264,128]{1,0:T(8,128)S(1)}) custom-call(bf16[256,1024]{1,0:T(8,128)(2,1)S(1)} %get-tuple-element.92.features, ...), custom_call_target="tpu_custom_call", output_to_operand_aliasing={{0}: (10, {}), {1}: (11, {}), {2}: (12, {})} | custom-call | tf_op jit(solution)/shard_map/inside_first/pallas_call | solution.py:392
  9.6 0.0 collective-permute-done.6.refs_1_
  9.6 0.0 collective-permute-done.7.refs_2_
  9.6 2.2 %collective-permute-done.8.refs_3_ = f32[264,128]{1,0:T(8,128)S(1)} collective-permute-done((f32[264,128]{1,0:T(8,128)S(1)}, f32[264,128]{1,0:T(8,128)S(1)}, u32[]{:S(2)}, u32[]{:S(2)}) %collective-permute-start.8) | collective-permute-done | bytes 135200 | tf_op jit(solution)/shard_map/ppermute | solution.py:420
  11.8 0.1 group_total.1
  11.9 0.1 collective-permute-start.9
  11.9 1.3 %inside_second.1 = f32[256,1024]{1,0:T(8,128)S(1)} custom-call(bf16[256,1024]{1,0:T(8,128)(2,1)S(1)} %get-tuple-element.92.features, bf16[256,128]{1,0:T(8,128)(2,1)S(1)} %get-tuple-element.93.b_input, bf16[256,128]{1,0:T(8,128)(2,1)S(1)} %get-tuple-element.94.c_input, f32[32,256]{1,0:T(8,128)S(1)} %get-tuple-element.95.cum_ref, ...), custom_call_target="tpu_custom_call", output_to_operand_aliasing={{}: (7, {})} | custom-call | tf_op jit(solution)/shard_map/inside_second/pallas_call | solution.py:392
  13.3 3.4 %collective-permute-done.9.got = f32[264,128]{1,0:T(8,128)S(1)} collective-permute-done((f32[264,128]{1,0:T(8,128)S(1)}, f32[264,128]{1,0:T(8,128)S(1)}, u32[]{:S(2)}, u32[]{:S(2)}) %collective-permute-start.9) | collective-permute-done | bytes 135200 | tf_op jit(solution)/shard_map/ppermute | solution.py:406
  16.7 7.2 %conditional.3 = (f32[2,256]{1,0:T(2,128)S(1)}, f32[8,128]{1,0:T(8,128)S(1)}) conditional(s32[]{:T(128)} %convert_element_type.4, (f32[264,128]{1,0:T(8,128)S(1)}, f32[264,128]{1,0:T(8,128)S(1)}, f32[264,128]{1,0:T(8,128)S(1)}, f32[264,128]{1,0:T(8,128)S(1)}, f32[264,128]{1,0:T(8,128)S(1)}, /*index=5*/bf16[256,128]{1,0:T(8,128)(2,1)S(1)}, ...), branch_computations={%region_2.0_spmd, %region_3.0_spmd} | conditional | bytes 1573000 | solution.py:546
  16.7 0.1 entering_states.3
  16.8 0.2 collective-permute-start.3
  16.9 1.7 %collective-permute-start.4 = (f32[256,128]{1,0:T(8,128)S(1)}, f32[256,128]{1,0:T(8,128)S(1)}, u32[]{:S(2)}, u32[]{:S(2)}) collective-permute-start(f32[256,128]{1,0:T(8,128)S(1)} %get-tuple-element.58), channel_id=1, source_target_pairs={{0,2},{1,5},{2,0},{3,7},{4,6},{5,1},{6,4},{7,3},{8,10},{9,13},{10,... | collective-permute-start | bytes 393224 | tf_op jit(solution)/shard_map/cond/branch_0_fun/ppermute | solution.py:420
  18.6 0.9 %collective-permute-start.5 = (f32[256,128]{1,0:T(8,128)S(1)}, f32[256,128]{1,0:T(8,128)S(1)}, u32[]{:S(2)}, u32[]{:S(2)}) collective-permute-start(f32[256,128]{1,0:T(8,128)S(1)} %get-tuple-element.59), channel_id=1, source_target_pairs={{0,4},{1,7},{2,6},{3,5},{4,0},{5,3},{6,2},{7,1},{8,12},{9,15},{10,... | collective-permute-start | bytes 393224 | tf_op jit(solution)/shard_map/cond/branch_0_fun/ppermute | solution.py:420
  19.5 1.2 %collective-permute-done.3.refs_1_ = f32[256,128]{1,0:T(8,128)S(1)} collective-permute-done((f32[256,128]{1,0:T(8,128)S(1)}, f32[256,128]{1,0:T(8,128)S(1)}, u32[]{:S(2)}, u32[]{:S(2)}) %collective-permute-start.3) | collective-permute-done | bytes 131104 | tf_op jit(solution)/shard_map/cond/branch_0_fun/ppermute | solution.py:420
  20.6 0.3 %collective-permute-done.4.refs_2_ = f32[256,128]{1,0:T(8,128)S(1)} collective-permute-done((f32[256,128]{1,0:T(8,128)S(1)}, f32[256,128]{1,0:T(8,128)S(1)}, u32[]{:S(2)}, u32[]{:S(2)}) %collective-permute-start.4) | collective-permute-done | bytes 131104 | tf_op jit(solution)/shard_map/cond/branch_0_fun/ppermute | solution.py:420
  21.0 2.4 %collective-permute-done.5.refs_3_ = f32[256,128]{1,0:T(8,128)S(1)} collective-permute-done((f32[256,128]{1,0:T(8,128)S(1)}, f32[256,128]{1,0:T(8,128)S(1)}, u32[]{:S(2)}, u32[]{:S(2)}) %collective-permute-start.5) | collective-permute-done | bytes 131104 | tf_op jit(solution)/shard_map/cond/branch_0_fun/ppermute | solution.py:420
  23.3 0.6 %readout.3 = f32[2,256]{1,0:T(2,128)S(1)} custom-call(f32[256,128]{1,0:T(8,128)S(1)} %get-tuple-element.56.refs_0_, f32[256,128]{1,0:T(8,128)S(1)} %collective-permute-done.3.refs_1_, f32[256,128]{1,0:T(8,128)S(1)} %collective-permute-done.4.refs_2_, f32[256,128]{1,0:T(8,128)S(1)} %collective-permute-done.5.refs_3_, ...), custom_call_target="tpu_custom_call" | custom-call | tf_op jit(solution)/shard_map/cond/branch_0_fun/readout/pallas_call | solution.py:392
  23.9 4.7 %collective-permute-start.10 = (f32[2,256]{1,0:T(2,128)S(1)}, f32[2,256]{1,0:T(2,128)S(1)}, u32[]{:S(2)}, u32[]{:S(2)}) collective-permute-start(f32[2,256]{1,0:T(2,128)S(1)} %get-tuple-element.113.mine), channel_id=1, source_target_pairs={{0,1},{1,0},{2,3},{3,2},{4,5},{5,4},{6,7},{7,6},{8,9},{9,8},{10,11... | collective-permute-start | bytes 6152 | tf_op jit(solution)/shard_map/ppermute | solution.py:406
  28.6 0.8 %collective-permute-done.10.other = f32[2,256]{1,0:T(2,128)S(1)} collective-permute-done((f32[2,256]{1,0:T(2,128)S(1)}, f32[2,256]{1,0:T(2,128)S(1)}, u32[]{:S(2)}, u32[]{:S(2)}) %collective-permute-start.10) | collective-permute-done | bytes 2080 | tf_op jit(solution)/shard_map/ppermute | solution.py:406
  29.4 0.7 %values_and_advantages.1 = (f32[1,256]{1,0:T(1,128)}, f32[1,256]{1,0:T(1,128)}) custom-call(f32[2,256]{1,0:T(2,128)S(1)} %get-tuple-element.113.mine, f32[2,256]{1,0:T(2,128)S(1)} %collective-permute-done.10.other, f32[8,256]{1,0:T(8,128)S(1)} %get-tuple-element.109.refs_4_.suffix, f32[8,128]{1,0:T(8,128)S(1)} %get-tuple-element.114.carry, ...), custom_call_target="tpu_custom_call" | custom-call | tf_op jit(solution)/shard_map/values_and_advantages/pallas_call | solution.py:392
  (3 shorter events, 0.0 us)
Async XLA Ops:
  2.7 6.9 %collective-permute-start.6 = (f32[264,128]{1,0:T(8,128)S(1)}, f32[264,128]{1,0:T(8,128)S(1)}, u32[]{:S(2)}, u32[]{:S(2)}) collective-permute-start(f32[264,128]{1,0:T(8,128)S(1)} %get-tuple-element.106), channel_id=1, source_target_pairs={{0,2},{1,5},{2,0},{3,7},{4,6},{5,1},{6,4},{7,3},{8,10},{9,13},{10,... | collective-permute-start | bytes 405512 | tf_op jit(solution)/shard_map/ppermute | solution.py:420
  4.1 5.5 %collective-permute-start.7 = (f32[264,128]{1,0:T(8,128)S(1)}, f32[264,128]{1,0:T(8,128)S(1)}, u32[]{:S(2)}, u32[]{:S(2)}) collective-permute-start(f32[264,128]{1,0:T(8,128)S(1)} %get-tuple-element.107), channel_id=1, source_target_pairs={{0,4},{1,3},{2,6},{3,1},{4,0},{5,7},{6,2},{7,5},{8,12},{9,11},{10,... | collective-permute-start | bytes 405512 | tf_op jit(solution)/shard_map/ppermute | solution.py:420
  5.3 6.5 %collective-permute-start.8 = (f32[264,128]{1,0:T(8,128)S(1)}, f32[264,128]{1,0:T(8,128)S(1)}, u32[]{:S(2)}, u32[]{:S(2)}) collective-permute-start(f32[264,128]{1,0:T(8,128)S(1)} %get-tuple-element.108), channel_id=1, source_target_pairs={{0,6},{1,7},{2,4},{3,5},{4,2},{5,3},{6,0},{7,1},{8,14},{9,15},{10,... | collective-permute-start | bytes 405512 | tf_op jit(solution)/shard_map/ppermute | solution.py:420
  11.9 4.8 %collective-permute-start.9 = (f32[264,128]{1,0:T(8,128)S(1)}, f32[264,128]{1,0:T(8,128)S(1)}, u32[]{:S(2)}, u32[]{:S(2)}) collective-permute-start(f32[264,128]{1,0:T(8,128)S(1)} %group_total.1), channel_id=1, source_target_pairs={{0,8},{2,10},{4,12},{6,14},{8,0},{10,2},{12,4},{14,6},{1,9},{3,11}... | collective-permute-start | bytes 405512 | tf_op jit(solution)/shard_map/ppermute | solution.py:406
  16.8 3.9 %collective-permute-start.3 = (f32[256,128]{1,0:T(8,128)S(1)}, f32[256,128]{1,0:T(8,128)S(1)}, u32[]{:S(2)}, u32[]{:S(2)}) collective-permute-start(f32[256,128]{1,0:T(8,128)S(1)} %get-tuple-element.57), channel_id=1, source_target_pairs={{0,6},{1,3},{2,4},{3,1},{4,2},{5,7},{6,0},{7,5},{8,14},{9,11},{10,... | collective-permute-start | bytes 393224 | tf_op jit(solution)/shard_map/cond/branch_0_fun/ppermute | solution.py:420
  16.9 4.1 %collective-permute-start.4 = (f32[256,128]{1,0:T(8,128)S(1)}, f32[256,128]{1,0:T(8,128)S(1)}, u32[]{:S(2)}, u32[]{:S(2)}) collective-permute-start(f32[256,128]{1,0:T(8,128)S(1)} %get-tuple-element.58), channel_id=1, source_target_pairs={{0,2},{1,5},{2,0},{3,7},{4,6},{5,1},{6,4},{7,3},{8,10},{9,13},{10,... | collective-permute-start | bytes 393224 | tf_op jit(solution)/shard_map/cond/branch_0_fun/ppermute | solution.py:420
  18.6 4.7 %collective-permute-start.5 = (f32[256,128]{1,0:T(8,128)S(1)}, f32[256,128]{1,0:T(8,128)S(1)}, u32[]{:S(2)}, u32[]{:S(2)}) collective-permute-start(f32[256,128]{1,0:T(8,128)S(1)} %get-tuple-element.59), channel_id=1, source_target_pairs={{0,4},{1,7},{2,6},{3,5},{4,0},{5,3},{6,2},{7,1},{8,12},{9,15},{10,... | collective-permute-start | bytes 393224 | tf_op jit(solution)/shard_map/cond/branch_0_fun/ppermute | solution.py:420
  23.9 5.5 %collective-permute-start.10 = (f32[2,256]{1,0:T(2,128)S(1)}, f32[2,256]{1,0:T(2,128)S(1)}, u32[]{:S(2)}, u32[]{:S(2)}) collective-permute-start(f32[2,256]{1,0:T(2,128)S(1)} %get-tuple-element.113.mine), channel_id=1, source_target_pairs={{0,1},{1,0},{2,3},{3,2},{4,5},{5,4},{6,7},{7,6},{8,9},{9,8},{10,11... | collective-permute-start | bytes 6152 | tf_op jit(solution)/shard_map/ppermute | solution.py:406

commit v6 on v5

--- a/solution.py
+++ b/solution.py
@@ -266,7 +266,7 @@
     return [one + other for one, other in zip(first, second)]
 
 
-def total_kernel(*refs):
+def total_kernel(two_groups, *refs):
     pieces, out = refs[:GROUP], refs[-1]
 
     @functools.partial(each_place, FIRST_ORDERS)
@@ -280,7 +280,18 @@
         amount = members[-1][3]
         for member in members[-2::-1]:
             amount = member[3] + member[2] * amount
-        write_piece(out, states, decays, keeps, amount)
+        if not two_groups:
+            write_piece(out, states, decays, keeps, amount)
+            return
+
+        @pl.when(lax.axis_index("ctx") < GROUP)
+        def _():
+            for k, state in enumerate(states):
+                out[k * state.shape[0] : (k + 1) * state.shape[0], :] = state
+
+        @pl.when(lax.axis_index("ctx") >= GROUP)
+        def _():
+            out[:EXTRA, :] = jnp.broadcast_to(amount, (EXTRA, LANES))
 
 
 def round_kernel(bit, *refs):
@@ -313,7 +324,9 @@
         size = members[0][0][0].shape
         arriving = [jnp.zeros(size, jnp.float32)] * 2
         keeps, amount = jnp.ones((1, LANES), jnp.float32), jnp.zeros((1, LANES), jnp.float32)
-        if has_got:
+        if has_got and got.shape[0] == 2 * size[0]:
+            arriving = [got[: size[0], :], got[size[0] :, :]]
+        elif has_got:
             theirs = parts_of(got)
             arriving = [jnp.where(is_later, state, 0.0) for state in theirs[0]]
             keeps = jnp.where(is_later, keeps, theirs[2])
@@ -372,7 +385,7 @@
     values[...] = value
     amount = carry[0:1, 0:1]
     if first_group_early:
-        later = jnp.where(lax.axis_index("ctx") < GROUP, parts_of(got)[3][:, 0:1], 0.0)
+        later = jnp.where(lax.axis_index("ctx") < GROUP, got[0:1, 0:1], 0.0)
         amount = amount + carry[1:2, 0:1] * later
     advantages[...] = suffix[0:1, :] + suffix[1:2, :] * amount - value
     copies = [
@@ -497,7 +510,13 @@
     got = [own_piece, *moved]
     near = (*made[:5], columns, wide_row)
     queries = made[2]
-    (total,) = call(total_kernel, [piece], "group_total", *got, suffix)
+    (total,) = call(
+        functools.partial(total_kernel, groups == 2),
+        [states if groups == 2 else piece],
+        "group_total",
+        *got,
+        suffix,
+    )
     past = None
     bit = 1
     while bit * 2 < groups:

time: 30.2 us -> 30.1 us (level)
  no operation moved by 1% of the time
where the time goes in v6:
time: 30.1 us; the launch traced here: 30 us
  starting transfers between devices  10.2 us (34%)
  waiting for transfers between devices  10.2 us (34%)
  Pallas kernels  8.84 us (29%)
  between operations  0.71 us (2%)
    pallas_call x7, Pallas kernels, call(): pl.pallas_call(kernel, out_shape=[jax.ShapeDtypeStruct(*shape) for shape...  8.84 us
    ppermute x6, waiting for transfers between devices, swap_slots(): lax.ppermute(piece, ('ctx', 'head'), pair)  6.02 us
    ppermute x6, starting transfers between devices, swap_slots(): lax.ppermute(piece, ('ctx', 'head'), pair)  5.43 us
    ppermute x2, starting transfers between devices, swap(): return lax.ppermute(value, axis, [(k, k ^ mask) for k in range(count)])  4.75 us
    ppermute x2, waiting for transfers between devices, swap(): return lax.ppermute(value, axis, [(k, k ^ mask) for k in range(count)])  4.18 us
  transfers between devices with their start and end apart: 8, of which 6 were waited for; matrix products, arithmetic and copies ran while one was open for 0% of the time, Pallas kernels for 18%

profile of v6, /device:TPU:17, one launch (start us, length us, event | category | flops | bytes accessed | tf_op | source)
XLA Modules:
  0.0 30.0 jit_solution(9711210963523219406)
XLA Ops:
  0.6 2.1 %block_states.1 = (f32[264,128]{1,0:T(8,128)S(1)}, f32[264,128]{1,0:T(8,128)S(1)}, f32[264,128]{1,0:T(8,128)S(1)}, bf16[256,1024]{1,0:T(8,128)(2,1)S(1)}, bf16[2...) custom-call(f32[32,256]{1,0:T(8,128)} %refs_0_.1, ...), custom_call_target="tpu_custom_call" | custom-call | tf_op jit(solution)/shard_map/block_states/pallas_call | solution.py:405
  2.7 1.4 %collective-permute-start.6 = (f32[264,128]{1,0:T(8,128)S(1)}, f32[264,128]{1,0:T(8,128)S(1)}, u32[]{:S(2)}, u32[]{:S(2)}) collective-permute-start(f32[264,128]{1,0:T(8,128)S(1)} %get-tuple-element.106), channel_id=1, source_target_pairs={{0,2},{1,5},{2,0},{3,7},{4,6},{5,1},{6,4},{7,3},{8,10},{9,13},{10,... | collective-permute-start | bytes 405512 | tf_op jit(solution)/shard_map/ppermute | solution.py:433
  4.1 1.2 %collective-permute-start.7 = (f32[264,128]{1,0:T(8,128)S(1)}, f32[264,128]{1,0:T(8,128)S(1)}, u32[]{:S(2)}, u32[]{:S(2)}) collective-permute-start(f32[264,128]{1,0:T(8,128)S(1)} %get-tuple-element.107), channel_id=1, source_target_pairs={{0,4},{1,3},{2,6},{3,1},{4,0},{5,7},{6,2},{7,5},{8,12},{9,11},{10,... | collective-permute-start | bytes 405512 | tf_op jit(solution)/shard_map/ppermute | solution.py:433
  5.3 0.1 collective-permute-start.8
  5.4 4.1 %inside_first.1 = (bf16[256,256]{1,0:T(8,128)(2,1)S(1)}, f32[2,1024]{1,0:T(2,128)S(1)}, f32[256,1024]{1,0:T(8,128)S(1)}, f32[8,256]{1,0:T(8,128)S(1)}, f32[264,128]{1,0:T(8,128)S(1)}) custom-call(bf16[256,1024]{1,0:T(8,128)(2,1)S(1)} %get-tuple-element.92.features, ...), custom_call_target="tpu_custom_call", output_to_operand_aliasing={{0}: (10, {}), {1}: (11, {}), {2}: (12, {})} | custom-call | tf_op jit(solution)/shard_map/inside_first/pallas_call | solution.py:405
  9.6 0.0 collective-permute-done.6.refs_1_
  9.6 0.0 collective-permute-done.7.refs_2_
  9.6 2.2 %collective-permute-done.8.refs_3_ = f32[264,128]{1,0:T(8,128)S(1)} collective-permute-done((f32[264,128]{1,0:T(8,128)S(1)}, f32[264,128]{1,0:T(8,128)S(1)}, u32[]{:S(2)}, u32[]{:S(2)}) %collective-permute-start.8) | collective-permute-done | bytes 135200 | tf_op jit(solution)/shard_map/ppermute | solution.py:433
  11.8 0.1 group_total.1
  11.9 0.1 collective-permute-start.9
  11.9 1.3 %inside_second.1 = f32[256,1024]{1,0:T(8,128)S(1)} custom-call(bf16[256,1024]{1,0:T(8,128)(2,1)S(1)} %get-tuple-element.92.features, bf16[256,128]{1,0:T(8,128)(2,1)S(1)} %get-tuple-element.93.b_input, bf16[256,128]{1,0:T(8,128)(2,1)S(1)} %get-tuple-element.94.c_input, f32[32,256]{1,0:T(8,128)S(1)} %get-tuple-element.95.cum_ref, ...), custom_call_target="tpu_custom_call", output_to_operand_aliasing={{}: (7, {})} | custom-call | tf_op jit(solution)/shard_map/inside_second/pallas_call | solution.py:405
  13.3 3.4 %collective-permute-done.9.got = f32[256,128]{1,0:T(8,128)S(1)} collective-permute-done((f32[256,128]{1,0:T(8,128)S(1)}, f32[256,128]{1,0:T(8,128)S(1)}, u32[]{:S(2)}, u32[]{:S(2)}) %collective-permute-start.9) | collective-permute-done | bytes 131104 | tf_op jit(solution)/shard_map/ppermute | solution.py:419
  16.6 7.2 %conditional.3 = (f32[2,256]{1,0:T(2,128)S(1)}, f32[8,128]{1,0:T(8,128)S(1)}) conditional(s32[]{:T(128)} %convert_element_type.4, (f32[264,128]{1,0:T(8,128)S(1)}, f32[264,128]{1,0:T(8,128)S(1)}, f32[264,128]{1,0:T(8,128)S(1)}, f32[264,128]{1,0:T(8,128)S(1)}, f32[256,128]{1,0:T(8,128)S(1)}, /*index=5*/bf16[256,128]{1,0:T(8,128)(2,1)S(1)}, ...), branch_computations={%region_2.0_spmd, %region_3.0_spmd} | conditional | bytes 1573000 | solution.py:565
  16.6 0.1 entering_states.3
  16.7 0.2 collective-permute-start.3
  16.9 1.7 %collective-permute-start.4 = (f32[256,128]{1,0:T(8,128)S(1)}, f32[256,128]{1,0:T(8,128)S(1)}, u32[]{:S(2)}, u32[]{:S(2)}) collective-permute-start(f32[256,128]{1,0:T(8,128)S(1)} %get-tuple-element.58), channel_id=1, source_target_pairs={{0,2},{1,5},{2,0},{3,7},{4,6},{5,1},{6,4},{7,3},{8,10},{9,13},{10,... | collective-permute-start | bytes 393224 | tf_op jit(solution)/shard_map/cond/branch_0_fun/ppermute | solution.py:433
  18.5 0.9 %collective-permute-start.5 = (f32[256,128]{1,0:T(8,128)S(1)}, f32[256,128]{1,0:T(8,128)S(1)}, u32[]{:S(2)}, u32[]{:S(2)}) collective-permute-start(f32[256,128]{1,0:T(8,128)S(1)} %get-tuple-element.59), channel_id=1, source_target_pairs={{0,4},{1,7},{2,6},{3,5},{4,0},{5,3},{6,2},{7,1},{8,12},{9,15},{10,... | collective-permute-start | bytes 393224 | tf_op jit(solution)/shard_map/cond/branch_0_fun/ppermute | solution.py:433
  19.4 1.2 %collective-permute-done.3.refs_1_ = f32[256,128]{1,0:T(8,128)S(1)} collective-permute-done((f32[256,128]{1,0:T(8,128)S(1)}, f32[256,128]{1,0:T(8,128)S(1)}, u32[]{:S(2)}, u32[]{:S(2)}) %collective-permute-start.3) | collective-permute-done | bytes 131104 | tf_op jit(solution)/shard_map/cond/branch_0_fun/ppermute | solution.py:433
  20.6 0.3 collective-permute-done.4.refs_2_
  20.9 2.4 %collective-permute-done.5.refs_3_ = f32[256,128]{1,0:T(8,128)S(1)} collective-permute-done((f32[256,128]{1,0:T(8,128)S(1)}, f32[256,128]{1,0:T(8,128)S(1)}, u32[]{:S(2)}, u32[]{:S(2)}) %collective-permute-start.5) | collective-permute-done | bytes 131104 | tf_op jit(solution)/shard_map/cond/branch_0_fun/ppermute | solution.py:433
  23.2 0.6 %readout.3 = f32[2,256]{1,0:T(2,128)S(1)} custom-call(f32[256,128]{1,0:T(8,128)S(1)} %get-tuple-element.56.refs_0_, f32[256,128]{1,0:T(8,128)S(1)} %collective-permute-done.3.refs_1_, f32[256,128]{1,0:T(8,128)S(1)} %collective-permute-done.4.refs_2_, f32[256,128]{1,0:T(8,128)S(1)} %collective-permute-done.5.refs_3_, ...), custom_call_target="tpu_custom_call" | custom-call | tf_op jit(solution)/shard_map/cond/branch_0_fun/readout/pallas_call | solution.py:405
  23.8 4.7 %collective-permute-start.10 = (f32[2,256]{1,0:T(2,128)S(1)}, f32[2,256]{1,0:T(2,128)S(1)}, u32[]{:S(2)}, u32[]{:S(2)}) collective-permute-start(f32[2,256]{1,0:T(2,128)S(1)} %get-tuple-element.113.mine), channel_id=1, source_target_pairs={{0,1},{1,0},{2,3},{3,2},{4,5},{5,4},{6,7},{7,6},{8,9},{9,8},{10,11... | collective-permute-start | bytes 6152 | tf_op jit(solution)/shard_map/ppermute | solution.py:419
  28.5 0.8 %collective-permute-done.10.other = f32[2,256]{1,0:T(2,128)S(1)} collective-permute-done((f32[2,256]{1,0:T(2,128)S(1)}, f32[2,256]{1,0:T(2,128)S(1)}, u32[]{:S(2)}, u32[]{:S(2)}) %collective-permute-start.10) | collective-permute-done | bytes 2080 | tf_op jit(solution)/shard_map/ppermute | solution.py:419
  29.3 0.7 %values_and_advantages.1 = (f32[1,256]{1,0:T(1,128)}, f32[1,256]{1,0:T(1,128)}) custom-call(f32[2,256]{1,0:T(2,128)S(1)} %get-tuple-element.113.mine, f32[2,256]{1,0:T(2,128)S(1)} %collective-permute-done.10.other, f32[8,256]{1,0:T(8,128)S(1)} %get-tuple-element.109.refs_4_.suffix, f32[8,128]{1,0:T(8,128)S(1)} %get-tuple-element.114.carry, ...), custom_call_target="tpu_custom_call" | custom-call | tf_op jit(solution)/shard_map/values_and_advantages/pallas_call | solution.py:405
  (3 shorter events, 0.0 us)
Async XLA Ops:
  2.7 6.9 %collective-permute-start.6 = (f32[264,128]{1,0:T(8,128)S(1)}, f32[264,128]{1,0:T(8,128)S(1)}, u32[]{:S(2)}, u32[]{:S(2)}) collective-permute-start(f32[264,128]{1,0:T(8,128)S(1)} %get-tuple-element.106), channel_id=1, source_target_pairs={{0,2},{1,5},{2,0},{3,7},{4,6},{5,1},{6,4},{7,3},{8,10},{9,13},{10,... | collective-permute-start | bytes 405512 | tf_op jit(solution)/shard_map/ppermute | solution.py:433
  4.1 5.5 %collective-permute-start.7 = (f32[264,128]{1,0:T(8,128)S(1)}, f32[264,128]{1,0:T(8,128)S(1)}, u32[]{:S(2)}, u32[]{:S(2)}) collective-permute-start(f32[264,128]{1,0:T(8,128)S(1)} %get-tuple-element.107), channel_id=1, source_target_pairs={{0,4},{1,3},{2,6},{3,1},{4,0},{5,7},{6,2},{7,5},{8,12},{9,11},{10,... | collective-permute-start | bytes 405512 | tf_op jit(solution)/shard_map/ppermute | solution.py:433
  5.3 6.5 %collective-permute-start.8 = (f32[264,128]{1,0:T(8,128)S(1)}, f32[264,128]{1,0:T(8,128)S(1)}, u32[]{:S(2)}, u32[]{:S(2)}) collective-permute-start(f32[264,128]{1,0:T(8,128)S(1)} %get-tuple-element.108), channel_id=1, source_target_pairs={{0,6},{1,7},{2,4},{3,5},{4,2},{5,3},{6,0},{7,1},{8,14},{9,15},{10,... | collective-permute-start | bytes 405512 | tf_op jit(solution)/shard_map/ppermute | solution.py:433
  11.9 4.8 %collective-permute-start.9 = (f32[256,128]{1,0:T(8,128)S(1)}, f32[256,128]{1,0:T(8,128)S(1)}, u32[]{:S(2)}, u32[]{:S(2)}) collective-permute-start(f32[256,128]{1,0:T(8,128)S(1)} %group_total.1), channel_id=1, source_target_pairs={{0,8},{2,10},{4,12},{6,14},{8,0},{10,2},{12,4},{14,6},{1,9},{3,11}... | collective-permute-start | bytes 393224 | tf_op jit(solution)/shard_map/ppermute | solution.py:419
  16.7 3.9 %collective-permute-start.3 = (f32[256,128]{1,0:T(8,128)S(1)}, f32[256,128]{1,0:T(8,128)S(1)}, u32[]{:S(2)}, u32[]{:S(2)}) collective-permute-start(f32[256,128]{1,0:T(8,128)S(1)} %get-tuple-element.57), channel_id=1, source_target_pairs={{0,6},{1,3},{2,4},{3,1},{4,2},{5,7},{6,0},{7,5},{8,14},{9,11},{10,... | collective-permute-start | bytes 393224 | tf_op jit(solution)/shard_map/cond/branch_0_fun/ppermute | solution.py:433
  16.9 4.0 %collective-permute-start.4 = (f32[256,128]{1,0:T(8,128)S(1)}, f32[256,128]{1,0:T(8,128)S(1)}, u32[]{:S(2)}, u32[]{:S(2)}) collective-permute-start(f32[256,128]{1,0:T(8,128)S(1)} %get-tuple-element.58), channel_id=1, source_target_pairs={{0,2},{1,5},{2,0},{3,7},{4,6},{5,1},{6,4},{7,3},{8,10},{9,13},{10,... | collective-permute-start | bytes 393224 | tf_op jit(solution)/shard_map/cond/branch_0_fun/ppermute | solution.py:433
  18.5 4.7 %collective-permute-start.5 = (f32[256,128]{1,0:T(8,128)S(1)}, f32[256,128]{1,0:T(8,128)S(1)}, u32[]{:S(2)}, u32[]{:S(2)}) collective-permute-start(f32[256,128]{1,0:T(8,128)S(1)} %get-tuple-element.59), channel_id=1, source_target_pairs={{0,4},{1,7},{2,6},{3,5},{4,0},{5,3},{6,2},{7,1},{8,12},{9,15},{10,... | collective-permute-start | bytes 393224 | tf_op jit(solution)/shard_map/cond/branch_0_fun/ppermute | solution.py:433
  23.8 5.5 %collective-permute-start.10 = (f32[2,256]{1,0:T(2,128)S(1)}, f32[2,256]{1,0:T(2,128)S(1)}, u32[]{:S(2)}, u32[]{:S(2)}) collective-permute-start(f32[2,256]{1,0:T(2,128)S(1)} %get-tuple-element.113.mine), channel_id=1, source_target_pairs={{0,1},{1,0},{2,3},{3,2},{4,5},{5,4},{6,7},{7,6},{8,9},{9,8},{10,11... | collective-permute-start | bytes 6152 | tf_op jit(solution)/shard_map/ppermute | solution.py:419

commit v7 on v6

--- a/solution.py
+++ b/solution.py
@@ -87,17 +87,16 @@
     wide = features.shape[1] // GROUP
     row = iota((EXTRA, LANES), 0)
     by_token = token[...].astype(jnp.bfloat16)
-    for slot, out in zip(slots, outs):
-        part = partner_index(FIRST_ORDERS, slot)
-        first_head = part * (heads // GROUP)
-        feat = features[:, pl.ds(pl.multiple_of(part * wide, wide), wide)]
-        spread = dot(by_token, selector(heads, 128, first_head, wide))
-        scaled = (spread * feat.astype(jnp.float32)).astype(jnp.bfloat16)
-        states = dot(keys, scaled)
-        decay = over_channels(total, first_head, wide)
+    places = [partner_index(FIRST_ORDERS, slot) for slot in slots]
+    spread = [dot(by_token, selector(heads, 128, part * (heads // GROUP), wide)) for part in places]
+    feats = [features[:, pl.ds(pl.multiple_of(part * wide, wide), wide)] for part in places]
+    scaled = [(one * feat.astype(jnp.float32)).astype(jnp.bfloat16) for one, feat in zip(spread, feats)]
+    states = [dot(keys, one) for one in scaled]
+    for part, one, out in zip(places, states, outs):
+        decay = over_channels(total, part * (heads // GROUP), wide)
         extra = jnp.where(row == wide // LANES, still_open, first_sum)
         for k in range(wide // LANES):
-            out[k * state : (k + 1) * state, :] = states[:, k * LANES : (k + 1) * LANES]
+            out[k * state : (k + 1) * state, :] = one[:, k * LANES : (k + 1) * LANES]
             extra = jnp.where(row == k, decay[:, k * LANES : (k + 1) * LANES], extra)
         out[wide // LANES * state :, :] = extra
 

time: 30.1 us -> 29.8 us (0.990)
  the two profiles are of different devices: /device:TPU:17 before, /device:TPU:0 now
where the time goes in v7:
time: 29.8 us; the launch traced here: 29.2 us
  starting transfers between devices  11.3 us (38%)
  Pallas kernels  8.61 us (29%)
  waiting for transfers between devices  8.54 us (29%)
  between operations  0.69 us (2%)
    pallas_call x7, Pallas kernels, call(): pl.pallas_call(kernel, out_shape=[jax.ShapeDtypeStruct(*shape) for shape...  8.61 us
    ppermute x6, starting transfers between devices, swap_slots(): lax.ppermute(piece, ('ctx', 'head'), pair)  8.14 us
    ppermute x6, waiting for transfers between devices, swap_slots(): lax.ppermute(piece, ('ctx', 'head'), pair)  7.39 us
    ppermute x2, starting transfers between devices, swap(): return lax.ppermute(value, axis, [(k, k ^ mask) for k in range(count)])  3.14 us
    ppermute x2, waiting for transfers between devices, swap(): return lax.ppermute(value, axis, [(k, k ^ mask) for k in range(count)])  1.15 us
  transfers between devices with their start and end apart: 8, of which 5 were waited for; matrix products, arithmetic and copies ran while one was open for 0% of the time, Pallas kernels for 19%

profile of v7, /device:TPU:0, one launch (start us, length us, event | category | flops | bytes accessed | tf_op | source)
XLA Modules:
  0.0 29.2 jit_solution(13405310564542691755)
XLA Ops:
  0.6 2.4 %block_states.1 = (f32[264,128]{1,0:T(8,128)S(1)}, f32[264,128]{1,0:T(8,128)S(1)}, f32[264,128]{1,0:T(8,128)S(1)}, bf16[256,1024]{1,0:T(8,128)(2,1)S(1)}, bf16[2...) custom-call(f32[32,256]{1,0:T(8,128)} %refs_0_.1, ...), custom_call_target="tpu_custom_call" | custom-call | tf_op jit(solution)/shard_map/block_states/pallas_call | solution.py:404
  3.1 3.0 %collective-permute-start.6 = (f32[264,128]{1,0:T(8,128)S(1)}, f32[264,128]{1,0:T(8,128)S(1)}, u32[]{:S(2)}, u32[]{:S(2)}) collective-permute-start(f32[264,128]{1,0:T(8,128)S(1)} %get-tuple-element.106), channel_id=1, source_target_pairs={{0,2},{1,5},{2,0},{3,7},{4,6},{5,1},{6,4},{7,3},{8,10},{9,13},{10,... | collective-permute-start | bytes 405512 | tf_op jit(solution)/shard_map/ppermute | solution.py:432
  6.1 1.5 %collective-permute-start.7 = (f32[264,128]{1,0:T(8,128)S(1)}, f32[264,128]{1,0:T(8,128)S(1)}, u32[]{:S(2)}, u32[]{:S(2)}) collective-permute-start(f32[264,128]{1,0:T(8,128)S(1)} %get-tuple-element.107), channel_id=1, source_target_pairs={{0,4},{1,3},{2,6},{3,1},{4,0},{5,7},{6,2},{7,5},{8,12},{9,11},{10,... | collective-permute-start | bytes 405512 | tf_op jit(solution)/shard_map/ppermute | solution.py:432
  7.7 0.0 collective-permute-start.8
  7.7 2.4 %inside_first.1 = (bf16[256,256]{1,0:T(8,128)(2,1)S(1)}, f32[2,1024]{1,0:T(2,128)S(1)}, f32[256,1024]{1,0:T(8,128)S(1)}, f32[8,256]{1,0:T(8,128)S(1)}, f32[264,128]{1,0:T(8,128)S(1)}) custom-call(bf16[256,1024]{1,0:T(8,128)(2,1)S(1)} %get-tuple-element.92.features, ...), custom_call_target="tpu_custom_call", output_to_operand_aliasing={{0}: (10, {}), {1}: (11, {}), {2}: (12, {})} | custom-call | tf_op jit(solution)/shard_map/inside_first/pallas_call | solution.py:404
  10.1 2.4 %collective-permute-done.6.refs_1_ = f32[264,128]{1,0:T(8,128)S(1)} collective-permute-done((f32[264,128]{1,0:T(8,128)S(1)}, f32[264,128]{1,0:T(8,128)S(1)}, u32[]{:S(2)}, u32[]{:S(2)}) %collective-permute-start.6) | collective-permute-done | bytes 135200 | tf_op jit(solution)/shard_map/ppermute | solution.py:432
  12.4 0.0 collective-permute-done.7.refs_2_
  12.4 1.2 %collective-permute-done.8.refs_3_ = f32[264,128]{1,0:T(8,128)S(1)} collective-permute-done((f32[264,128]{1,0:T(8,128)S(1)}, f32[264,128]{1,0:T(8,128)S(1)}, u32[]{:S(2)}, u32[]{:S(2)}) %collective-permute-start.8) | collective-permute-done | bytes 135200 | tf_op jit(solution)/shard_map/ppermute | solution.py:432
  13.6 0.1 group_total.1
  13.7 3.1 %collective-permute-start.9 = (f32[256,128]{1,0:T(8,128)S(1)}, f32[256,128]{1,0:T(8,128)S(1)}, u32[]{:S(2)}, u32[]{:S(2)}) collective-permute-start(f32[256,128]{1,0:T(8,128)S(1)} %group_total.1), channel_id=1, source_target_pairs={{0,8},{2,10},{4,12},{6,14},{8,0},{10,2},{12,4},{14,6},{1,9},{3,11}... | collective-permute-start | bytes 393224 | tf_op jit(solution)/shard_map/ppermute | solution.py:418
  16.7 2.4 %inside_second.1 = f32[256,1024]{1,0:T(8,128)S(1)} custom-call(bf16[256,1024]{1,0:T(8,128)(2,1)S(1)} %get-tuple-element.92.features, bf16[256,128]{1,0:T(8,128)(2,1)S(1)} %get-tuple-element.93.b_input, bf16[256,128]{1,0:T(8,128)(2,1)S(1)} %get-tuple-element.94.c_input, f32[32,256]{1,0:T(8,128)S(1)} %get-tuple-element.95.cum_ref, ...), custom_call_target="tpu_custom_call", output_to_operand_aliasing={{}: (7, {})} | custom-call | tf_op jit(solution)/shard_map/inside_second/pallas_call | solution.py:404
  19.1 8.1 %conditional.2 = (f32[2,256]{1,0:T(2,128)S(1)}, f32[8,128]{1,0:T(8,128)S(1)}) conditional(s32[]{:T(128)} %convert_element_type.4, () %tuple.23, (f32[264,128]{1,0:T(8,128)S(1)}, f32[264,128]{1,0:T(8,128)S(1)}, f32[264,128]{1,0:T(8,128)S(1)}, f32[264,128]{1,0:T(8,128)S(1)}, bf16[256,128]{1,0:T(8,128)(2,1)S(1)}, ...), branch_computations={%region_0.0_spmd, %region_1.0_spmd} | conditional | bytes 1573000 | solution.py:563
  19.1 0.1 entering_states.2
  19.2 1.1 %collective-permute-start = (f32[256,128]{1,0:T(8,128)S(1)}, f32[256,128]{1,0:T(8,128)S(1)}, u32[]{:S(2)}, u32[]{:S(2)}) collective-permute-start(f32[256,128]{1,0:T(8,128)S(1)} %get-tuple-element.43), channel_id=1, source_target_pairs={{0,6},{1,3},{2,4},{3,1},{4,2},{5,7},{6,0},{7,5},{8,14},{9,11},{10,... | collective-permute-start | bytes 393224 | tf_op jit(solution)/shard_map/cond/branch_1_fun/ppermute | solution.py:432
  20.3 1.1 %collective-permute-start.1 = (f32[256,128]{1,0:T(8,128)S(1)}, f32[256,128]{1,0:T(8,128)S(1)}, u32[]{:S(2)}, u32[]{:S(2)}) collective-permute-start(f32[256,128]{1,0:T(8,128)S(1)} %get-tuple-element.44), channel_id=1, source_target_pairs={{0,2},{1,5},{2,0},{3,7},{4,6},{5,1},{6,4},{7,3},{8,10},{9,13},{10,... | collective-permute-start | bytes 393224 | tf_op jit(solution)/shard_map/cond/branch_1_fun/ppermute | solution.py:432
  21.4 1.4 %collective-permute-start.2 = (f32[256,128]{1,0:T(8,128)S(1)}, f32[256,128]{1,0:T(8,128)S(1)}, u32[]{:S(2)}, u32[]{:S(2)}) collective-permute-start(f32[256,128]{1,0:T(8,128)S(1)} %get-tuple-element.45), channel_id=1, source_target_pairs={{0,4},{1,7},{2,6},{3,5},{4,0},{5,3},{6,2},{7,1},{8,12},{9,15},{10,... | collective-permute-start | bytes 393224 | tf_op jit(solution)/shard_map/cond/branch_1_fun/ppermute | solution.py:432
  22.8 2.6 %collective-permute-done.refs_1_ = f32[256,128]{1,0:T(8,128)S(1)} collective-permute-done((f32[256,128]{1,0:T(8,128)S(1)}, f32[256,128]{1,0:T(8,128)S(1)}, u32[]{:S(2)}, u32[]{:S(2)}) %collective-permute-start) | collective-permute-done | bytes 131104 | tf_op jit(solution)/shard_map/cond/branch_1_fun/ppermute | solution.py:432
  25.4 1.3 %collective-permute-done.1.refs_2_ = f32[256,128]{1,0:T(8,128)S(1)} collective-permute-done((f32[256,128]{1,0:T(8,128)S(1)}, f32[256,128]{1,0:T(8,128)S(1)}, u32[]{:S(2)}, u32[]{:S(2)}) %collective-permute-start.1) | collective-permute-done | bytes 131104 | tf_op jit(solution)/shard_map/cond/branch_1_fun/ppermute | solution.py:432
  26.7 0.0 collective-permute-done.2.refs_3_
  26.7 0.6 %readout.2 = f32[2,256]{1,0:T(2,128)S(1)} custom-call(f32[256,128]{1,0:T(8,128)S(1)} %get-tuple-element.42.refs_0_, f32[256,128]{1,0:T(8,128)S(1)} %collective-permute-done.refs_1_, f32[256,128]{1,0:T(8,128)S(1)} %collective-permute-done.1.refs_2_, f32[256,128]{1,0:T(8,128)S(1)} %collective-permute-done.2.refs_3_, ...), custom_call_target="tpu_custom_call" | custom-call | tf_op jit(solution)/shard_map/cond/branch_1_fun/readout/pallas_call | solution.py:404
  27.2 0.0 collective-permute-done.9.got
  27.3 0.1 collective-permute-start.10
  27.4 1.1 %collective-permute-done.10.other = f32[2,256]{1,0:T(2,128)S(1)} collective-permute-done((f32[2,256]{1,0:T(2,128)S(1)}, f32[2,256]{1,0:T(2,128)S(1)}, u32[]{:S(2)}, u32[]{:S(2)}) %collective-permute-start.10) | collective-permute-done | bytes 2080 | tf_op jit(solution)/shard_map/ppermute | solution.py:418
  28.5 0.7 %values_and_advantages.1 = (f32[1,256]{1,0:T(1,128)}, f32[1,256]{1,0:T(1,128)}) custom-call(f32[2,256]{1,0:T(2,128)S(1)} %get-tuple-element.113.mine, f32[2,256]{1,0:T(2,128)S(1)} %collective-permute-done.10.other, f32[8,256]{1,0:T(8,128)S(1)} %get-tuple-element.109.refs_4_.suffix, f32[8,128]{1,0:T(8,128)S(1)} %get-tuple-element.114.carry, ...), custom_call_target="tpu_custom_call" | custom-call | tf_op jit(solution)/shard_map/values_and_advantages/pallas_call | solution.py:404
  (2 shorter events, 0.0 us)
Async XLA Ops:
  3.1 9.3 %collective-permute-start.6 = (f32[264,128]{1,0:T(8,128)S(1)}, f32[264,128]{1,0:T(8,128)S(1)}, u32[]{:S(2)}, u32[]{:S(2)}) collective-permute-start(f32[264,128]{1,0:T(8,128)S(1)} %get-tuple-element.106), channel_id=1, source_target_pairs={{0,2},{1,5},{2,0},{3,7},{4,6},{5,1},{6,4},{7,3},{8,10},{9,13},{10,... | collective-permute-start | bytes 405512 | tf_op jit(solution)/shard_map/ppermute | solution.py:432
  6.1 6.3 %collective-permute-start.7 = (f32[264,128]{1,0:T(8,128)S(1)}, f32[264,128]{1,0:T(8,128)S(1)}, u32[]{:S(2)}, u32[]{:S(2)}) collective-permute-start(f32[264,128]{1,0:T(8,128)S(1)} %get-tuple-element.107), channel_id=1, source_target_pairs={{0,4},{1,3},{2,6},{3,1},{4,0},{5,7},{6,2},{7,5},{8,12},{9,11},{10,... | collective-permute-start | bytes 405512 | tf_op jit(solution)/shard_map/ppermute | solution.py:432
  7.7 5.9 %collective-permute-start.8 = (f32[264,128]{1,0:T(8,128)S(1)}, f32[264,128]{1,0:T(8,128)S(1)}, u32[]{:S(2)}, u32[]{:S(2)}) collective-permute-start(f32[264,128]{1,0:T(8,128)S(1)} %get-tuple-element.108), channel_id=1, source_target_pairs={{0,6},{1,7},{2,4},{3,5},{4,2},{5,3},{6,0},{7,1},{8,14},{9,15},{10,... | collective-permute-start | bytes 405512 | tf_op jit(solution)/shard_map/ppermute | solution.py:432
  13.7 13.6 %collective-permute-start.9 = (f32[256,128]{1,0:T(8,128)S(1)}, f32[256,128]{1,0:T(8,128)S(1)}, u32[]{:S(2)}, u32[]{:S(2)}) collective-permute-start(f32[256,128]{1,0:T(8,128)S(1)} %group_total.1), channel_id=1, source_target_pairs={{0,8},{2,10},{4,12},{6,14},{8,0},{10,2},{12,4},{14,6},{1,9},{3,11}... | collective-permute-start | bytes 393224 | tf_op jit(solution)/shard_map/ppermute | solution.py:418
  19.2 6.1 %collective-permute-start = (f32[256,128]{1,0:T(8,128)S(1)}, f32[256,128]{1,0:T(8,128)S(1)}, u32[]{:S(2)}, u32[]{:S(2)}) collective-permute-start(f32[256,128]{1,0:T(8,128)S(1)} %get-tuple-element.43), channel_id=1, source_target_pairs={{0,6},{1,3},{2,4},{3,1},{4,2},{5,7},{6,0},{7,5},{8,14},{9,11},{10,... | collective-permute-start | bytes 393224 | tf_op jit(solution)/shard_map/cond/branch_1_fun/ppermute | solution.py:432
  20.3 6.3 %collective-permute-start.1 = (f32[256,128]{1,0:T(8,128)S(1)}, f32[256,128]{1,0:T(8,128)S(1)}, u32[]{:S(2)}, u32[]{:S(2)}) collective-permute-start(f32[256,128]{1,0:T(8,128)S(1)} %get-tuple-element.44), channel_id=1, source_target_pairs={{0,2},{1,5},{2,0},{3,7},{4,6},{5,1},{6,4},{7,3},{8,10},{9,13},{10,... | collective-permute-start | bytes 393224 | tf_op jit(solution)/shard_map/cond/branch_1_fun/ppermute | solution.py:432
  21.4 5.3 %collective-permute-start.2 = (f32[256,128]{1,0:T(8,128)S(1)}, f32[256,128]{1,0:T(8,128)S(1)}, u32[]{:S(2)}, u32[]{:S(2)}) collective-permute-start(f32[256,128]{1,0:T(8,128)S(1)} %get-tuple-element.45), channel_id=1, source_target_pairs={{0,4},{1,7},{2,6},{3,5},{4,0},{5,3},{6,2},{7,1},{8,12},{9,15},{10,... | collective-permute-start | bytes 393224 | tf_op jit(solution)/shard_map/cond/branch_1_fun/ppermute | solution.py:432
  27.3 1.2 %collective-permute-start.10 = (f32[2,256]{1,0:T(2,128)S(1)}, f32[2,256]{1,0:T(2,128)S(1)}, u32[]{:S(2)}, u32[]{:S(2)}) collective-permute-start(f32[2,256]{1,0:T(2,128)S(1)} %get-tuple-element.113.mine), channel_id=1, source_target_pairs={{0,1},{1,0},{2,3},{3,2},{4,5},{5,4},{6,7},{7,6},{8,9},{9,8},{10,11... | collective-permute-start | bytes 6152 | tf_op jit(solution)/shard_map/ppermute | solution.py:418

commit v8 on v7

--- a/solution.py
+++ b/solution.py
@@ -169,10 +169,9 @@
         feat = features[:, lanes]
         total = feat.astype(jnp.float32) * wide_row[1:2, lanes]
         owner = iota((span, 128), 1) // HEAD_DIM
-        for j in range(at_once):
-            head = first + j
-            cum = cum_ref[pl.ds(head, 1), :]
-            high, middle, low = split3(cum)
+        gaps = []
+        for head in (first + j for j in range(at_once)):
+            high, middle, low = split3(cum_ref[pl.ds(head, 1), :])
             other = jnp.where(
                 row < 3 * heads,
                 jnp.where(lax.rem(row, heads) == head, 1.0, 0.0),
@@ -182,9 +181,13 @@
                     jnp.where(row == 3 * heads + 1, -middle, jnp.where(row == 3 * heads + 2, -low, 0.0)),
                 ),
             ).astype(jnp.bfloat16)
-            gap = jnp.minimum(dot(by_token, other), 0.0)
-            weights = (scores * jnp.exp(gap) * step_ref[pl.ds(head, 1), :]).astype(jnp.bfloat16)
-            total = total + dot(weights, jnp.where(owner == j, feat, jnp.zeros_like(feat)))
+            gaps.append(jnp.minimum(dot(by_token, other), 0.0))
+        weights = [
+            (scores * jnp.exp(gap) * step_ref[pl.ds(first + j, 1), :]).astype(jnp.bfloat16)
+            for j, gap in enumerate(gaps)
+        ]
+        for j, weight in enumerate(weights):
+            total = total + dot(weight, jnp.where(owner == j, feat, jnp.zeros_like(feat)))
         out[:, lanes] = total
         return carry
 

time: 29.8 us -> 29.7 us (level)
  waiting for transfers between devices: 8.54 us -> 9.01 us
  Pallas kernels: 8.61 us -> 8.17 us
    ppermute x6, waiting for transfers between devices: 7.39 us -> 7.86 us  [swap_slots(): lax.ppermute(piece, ('ctx', 'head'), pair)]
    pallas_call x7, Pallas kernels: 8.61 us -> 8.17 us  [call(): pl.pallas_call(kernel, out_shape=[jax.ShapeDtypeStruct(*shape) for shape...]
  transfers between devices with their start and end apart: 8 -> 8, of which waited for: 5 -> 5; matrix products, arithmetic and copies ran while one was open for 0% -> 0% of each run, Pallas kernels for 19% -> 17%
where the time goes in v8:
time: 29.7 us; the launch traced here: 29.2 us
  starting transfers between devices  11.3 us (38%)
  waiting for transfers between devices  9.01 us (30%)
  Pallas kernels  8.17 us (28%)
  between operations  0.69 us (2%)
    pallas_call x7, Pallas kernels, call(): pl.pallas_call(kernel, out_shape=[jax.ShapeDtypeStruct(*shape) for shape...  8.17 us
    ppermute x6, starting transfers between devices, swap_slots(): lax.ppermute(piece, ('ctx', 'head'), pair)  8.14 us
    ppermute x6, waiting for transfers between devices, swap_slots(): lax.ppermute(piece, ('ctx', 'head'), pair)  7.86 us
    ppermute x2, starting transfers between devices, swap(): return lax.ppermute(value, axis, [(k, k ^ mask) for k in range(count)])  3.12 us
    ppermute x2, waiting for transfers between devices, swap(): return lax.ppermute(value, axis, [(k, k ^ mask) for k in range(count)])  1.15 us
  transfers between devices with their start and end apart: 8, of which 5 were waited for; matrix products, arithmetic and copies ran while one was open for 0% of the time, Pallas kernels for 17%

profile of v8, /device:TPU:0, one launch (start us, length us, event | category | flops | bytes accessed | tf_op | source)
XLA Modules:
  0.0 29.2 jit_solution(2121729581487985601)
XLA Ops:
  0.6 2.4 %block_states.1 = (f32[264,128]{1,0:T(8,128)S(1)}, f32[264,128]{1,0:T(8,128)S(1)}, f32[264,128]{1,0:T(8,128)S(1)}, bf16[256,1024]{1,0:T(8,128)(2,1)S(1)}, bf16[2...) custom-call(f32[32,256]{1,0:T(8,128)} %refs_0_.1, ...), custom_call_target="tpu_custom_call" | custom-call | tf_op jit(solution)/shard_map/block_states/pallas_call | solution.py:407
  3.0 3.0 %collective-permute-start.6 = (f32[264,128]{1,0:T(8,128)S(1)}, f32[264,128]{1,0:T(8,128)S(1)}, u32[]{:S(2)}, u32[]{:S(2)}) collective-permute-start(f32[264,128]{1,0:T(8,128)S(1)} %get-tuple-element.106), channel_id=1, source_target_pairs={{0,2},{1,5},{2,0},{3,7},{4,6},{5,1},{6,4},{7,3},{8,10},{9,13},{10,... | collective-permute-start | bytes 405512 | tf_op jit(solution)/shard_map/ppermute | solution.py:435
  6.0 1.6 %collective-permute-start.7 = (f32[264,128]{1,0:T(8,128)S(1)}, f32[264,128]{1,0:T(8,128)S(1)}, u32[]{:S(2)}, u32[]{:S(2)}) collective-permute-start(f32[264,128]{1,0:T(8,128)S(1)} %get-tuple-element.107), channel_id=1, source_target_pairs={{0,4},{1,3},{2,6},{3,1},{4,0},{5,7},{6,2},{7,5},{8,12},{9,11},{10,... | collective-permute-start | bytes 405512 | tf_op jit(solution)/shard_map/ppermute | solution.py:435
  7.6 0.0 collective-permute-start.8
  7.6 2.2 %inside_first.1 = (bf16[256,256]{1,0:T(8,128)(2,1)S(1)}, f32[2,1024]{1,0:T(2,128)S(1)}, f32[256,1024]{1,0:T(8,128)S(1)}, f32[8,256]{1,0:T(8,128)S(1)}, f32[264,128]{1,0:T(8,128)S(1)}) custom-call(bf16[256,1024]{1,0:T(8,128)(2,1)S(1)} %get-tuple-element.92.features, ...), custom_call_target="tpu_custom_call", output_to_operand_aliasing={{0}: (10, {}), {1}: (11, {}), {2}: (12, {})} | custom-call | tf_op jit(solution)/shard_map/inside_first/pallas_call | solution.py:407
  9.8 2.6 %collective-permute-done.6.refs_1_ = f32[264,128]{1,0:T(8,128)S(1)} collective-permute-done((f32[264,128]{1,0:T(8,128)S(1)}, f32[264,128]{1,0:T(8,128)S(1)}, u32[]{:S(2)}, u32[]{:S(2)}) %collective-permute-start.6) | collective-permute-done | bytes 135200 | tf_op jit(solution)/shard_map/ppermute | solution.py:435
  12.4 0.0 collective-permute-done.7.refs_2_
  12.4 1.1 %collective-permute-done.8.refs_3_ = f32[264,128]{1,0:T(8,128)S(1)} collective-permute-done((f32[264,128]{1,0:T(8,128)S(1)}, f32[264,128]{1,0:T(8,128)S(1)}, u32[]{:S(2)}, u32[]{:S(2)}) %collective-permute-start.8) | collective-permute-done | bytes 135200 | tf_op jit(solution)/shard_map/ppermute | solution.py:435
  13.5 0.1 group_total.1
  13.6 3.0 %collective-permute-start.9 = (f32[256,128]{1,0:T(8,128)S(1)}, f32[256,128]{1,0:T(8,128)S(1)}, u32[]{:S(2)}, u32[]{:S(2)}) collective-permute-start(f32[256,128]{1,0:T(8,128)S(1)} %group_total.1), channel_id=1, source_target_pairs={{0,8},{2,10},{4,12},{6,14},{8,0},{10,2},{12,4},{14,6},{1,9},{3,11}... | collective-permute-start | bytes 393224 | tf_op jit(solution)/shard_map/ppermute | solution.py:421
  16.7 2.2 %inside_second.1 = f32[256,1024]{1,0:T(8,128)S(1)} custom-call(bf16[256,1024]{1,0:T(8,128)(2,1)S(1)} %get-tuple-element.92.features, bf16[256,128]{1,0:T(8,128)(2,1)S(1)} %get-tuple-element.93.b_input, bf16[256,128]{1,0:T(8,128)(2,1)S(1)} %get-tuple-element.94.c_input, f32[32,256]{1,0:T(8,128)S(1)} %get-tuple-element.95.cum_ref, ...), custom_call_target="tpu_custom_call", output_to_operand_aliasing={{}: (7, {})} | custom-call | tf_op jit(solution)/shard_map/inside_second/pallas_call | solution.py:407
  18.8 8.4 %conditional.2 = (f32[2,256]{1,0:T(2,128)S(1)}, f32[8,128]{1,0:T(8,128)S(1)}) conditional(s32[]{:T(128)} %convert_element_type.4, () %tuple.23, (f32[264,128]{1,0:T(8,128)S(1)}, f32[264,128]{1,0:T(8,128)S(1)}, f32[264,128]{1,0:T(8,128)S(1)}, f32[264,128]{1,0:T(8,128)S(1)}, bf16[256,128]{1,0:T(8,128)(2,1)S(1)}, ...), branch_computations={%region_0.0_spmd, %region_1.0_spmd} | conditional | bytes 1573000 | solution.py:566
  18.9 0.1 entering_states.2
  19.0 1.1 %collective-permute-start = (f32[256,128]{1,0:T(8,128)S(1)}, f32[256,128]{1,0:T(8,128)S(1)}, u32[]{:S(2)}, u32[]{:S(2)}) collective-permute-start(f32[256,128]{1,0:T(8,128)S(1)} %get-tuple-element.43), channel_id=1, source_target_pairs={{0,6},{1,3},{2,4},{3,1},{4,2},{5,7},{6,0},{7,5},{8,14},{9,11},{10,... | collective-permute-start | bytes 393224 | tf_op jit(solution)/shard_map/cond/branch_1_fun/ppermute | solution.py:435
  20.1 1.1 %collective-permute-start.1 = (f32[256,128]{1,0:T(8,128)S(1)}, f32[256,128]{1,0:T(8,128)S(1)}, u32[]{:S(2)}, u32[]{:S(2)}) collective-permute-start(f32[256,128]{1,0:T(8,128)S(1)} %get-tuple-element.44), channel_id=1, source_target_pairs={{0,2},{1,5},{2,0},{3,7},{4,6},{5,1},{6,4},{7,3},{8,10},{9,13},{10,... | collective-permute-start | bytes 393224 | tf_op jit(solution)/shard_map/cond/branch_1_fun/ppermute | solution.py:435
  21.2 1.3 %collective-permute-start.2 = (f32[256,128]{1,0:T(8,128)S(1)}, f32[256,128]{1,0:T(8,128)S(1)}, u32[]{:S(2)}, u32[]{:S(2)}) collective-permute-start(f32[256,128]{1,0:T(8,128)S(1)} %get-tuple-element.45), channel_id=1, source_target_pairs={{0,4},{1,7},{2,6},{3,5},{4,0},{5,3},{6,2},{7,1},{8,12},{9,15},{10,... | collective-permute-start | bytes 393224 | tf_op jit(solution)/shard_map/cond/branch_1_fun/ppermute | solution.py:435
  22.5 2.9 %collective-permute-done.refs_1_ = f32[256,128]{1,0:T(8,128)S(1)} collective-permute-done((f32[256,128]{1,0:T(8,128)S(1)}, f32[256,128]{1,0:T(8,128)S(1)}, u32[]{:S(2)}, u32[]{:S(2)}) %collective-permute-start) | collective-permute-done | bytes 131104 | tf_op jit(solution)/shard_map/cond/branch_1_fun/ppermute | solution.py:435
  25.4 1.3 %collective-permute-done.1.refs_2_ = f32[256,128]{1,0:T(8,128)S(1)} collective-permute-done((f32[256,128]{1,0:T(8,128)S(1)}, f32[256,128]{1,0:T(8,128)S(1)}, u32[]{:S(2)}, u32[]{:S(2)}) %collective-permute-start.1) | collective-permute-done | bytes 131104 | tf_op jit(solution)/shard_map/cond/branch_1_fun/ppermute | solution.py:435
  26.7 0.0 collective-permute-done.2.refs_3_
  26.7 0.6 %readout.2 = f32[2,256]{1,0:T(2,128)S(1)} custom-call(f32[256,128]{1,0:T(8,128)S(1)} %get-tuple-element.42.refs_0_, f32[256,128]{1,0:T(8,128)S(1)} %collective-permute-done.refs_1_, f32[256,128]{1,0:T(8,128)S(1)} %collective-permute-done.1.refs_2_, f32[256,128]{1,0:T(8,128)S(1)} %collective-permute-done.2.refs_3_, ...), custom_call_target="tpu_custom_call" | custom-call | tf_op jit(solution)/shard_map/cond/branch_1_fun/readout/pallas_call | solution.py:407
  27.2 0.0 collective-permute-done.9.got
  27.3 0.1 collective-permute-start.10
  27.4 1.1 %collective-permute-done.10.other = f32[2,256]{1,0:T(2,128)S(1)} collective-permute-done((f32[2,256]{1,0:T(2,128)S(1)}, f32[2,256]{1,0:T(2,128)S(1)}, u32[]{:S(2)}, u32[]{:S(2)}) %collective-permute-start.10) | collective-permute-done | bytes 2080 | tf_op jit(solution)/shard_map/ppermute | solution.py:421
  28.5 0.7 %values_and_advantages.1 = (f32[1,256]{1,0:T(1,128)}, f32[1,256]{1,0:T(1,128)}) custom-call(f32[2,256]{1,0:T(2,128)S(1)} %get-tuple-element.113.mine, f32[2,256]{1,0:T(2,128)S(1)} %collective-permute-done.10.other, f32[8,256]{1,0:T(8,128)S(1)} %get-tuple-element.109.refs_4_.suffix, f32[8,128]{1,0:T(8,128)S(1)} %get-tuple-element.114.carry, ...), custom_call_target="tpu_custom_call" | custom-call | tf_op jit(solution)/shard_map/values_and_advantages/pallas_call | solution.py:407
  (2 shorter events, 0.0 us)
Async XLA Ops:
  3.0 9.4 %collective-permute-start.6 = (f32[264,128]{1,0:T(8,128)S(1)}, f32[264,128]{1,0:T(8,128)S(1)}, u32[]{:S(2)}, u32[]{:S(2)}) collective-permute-start(f32[264,128]{1,0:T(8,128)S(1)} %get-tuple-element.106), channel_id=1, source_target_pairs={{0,2},{1,5},{2,0},{3,7},{4,6},{5,1},{6,4},{7,3},{8,10},{9,13},{10,... | collective-permute-start | bytes 405512 | tf_op jit(solution)/shard_map/ppermute | solution.py:435
  6.0 6.4 %collective-permute-start.7 = (f32[264,128]{1,0:T(8,128)S(1)}, f32[264,128]{1,0:T(8,128)S(1)}, u32[]{:S(2)}, u32[]{:S(2)}) collective-permute-start(f32[264,128]{1,0:T(8,128)S(1)} %get-tuple-element.107), channel_id=1, source_target_pairs={{0,4},{1,3},{2,6},{3,1},{4,0},{5,7},{6,2},{7,5},{8,12},{9,11},{10,... | collective-permute-start | bytes 405512 | tf_op jit(solution)/shard_map/ppermute | solution.py:435
  7.6 5.9 %collective-permute-start.8 = (f32[264,128]{1,0:T(8,128)S(1)}, f32[264,128]{1,0:T(8,128)S(1)}, u32[]{:S(2)}, u32[]{:S(2)}) collective-permute-start(f32[264,128]{1,0:T(8,128)S(1)} %get-tuple-element.108), channel_id=1, source_target_pairs={{0,6},{1,7},{2,4},{3,5},{4,2},{5,3},{6,0},{7,1},{8,14},{9,15},{10,... | collective-permute-start | bytes 405512 | tf_op jit(solution)/shard_map/ppermute | solution.py:435
  13.6 13.6 %collective-permute-start.9 = (f32[256,128]{1,0:T(8,128)S(1)}, f32[256,128]{1,0:T(8,128)S(1)}, u32[]{:S(2)}, u32[]{:S(2)}) collective-permute-start(f32[256,128]{1,0:T(8,128)S(1)} %group_total.1), channel_id=1, source_target_pairs={{0,8},{2,10},{4,12},{6,14},{8,0},{10,2},{12,4},{14,6},{1,9},{3,11}... | collective-permute-start | bytes 393224 | tf_op jit(solution)/shard_map/ppermute | solution.py:421
  19.0 6.4 %collective-permute-start = (f32[256,128]{1,0:T(8,128)S(1)}, f32[256,128]{1,0:T(8,128)S(1)}, u32[]{:S(2)}, u32[]{:S(2)}) collective-permute-start(f32[256,128]{1,0:T(8,128)S(1)} %get-tuple-element.43), channel_id=1, source_target_pairs={{0,6},{1,3},{2,4},{3,1},{4,2},{5,7},{6,0},{7,5},{8,14},{9,11},{10,... | collective-permute-start | bytes 393224 | tf_op jit(solution)/shard_map/cond/branch_1_fun/ppermute | solution.py:435
  20.1 6.6 %collective-permute-start.1 = (f32[256,128]{1,0:T(8,128)S(1)}, f32[256,128]{1,0:T(8,128)S(1)}, u32[]{:S(2)}, u32[]{:S(2)}) collective-permute-start(f32[256,128]{1,0:T(8,128)S(1)} %get-tuple-element.44), channel_id=1, source_target_pairs={{0,2},{1,5},{2,0},{3,7},{4,6},{5,1},{6,4},{7,3},{8,10},{9,13},{10,... | collective-permute-start | bytes 393224 | tf_op jit(solution)/shard_map/cond/branch_1_fun/ppermute | solution.py:435
  21.2 5.5 %collective-permute-start.2 = (f32[256,128]{1,0:T(8,128)S(1)}, f32[256,128]{1,0:T(8,128)S(1)}, u32[]{:S(2)}, u32[]{:S(2)}) collective-permute-start(f32[256,128]{1,0:T(8,128)S(1)} %get-tuple-element.45), channel_id=1, source_target_pairs={{0,4},{1,7},{2,6},{3,5},{4,0},{5,3},{6,2},{7,1},{8,12},{9,15},{10,... | collective-permute-start | bytes 393224 | tf_op jit(solution)/shard_map/cond/branch_1_fun/ppermute | solution.py:435
  27.3 1.2 %collective-permute-start.10 = (f32[2,256]{1,0:T(2,128)S(1)}, f32[2,256]{1,0:T(2,128)S(1)}, u32[]{:S(2)}, u32[]{:S(2)}) collective-permute-start(f32[2,256]{1,0:T(2,128)S(1)} %get-tuple-element.113.mine), channel_id=1, source_target_pairs={{0,1},{1,0},{2,3},{3,2},{4,5},{5,4},{6,7},{7,6},{8,9},{9,8},{10,11... | collective-permute-start | bytes 6152 | tf_op jit(solution)/shard_map/ppermute | solution.py:421
